TPU v7x, 512 devices: a whole 4x8x8 slice. The times are simulated.
512 devices in a mesh: dp: 16 (over y, core), expert: 32 (over x, z).
Axes of the slice: x: 4, y: 8, z: 8, core: 2. Of those that a mesh axis runs over, the one named last changes fastest.
Arguments:
- tokens: bfloat16 [65536, 1024], P(('dp', 'expert')), may hold values from -6 to 6
- cotangent: bfloat16 [65536, 1024], P(('dp', 'expert')), may hold values from -24 to 24
- router_weight: float32 [32, 1024], replicated, may hold values from -0.1875 to 0.1875
- gate_weight: bfloat16 [32, 1024, 768], P('expert', 'dp'), may hold values from -0.1875 to 0.1875
- up_weight: bfloat16 [32, 1024, 768], P('expert', 'dp'), may hold values from -0.1875 to 0.1875
- down_weight: bfloat16 [32, 768, 1024], P('expert', 'dp'), may hold values from -0.21875 to 0.21875
- routes: int32 [65536, 6], P(('dp', 'expert')), may hold values from 0 to 31, all different within a row
- drop_mask: int32 [65536], P(('dp', 'expert')), may hold values 0 or 1
Outputs:
- token_grad: bfloat16 [65536, 1024], P(('dp', 'expert'))
- gate_grad: bfloat16 [32, 1024, 768], P('expert', 'dp')
- up_grad: bfloat16 [32, 1024, 768], P('expert', 'dp')
- router_grad: float32 [32, 1024], replicated
Inputs may be any that keep to these rules, and one draw needn't show every extreme that they name: `routes`: each row names 6 different experts, and every expert is named by some row.
All inputs are finite; a program needn't handle non-finite values. No bound on the sum of `drop_mask` on one device may be relied on, other than what follows from the above.
Results may differ from a plain program's by a relative error of at most 0.023.
Values may be sent and summed in bfloat16 or wider, within the bound.
No kernel may reach another device: no remote copies, remote signals or barrier semaphores. Data moves between devices by JAX's collectives and lax.ppermute only.
A program may use at most 64 MiB of HBM per device.

v0:
```python
import jax
import jax.numpy as jnp
from jax import lax
from jax.sharding import PartitionSpec as P

highest = lax.Precision.HIGHEST


def route_positions(block_routes, block_mask, experts, capacity):
    top_count = block_routes.shape[1]
    flat_routes = block_routes.reshape(-1)
    live_route = jnp.repeat(block_mask, top_count) == 1
    expert_ids = jnp.arange(experts, dtype=jnp.int32)
    matches = ((flat_routes[:, None] == expert_ids[None, :]) & live_route[:, None]).astype(
        jnp.int32
    )
    before = jnp.cumsum(matches, axis=0) - matches
    slot_index = jnp.sum(before * matches, axis=1)
    kept_route = live_route & (slot_index < capacity)
    sink_index = experts * capacity
    return jnp.where(kept_route, flat_routes * capacity + slot_index, sink_index)


def slot_sources(positions, experts, capacity):
    route_count = positions.shape[0]
    slot_table = jnp.full((experts * capacity + 1,), route_count, jnp.int32)
    slot_table = slot_table.at[positions].set(jnp.arange(route_count, dtype=jnp.int32))
    return slot_table[: experts * capacity]


def contract_last(left, right):
    return lax.dot_general(
        left, right, (((1,), (1,)), ((), ())), preferred_element_type=jnp.float32
    )


def contract_first(left, right):
    return lax.dot_general(
        left, right, (((0,), (0,)), ((), ())), preferred_element_type=jnp.float32
    )


def per_device(
    tokens, cotangent, router_weight, gate_weight, up_weight, down_weight, routes, drop_mask
):
    tok_rows, features = tokens.shape
    experts = router_weight.shape[0]
    top_count = routes.shape[1]
    hidden = gate_weight.shape[2]
    capacity = tok_rows * top_count * 2 // (3 * experts)
    logits = jnp.dot(tokens.astype(jnp.float32), router_weight.T, precision=highest)
    weights = jnp.exp(logits)
    router_probs = weights / jnp.sum(weights, axis=1, keepdims=True)
    route_probs = jnp.take_along_axis(router_probs, routes, axis=1).astype(jnp.bfloat16)
    positions = route_positions(routes, drop_mask, experts, capacity)
    sources = slot_sources(positions, experts, capacity)
    token_index = sources // top_count
    token_pad = jnp.concatenate([tokens, jnp.zeros((1, features), tokens.dtype)], 0)
    cotan_pad = jnp.concatenate([cotangent, jnp.zeros((1, features), cotangent.dtype)], 0)
    prob_pad = jnp.concatenate([route_probs.reshape(-1), jnp.zeros((1,), route_probs.dtype)])
    sent_tokens = token_pad[token_index]
    sent_cotangent = cotan_pad[token_index]
    sent_probs = prob_pad[sources]
    pair_shard = jnp.concatenate([gate_weight, up_weight], 0)
    down_shard = down_weight[0]
    slot_tokens, slot_cotangent, slot_probs = (
        lax.all_to_all(sent_tokens, "expert", split_axis=0, concat_axis=0, tiled=True),
        lax.all_to_all(sent_cotangent, "expert", split_axis=0, concat_axis=0, tiled=True),
        lax.all_to_all(sent_probs, "expert", split_axis=0, concat_axis=0, tiled=True),
    )
    full_pair, full_down = (
        lax.all_gather(pair_shard, "dp", axis=1, tiled=True),
        lax.all_gather(down_shard, "dp", axis=0, tiled=True),
    )
    gate_proj = jnp.dot(slot_tokens, full_pair[0], preferred_element_type=jnp.float32)
    up_proj = jnp.dot(slot_tokens, full_pair[1], preferred_element_type=jnp.float32)
    hidden_grad = contract_last(slot_cotangent, full_down)
    sigmoid_gate = jax.nn.sigmoid(gate_proj)
    activated = gate_proj * sigmoid_gate
    slope = sigmoid_gate * (1.0 + gate_proj * (1.0 - sigmoid_gate))
    prob_grad = jnp.sum(hidden_grad * activated * up_proj, axis=1).astype(jnp.bfloat16)
    scaled = slot_probs.astype(jnp.float32)[:, None] * hidden_grad
    gate_delta = (scaled * up_proj * slope).astype(jnp.bfloat16)
    up_delta = (scaled * activated).astype(jnp.bfloat16)
    slot_grad = (
        contract_last(gate_delta, full_pair[0]) + contract_last(up_delta, full_pair[1])
    ).astype(jnp.bfloat16)
    stacked_deltas = jnp.concatenate([gate_delta, up_delta], 1)
    whole_term = contract_first(slot_tokens, stacked_deltas)
    summed = lax.psum_scatter(
        whole_term.astype(jnp.bfloat16), "dp", scatter_dimension=0, tiled=True
    ).astype(jnp.float32)
    gate_sum = summed[:, :hidden]
    up_sum = summed[:, hidden:]
    grad_back, prob_back = (
        lax.all_to_all(slot_grad, "expert", split_axis=0, concat_axis=0, tiled=True),
        lax.all_to_all(prob_grad, "expert", split_axis=0, concat_axis=0, tiled=True),
    )
    grad_pad = jnp.concatenate([grad_back, jnp.zeros((1, features), grad_back.dtype)], 0)
    back_pad = jnp.concatenate([prob_back, jnp.zeros((1,), prob_back.dtype)])
    picked = grad_pad[positions].astype(jnp.float32)
    expert_sum = jnp.sum(picked.reshape(tok_rows, top_count, features), axis=1)
    prob_route = back_pad[positions].astype(jnp.float32).reshape(tok_rows, top_count)
    expert_ids = jnp.arange(experts, dtype=jnp.int32)
    matches = routes[:, :, None] == expert_ids[None, None, :]
    prob_full = jnp.sum(
        jnp.where(matches, prob_route[:, :, None], jnp.zeros((), jnp.float32)), axis=1
    )
    logit_grad = router_probs * (
        prob_full - jnp.sum(router_probs * prob_full, axis=1, keepdims=True)
    )
    token_grad = (expert_sum + jnp.dot(logit_grad, router_weight, precision=highest)).astype(
        jnp.bfloat16
    )
    router_term = jnp.dot(logit_grad.T, tokens.astype(jnp.float32), precision=highest)
    router_grad = lax.psum(router_term, ("dp", "expert"))
    return (
        token_grad,
        gate_sum.astype(jnp.bfloat16)[None],
        up_sum.astype(jnp.bfloat16)[None],
        router_grad,
    )


def solution(mesh):
    placed = (
        P(("dp", "expert"), None),
        P(("dp", "expert"), None),
        P(),
        P("expert", "dp", None),
        P("expert", "dp", None),
        P("expert", "dp", None),
        P(("dp", "expert"), None),
        P(("dp", "expert")),
    )
    return jax.shard_map(
        per_device,
        mesh=mesh,
        in_specs=placed,
        out_specs=(
            P(("dp", "expert"), None),
            P("expert", "dp", None),
            P("expert", "dp", None),
            P(),
        ),
        check_vma=False,
    )
```

profile of v0, /device:TPU:1, one launch (start us, length us, event | category | flops | bytes accessed | tf_op | source)
XLA Modules:
  0.0 492.9 jit_solution(13159053362062558256)
XLA Ops:
  7.2 0.7 all-gather.6.cloned.1.call-update
  8.0 1.6 pad_maximum_fusion
  9.6 0.7 broadcast_compare_fusion
  10.3 0.1 broadcast_in_dim.51
  10.4 0.2 eq.79
  10.5 0.1 eq.74
  10.7 0.1 eq.69
  10.8 0.8 copy.50
  11.6 0.1 eq.75
  11.8 0.1 eq.70
  11.9 0.7 broadcast_multiply_fusion
  12.6 0.1 copy.53
  12.7 0.1 mul.56
  12.9 1.7 reduce-window.6
  14.6 0.3 slice_reduce_fusion
  15.0 0.1 fusion.12
  15.1 3.4 scatter_custom_fusion
  18.5 2.8 gather_fusion.1
  21.3 13.8 %all-to-all-start.1 = ((bf16[32,16,1024]{2,1,0:T(8,128)(2,1)}), bf16[32,16,1024]{2,1,0:T(8,128)(2,1)S(1)}, u32[]{:S(2)}, u32[]{:S(2)}) async-start(bf16[32,16,1024]{2,1,0:T(8,128)(2,1)} %bitcast.2), calls=%async_computation.1 | async-start | bytes 2097152 | tf_op jit(solution)/shard_map/all_to_all | solution.py:68
  35.2 2.8 gather_fusion.2
  38.0 21.8 %all-to-all-done.1 = bf16[32,16,1024]{2,1,0:T(8,128)(2,1)S(1)} async-done(((bf16[32,16,1024]{2,1,0:T(8,128)(2,1)}), bf16[32,16,1024]{2,1,0:T(8,128)(2,1)S(1)}, u32[]{:S(2)}, u32[]{:S(2)}) %all-to-all-start.1) | async-done | bytes 1048608 | tf_op jit(solution)/shard_map/all_to_all | solution.py:68
  59.8 8.6 %all-to-all-start.2 = ((bf16[32,16,1024]{2,1,0:T(8,128)(2,1)}), bf16[32,16,1024]{2,1,0:T(8,128)(2,1)S(1)}, u32[]{:S(2)}, u32[]{:S(2)}) async-start(bf16[32,16,1024]{2,1,0:T(8,128)(2,1)} %bitcast.5), calls=%async_computation.2 | async-start | bytes 2097152 | tf_op jit(solution)/shard_map/all_to_all | solution.py:67
  68.4 0.4 fusion.22
  68.8 2.8 fusion.3
  71.6 21.6 %all-to-all-done.2 = bf16[32,16,1024]{2,1,0:T(8,128)(2,1)S(1)} async-done(((bf16[32,16,1024]{2,1,0:T(8,128)(2,1)}), bf16[32,16,1024]{2,1,0:T(8,128)(2,1)S(1)}, u32[]{:S(2)}, u32[]{:S(2)}) %all-to-all-start.2) | async-done | bytes 1048608 | tf_op jit(solution)/shard_map/all_to_all | solution.py:67
  93.2 9.7 %all-gather.4.cloned.1.call-done = bf16[2,1024,768]{2,1,0:T(8,128)(2,1)} async-done(((bf16[2,64,768]{2,1,0:T(8,128)(2,1)}), bf16[2,1024,768]{2,1,0:T(8,128)(2,1)}) %all-gather.4.cloned.1.call-update) | async-done | bytes 3145744 | tf_op jit(solution)/shard_map/all_gather | solution.py:72
  102.9 2.5 fusion.8
  105.5 2.3 multiply_reduce_fusion
  107.7 0.7 convert_element_type.94
  108.4 9.9 %all-to-all-start.4 = ((bf16[32,16,1]{1,2,0:T(2,128)(2,1)}), bf16[32,16,1]{1,2,0:T(2,128)(2,1)S(1)}, u32[]{:S(2)}, u32[]{:S(2)}) async-start(bf16[32,16,1]{1,2,0:T(2,128)(2,1)} %convert_element_type.94), calls=%async_computation.4 | async-start | bytes 32768 | tf_op jit(solution)/shard_map/all_to_all | solution.py:97
  118.4 0.1 copy.47
  118.5 0.1 reshape.191
  118.7 8.2 %all-to-all-done.4 = bf16[32,16,1]{1,2,0:T(2,128)(2,1)S(1)} async-done(((bf16[32,16,1]{1,2,0:T(2,128)(2,1)}), bf16[32,16,1]{1,2,0:T(2,128)(2,1)S(1)}, u32[]{:S(2)}, u32[]{:S(2)}) %all-to-all-start.4) | async-done | bytes 1056 | tf_op jit(solution)/shard_map/all_to_all | solution.py:97
  127.0 0.1 all_to_all.48
  127.1 5.0 %gather_fusion.4 = bf16[768]{0:T(1024)(128)(2,1)S(1)} fusion(bf16[513]{0:T(1024)(128)(2,1)S(1)} %pad_maximum_fusion.2, s32[1024]{0:T(1024)S(1)} %pad_clamp_fusion), kind=kCustom, calls=%fused_computation.4 | custom fusion | bytes 6144 | tf_op jit(solution)/shard_map/gather | solution.py:103
  132.1 0.1 reshape.150
  132.3 5.1 %gather_fusion.5 = bf16[768]{0:T(1024)(128)(2,1)S(1)} fusion(f32[128,32]{0,1:T(8,128)S(1)} %get-tuple-element.5, s32[768]{0:T(1024)S(1)} %reshape.191), kind=kCustom, calls=%fused_computation.5 | custom fusion | bytes 9216 | tf_op jit(solution)/shard_map/jit(take_along_axis)/gather | solution.py:54
  137.5 0.1 reshape.194
  137.6 0.1 copy.48
  137.7 0.1 copy.49
  137.8 0.2 convert_element_type.75
  138.0 3.5 gather_fusion
  141.5 0.1 all_to_all.49
  141.6 11.6 %all_to_all.55 = bf16[32,16,1]{1,2,0:T(2,128)(2,1)S(1)} all-to-all(bf16[32,16,1]{1,2,0:T(2,128)(2,1)S(1)} %all_to_all.49), channel_id=1, replica_groups=mesh['dp'=16,'expert'=32] {'expert'}, dimensions={0} | all-to-all | bytes 2048 | tf_op jit(solution)/shard_map/all_to_all | solution.py:69
  153.3 0.1 reshape.148
  153.4 2.6 multiply_convert_fusion
  156.0 0.9 copy-done.4
  156.9 0.2 copy-done.6
  157.1 3.5 convolution_convert_fusion
  160.7 1.1 copy-done.7
  161.8 2.6 fusion.7
  164.4 2.0 add_convert_fusion
  166.4 3.9 all-to-all-start.3
  170.4 0.9 fusion.16
  171.3 22.6 %all-to-all-done.3 = bf16[32,16,1024]{2,1,0:T(8,128)(2,1)S(1)} async-done(((bf16[32,16,1024]{2,1,0:T(8,128)(2,1)}), bf16[32,16,1024]{2,1,0:T(8,128)(2,1)S(1)}, u32[]{:S(2)}, u32[]{:S(2)}) %all-to-all-start.3) | async-done | bytes 1048608 | tf_op jit(solution)/shard_map/all_to_all | solution.py:96
  194.0 0.1 concatenate.25
  194.0 2.8 gather_fusion.3
  196.9 2.2 reshape.149
  199.0 3.5 reduce_sum.59
  202.6 1.3 fusion.9
  203.9 13.0 %reduce-scatter.2.cloned.1.call-done = bf16[64,1536]{1,0:T(8,128)(2,1)} async-done(((bf16[1024,1536]{1,0:T(8,128)(2,1)}), bf16[64,1536]{1,0:T(8,128)(2,1)}) %reduce-scatter.2.cloned.1.call-update) | async-done | bytes 196624 | tf_op jit(solution)/shard_map/reduce_scatter | solution.py:90
  216.9 1.6 slice_bitcast_fusion.6
  218.5 266.2 %all-reduce.5.cloned.1.call-done = f32[32,1024]{1,0:T(8,128)} async-done(((f32[32,1024]{1,0:T(8,128)}), f32[32,1024]{1,0:T(8,128)}) %all-reduce.5.cloned.1.call-update) | async-done | bytes 131088 | tf_op jit(solution)/shard_map/psum | solution.py:116
  484.8 1.6 copy.60
  (47 shorter events, 0.7 us)
Async XLA Ops:
  7.2 61.3 %copy-start = (f32[32,1024]{1,0:T(8,128)S(1)}, f32[32,1024]{1,0:T(8,128)}, u32[]{:S(2)}) copy-start(f32[32,1024]{1,0:T(8,128)} %param.10) | copy-start | bytes 393220
  7.2 7.7 %copy-start.8 = (bf16[128,1024]{1,0:T(8,128)(2,1)S(1)}, bf16[128,1024]{1,0:T(8,128)(2,1)}, u32[]{:S(2)}) copy-start(bf16[128,1024]{1,0:T(8,128)(2,1)} %param.9) | copy-start | bytes 786436
  7.2 61.6 %all-gather.6.cloned.1.call-start = ((), (), s32[]{:S(2)}) async-start(), calls=%async_computation.9 | async-start | bytes 1671168 | tf_op jit(solution)/shard_map/all_gather | solution.py:73
  7.9 95.0 %all-gather.4.cloned.1.call-start = ((), (), s32[]{:S(2)}) async-start(), calls=%async_computation.6 | async-start | bytes 3342336 | tf_op jit(solution)/shard_map/all_gather | solution.py:72
  21.3 13.9 %copy-start.1 = (bf16[128,1024]{1,0:T(8,128)(2,1)S(1)}, bf16[128,1024]{1,0:T(8,128)(2,1)}, u32[]{:S(2)}) copy-start(bf16[128,1024]{1,0:T(8,128)(2,1)} %param.8) | copy-start | bytes 786436
  21.3 38.5 %all-to-all-start.1 = ((bf16[32,16,1024]{2,1,0:T(8,128)(2,1)}), bf16[32,16,1024]{2,1,0:T(8,128)(2,1)S(1)}, u32[]{:S(2)}, u32[]{:S(2)}) async-start(bf16[32,16,1024]{2,1,0:T(8,128)(2,1)} %bitcast.2), calls=%async_computation.1 | async-start | bytes 2097152 | tf_op jit(solution)/shard_map/all_to_all | solution.py:68
  38.0 30.4 %copy-start.9 = (s32[128,6]{0,1:T(8,128)S(1)}, s32[128,6]{0,1:T(8,128)}, u32[]{:S(2)}) copy-start(s32[128,6]{0,1:T(8,128)} %param.14) | copy-start | bytes 9220
  59.8 9.0 %copy-start.3 = (bf16[32,16,1024]{2,1,0:T(8,128)(2,1)}, bf16[32,16,1024]{2,1,0:T(8,128)(2,1)S(1)}, u32[]{:S(2)}) copy-start(bf16[32,16,1024]{2,1,0:T(8,128)(2,1)S(1)} %all-to-all-done.1) | copy-start | bytes 3145732
  59.8 33.4 %all-to-all-start.2 = ((bf16[32,16,1024]{2,1,0:T(8,128)(2,1)}), bf16[32,16,1024]{2,1,0:T(8,128)(2,1)S(1)}, u32[]{:S(2)}, u32[]{:S(2)}) async-start(bf16[32,16,1024]{2,1,0:T(8,128)(2,1)} %bitcast.5), calls=%async_computation.2 | async-start | bytes 2097152 | tf_op jit(solution)/shard_map/all_to_all | solution.py:67
  102.9 2.5 copy-start.10
  105.4 2.3 copy-start.2
  108.4 18.5 %all-to-all-start.4 = ((bf16[32,16,1]{1,2,0:T(2,128)(2,1)}), bf16[32,16,1]{1,2,0:T(2,128)(2,1)S(1)}, u32[]{:S(2)}, u32[]{:S(2)}) async-start(bf16[32,16,1]{1,2,0:T(2,128)(2,1)} %convert_element_type.94), calls=%async_computation.4 | async-start | bytes 32768 | tf_op jit(solution)/shard_map/all_to_all | solution.py:97
  118.3 98.6 %reduce-scatter.2.cloned.1.call-start = ((), (), s32[]{:S(2)}) async-start(), calls=%async_computation.7 | async-start | bytes 3342336 | tf_op jit(solution)/shard_map/reduce_scatter | solution.py:90
  156.0 0.9 copy-start.4
  156.0 1.1 copy-start.6
  160.7 1.1 copy-start.7
  161.8 2.6 copy-start.5
  161.8 2.6 copy-start.11
  166.4 27.5 %all-to-all-start.3 = ((bf16[32,16,1024]{2,1,0:T(8,128)(2,1)}), bf16[32,16,1024]{2,1,0:T(8,128)(2,1)S(1)}, u32[]{:S(2)}, u32[]{:S(2)}) async-start(bf16[32,16,1024]{2,1,0:T(8,128)(2,1)} %bitcast.9), calls=%async_computation.3 | async-start | bytes 2097152 | tf_op jit(solution)/shard_map/all_to_all | solution.py:96
  170.4 314.4 %all-reduce.5.cloned.1.call-start = ((), (), s32[]{:S(2)}) async-start(), calls=%async_computation.8 | async-start | bytes 262144 | tf_op jit(solution)/shard_map/psum | solution.py:116
Sparse Core Ops, SparseCore 0:
  10.2 47.2 all-gather.5
  60.2 42.6 all-gather.3
  160.8 56.0 reduce-scatter.1
  222.3 262.4 all-reduce.4
where the time goes:
time: 494 us; the launch traced here: 493 us
  waiting for transfers between devices  364 us (74%)
  local copies, waits for them, and re-layouts  37.1 us (8%)
  starting transfers between devices  36.4 us (7%)
  matrix products  18.3 us (4%)
  between operations  14.2 us (3%)
  blocking collectives  11.6 us (2%)
  other arithmetic  11.3 us (2%)
    psum x1, waiting for transfers between devices, per_device(): router_grad = lax.psum(router_term, ('dp', 'expert'))  266 us
    all_to_all x1, waiting for transfers between devices, per_device(): lax.all_to_all(slot_grad, 'expert', split_axis=0, concat_axis=0, tiled=True)  22.6 us
    all_to_all x1, waiting for transfers between devices, per_device(): lax.all_to_all(sent_cotangent, 'expert', split_axis=0, concat_axis=0, til...  21.8 us
    all_to_all x1, waiting for transfers between devices, per_device(): lax.all_to_all(sent_tokens, 'expert', split_axis=0, concat_axis=0, tiled=...  21.6 us
    all_to_all x1, starting transfers between devices, per_device(): lax.all_to_all(sent_cotangent, 'expert', split_axis=0, concat_axis=0, til...  13.8 us
    reduce_scatter x1, waiting for transfers between devices, per_device(): lax.psum_scatter(whole_term.astype(jnp.bfloat16), 'dp', scatter_dimension...  13 us
    all_to_all x1, blocking collectives, per_device(): lax.all_to_all(sent_probs, 'expert', split_axis=0, concat_axis=0, tiled=T...  11.6 us
    all_to_all x1, starting transfers between devices, per_device(): lax.all_to_all(prob_grad, 'expert', split_axis=0, concat_axis=0, tiled=True)  9.9 us
  transfers between devices with their start and end apart: 8, of which 7 were waited for; matrix products, arithmetic and copies ran while one was open for 7% of the time, Pallas kernels for 0%

commit v1 on v0

v1 whole, which is shorter than its diff:
```python
import jax
import jax.numpy as jnp
from jax import lax
from jax.experimental import pallas as pl
from jax.experimental.pallas import tpu as pltpu
from jax.sharding import Mesh, PartitionSpec as P

f32 = jnp.float32
bf16 = jnp.bfloat16
DP = ("y", "core")
EXPERT = ("x", "z")
CHUNK = 256
ROWS = (((0,), (0,)), ((), ()))
LAST = (((1,), (1,)), ((), ()))
PLAIN = (((1,), (0,)), ((), ()))


def dot(left, right, dims=PLAIN):
    return lax.dot_general(left, right, dims, preferred_element_type=f32)


def split3(value):
    high = value.astype(bf16)
    rest = value - high.astype(f32)
    mid = rest.astype(bf16)
    low = (rest - mid.astype(f32)).astype(bf16)
    return high, mid, low


def dispatch_kernel(routes_ref, mask_ref, tokens_ref, cotangent_ref, sent_ref, select_ref):
    experts, both, _ = sent_ref.shape
    capacity = both // 2
    tok_rows, top_count = routes_ref.shape
    lane = lax.broadcasted_iota(jnp.int32, (tok_rows, experts), 1)
    live = jnp.zeros((tok_rows, experts), f32)
    for k in range(top_count):
        live = live + jnp.where(routes_ref[:, k : k + 1] == lane, 1.0, 0.0)
    row = lax.broadcasted_iota(jnp.int32, (tok_rows, tok_rows), 0)
    column = lax.broadcasted_iota(jnp.int32, (tok_rows, tok_rows), 1)
    same = jnp.where(row == column, 1.0, 0.0).astype(bf16)
    earlier = jnp.where(row < column, 1.0, 0.0).astype(bf16)
    live = dot(live.astype(bf16), same, ROWS)
    live = jnp.where(mask_ref[...] == 1, live, 0.0)
    before = dot(live.astype(bf16), earlier)
    place = jnp.where(live > 0.5, before, -1.0).astype(bf16)
    slots = experts * capacity
    owner = lax.broadcasted_iota(jnp.int32, (slots, experts), 0) // capacity
    spread = jnp.where(owner == lax.broadcasted_iota(jnp.int32, (slots, experts), 1), 1.0, 0.0)
    place = dot(spread.astype(bf16), place)
    index = lax.broadcasted_iota(jnp.int32, (slots, tok_rows), 0) % capacity
    select = jnp.where(place == index.astype(f32), 1.0, 0.0).astype(bf16)
    select_ref[...] = select
    for start in range(0, tokens_ref.shape[1], CHUNK):
        columns = slice(start, start + CHUNK)
        for half, ref in enumerate((tokens_ref, cotangent_ref)):
            packed = dot(select, ref[:, columns]).astype(bf16)
            sent_ref[:, half * capacity : (half + 1) * capacity, columns] = packed.reshape(
                experts, capacity, CHUNK
            )


def delta_kernel(
    expert_ref, slots_ref, weights_ref, router_ref, part_ref, delta_ref, share_ref, term_ref,
    flipped_ref, down_ref,
):
    sources, both, features = slots_ref.shape
    capacity = both // 2
    slots = sources * capacity
    shards, shard_rows, hidden = weights_ref.shape
    part = shard_rows // 3
    narrow = hidden // shards
    experts = router_ref.shape[0]
    slot_tokens = slots_ref[:, :capacity, :].reshape(slots, features)
    slot_cotangent = slots_ref[:, capacity:, :].reshape(slots, features)
    flipped_ref[...] = slot_tokens.T
    down_ref[:, :hidden] = weights_ref[:, 2 * part : 2 * part + narrow, :].reshape(hidden, hidden)
    extra = features - hidden
    pieces = [
        weights_ref[:, 2 * part + narrow :, i * extra : (i + 1) * extra]
        for i in range(hidden // extra)
    ]
    down_ref[:, hidden:] = jnp.stack(pieces, axis=1).reshape(hidden, extra)

    stack = jnp.concatenate(split3(router_ref[...]), axis=0)
    logits = dot(slot_tokens, stack, LAST)
    logits = logits[:, :experts] + (
        logits[:, experts : 2 * experts] + logits[:, 2 * experts :]
    )
    weights = jnp.exp(logits)
    probs = weights / jnp.sum(weights, axis=1, keepdims=True)
    mine = lax.broadcasted_iota(jnp.int32, (slots, experts), 1) == expert_ref[0]
    own = jnp.sum(jnp.where(mine, probs, 0.0), axis=1, keepdims=True)
    rounded = own.astype(bf16).astype(f32)

    prob_grad = jnp.zeros((slots, 1), f32)
    for start in range(0, hidden, CHUNK):
        columns = slice(start, start + CHUNK)
        gate = weights_ref[:, :part, columns].reshape(features, CHUNK)
        up = weights_ref[:, part : 2 * part, columns].reshape(features, CHUNK)
        gate_proj = dot(slot_tokens, gate)
        up_proj = dot(slot_tokens, up)
        hidden_grad = dot(slot_cotangent, down_ref[columns, :], LAST)
        sigmoid_gate = 1.0 / (1.0 + jnp.exp(-gate_proj))
        activated = gate_proj * sigmoid_gate
        slope = sigmoid_gate * (1.0 + gate_proj * (1.0 - sigmoid_gate))
        prob_grad = prob_grad + jnp.sum(
            hidden_grad * activated * up_proj, axis=1, keepdims=True
        )
        scaled = rounded * hidden_grad
        gate_delta = (scaled * up_proj * slope).astype(bf16)
        up_delta = (scaled * activated).astype(bf16)
        delta_ref[:, columns] = gate_delta
        delta_ref[:, hidden + start : hidden + start + CHUNK] = up_delta
        for half, delta in enumerate((gate_delta, up_delta)):
            product = dot(flipped_ref[...], delta).astype(bf16)
            part_ref[:, half * part : (half + 1) * part, columns] = product.reshape(
                shards, part, CHUNK
            )
    share = prob_grad.astype(bf16).astype(f32) * own
    share = share * (jnp.where(mine, 1.0, 0.0) - probs)
    share_ref[...] = share
    term = dot(jnp.concatenate(split3(share), axis=1), slot_tokens, ROWS)
    term_ref[...] = term[:experts] + (term[experts : 2 * experts] + term[2 * experts :])


def slot_grad_kernel(delta_ref, weights_ref, share_ref, router_ref, grad_ref):
    shards, shard_rows, hidden = weights_ref.shape
    part = shard_rows // 3
    features = grad_ref.shape[1]
    step = CHUNK // part
    share_high, share_mid, _ = split3(share_ref[...])
    router_high, router_mid, _ = split3(router_ref[...])
    left = jnp.concatenate([share_high, share_high, share_mid], axis=1)
    right = jnp.concatenate([router_high, router_mid, router_high], axis=0)
    for block in range(features // CHUNK):
        gate = weights_ref[block * step : (block + 1) * step, :part, :].reshape(CHUNK, hidden)
        up = weights_ref[block * step : (block + 1) * step, part : 2 * part, :].reshape(
            CHUNK, hidden
        )
        columns = slice(block * CHUNK, (block + 1) * CHUNK)
        total = dot(delta_ref[:, :hidden], gate, LAST) + dot(delta_ref[:, hidden:], up, LAST)
        grad_ref[:, columns] = (total + dot(left, right[:, columns])).astype(bf16)


def combine_kernel(select_ref, back_ref, out_ref):
    for start in range(0, out_ref.shape[1], CHUNK):
        columns = slice(start, start + CHUNK)
        out_ref[:, columns] = dot(select_ref[...], back_ref[:, columns], ROWS).astype(bf16)


def call(kernel, outs, flops, size, scratch=(), smem=0, name=None):
    def run(*operands):
        vmem = pl.BlockSpec(memory_space=pltpu.VMEM)
        specs = [pl.BlockSpec(memory_space=pltpu.SMEM)] * smem + [vmem] * (len(operands) - smem)
        return pl.pallas_call(
            kernel,
            out_shape=[jax.ShapeDtypeStruct(s, d) for s, d in outs],
            in_specs=specs,
            out_specs=[vmem] * len(outs),
            scratch_shapes=list(scratch),
            compiler_params=pltpu.CompilerParams(vmem_limit_bytes=48 * 1024 * 1024),
            cost_estimate=pl.CostEstimate(flops=flops, bytes_accessed=size, transcendentals=0),
            name=name,
        )(*operands)

    return run


def pack_down(down_shard, hidden):
    extra = down_shard.shape[1] - hidden
    tail = down_shard[:, hidden:].reshape(hidden // extra, -1, extra)
    return jnp.concatenate(
        [down_shard[:, :hidden], jnp.concatenate([t for t in tail], axis=1)], axis=0
    )


def per_device(
    tokens, cotangent, router_weight, gate_weight, up_weight, down_weight, routes, drop_mask
):
    tok_rows, features = tokens.shape
    experts = router_weight.shape[0]
    top_count = routes.shape[1]
    _, part, hidden = gate_weight.shape
    shards = features // part
    capacity = tok_rows * top_count * 2 // (3 * experts)
    slots = experts * capacity

    shard = jnp.concatenate(
        [gate_weight[0], up_weight[0], pack_down(down_weight[0], hidden)], axis=0
    )
    weights = lax.all_gather(shard, DP, axis=0, tiled=True)
    weights = weights.reshape(shards, 3 * part, hidden)

    sent, select = call(
        dispatch_kernel,
        [((experts, 2 * capacity, features), bf16), ((slots, tok_rows), bf16)],
        4 * slots * tok_rows * features,
        3 * 2**20,
        name="dispatch",
    )(routes, drop_mask.reshape(1, tok_rows), tokens, cotangent)
    slot_rows = lax.all_to_all(sent, EXPERT, split_axis=0, concat_axis=0, tiled=True)

    me = lax.axis_index(EXPERT).astype(jnp.int32).reshape(1)
    parts, deltas, share, term = call(
        delta_kernel,
        [
            ((shards, 2 * part, hidden), bf16),
            ((slots, 2 * hidden), bf16),
            ((slots, experts), f32),
            ((experts, features), f32),
        ],
        10 * slots * features * hidden,
        10 * 2**20,
        scratch=[pltpu.VMEM((features, slots), bf16), pltpu.VMEM((hidden, features), bf16)],
        smem=1,
        name="deltas",
    )(me, slot_rows, weights, router_weight)
    sums = lax.psum_scatter(
        parts.reshape(shards * 2 * part, hidden), DP, scatter_dimension=0, tiled=True
    )
    (slot_grad,) = call(
        slot_grad_kernel,
        [((slots, features), bf16)],
        4 * slots * features * hidden,
        6 * 2**20,
        name="slot_grad",
    )(deltas, weights, share, router_weight)
    back = lax.all_to_all(slot_grad, EXPERT, split_axis=0, concat_axis=0, tiled=True)
    (token_grad,) = call(
        combine_kernel,
        [((tok_rows, features), bf16)],
        2 * slots * tok_rows * features,
        2 * 2**20,
        name="combine",
    )(select, back)

    term = lax.all_to_all(term, EXPERT, split_axis=0, concat_axis=0, tiled=True)
    term = jnp.sum(term, axis=0, keepdims=True)
    term = jnp.sum(lax.all_gather(term, DP, axis=0, tiled=True), axis=0, keepdims=True)
    router_grad = lax.all_to_all(
        jnp.broadcast_to(term, (experts, features)), EXPERT, split_axis=0, concat_axis=0, tiled=True
    )
    return token_grad, sums[:part][None], sums[part:][None], router_grad


def solution(mesh):
    fine = Mesh(mesh.devices.reshape(8, 2, 4, 8), DP + EXPERT)
    rows = P(DP + EXPERT, None)
    shard = P(EXPERT, DP, None)
    return jax.shard_map(
        per_device,
        mesh=fine,
        in_specs=(rows, rows, P(), shard, shard, shard, rows, P(DP + EXPERT)),
        out_specs=(rows, shard, shard, P()),
        check_vma=False,
    )
```

time: 494 us -> 183 us (0.37)
  waiting for transfers between devices: 364 us -> 77 us
  local copies, waits for them, and re-layouts: 37.1 us -> 10.8 us
  blocking collectives: 11.6 us -> 36 us
  matrix products: 18.3 us -> 0 us
  Pallas kernels: 0 us -> 17.3 us
  starting transfers between devices: 36.4 us -> 23.4 us
  other arithmetic: 11.3 us -> 1.79 us
    psum x1 -> x0, waiting for transfers between devices: 266 us -> none  [per_device(): router_grad = lax.psum(router_term, ('dp', 'expert'))]
    gather x10 -> x0, local copies, waits for them, and re-layouts: 22.5 us -> none  [the longest x5 5.57 us: per_device(): jnp.take_along_axis(router_probs, routes, axis=1).astype(jnp.bfloat16)]
    all_gather x0 -> x1, blocking collectives: none -> 19.9 us  [per_device(): lax.all_gather(term, DP, axis=0, tiled=True)]
    dot_general x9 -> x0, matrix products: 18.3 us -> none  [the longest x3 7.32 us: contract_last(): lax.dot_general(left, right, (((1,), (1,)), ((), ())), preferred_element_...]
    pallas_call x0 -> x4, Pallas kernels: none -> 17.3 us  [run(): pl.pallas_call(kernel, out_shape=[jax.ShapeDtypeStruct(s, d) for s, d in...]
    reduce_scatter x1, waiting for transfers between devices: 13 us -> 0.01 us  [per_device(): lax.psum_scatter(parts.reshape(shards * 2 * part, hidden), DP, scatter_di...]
    all_to_all x4 -> x3, starting transfers between devices: 36.3 us -> 23.3 us  [the longest x1 13.8 us: per_device(): lax.all_to_all(sent, EXPERT, split_axis=0, concat_axis=0, tiled=True)]
    all_gather x2 -> x1, waiting for transfers between devices: 9.75 us -> 0.01 us  [per_device(): weights = lax.all_gather(shard, DP, axis=0, tiled=True)]
  transfers between devices with their start and end apart: 8 -> 5, of which waited for: 7 -> 3; matrix products, arithmetic and copies ran while one was open for 7% -> 1% of each run, Pallas kernels for 0% -> 4%
where the time goes in v1:
time: 183 us; the launch traced here: 180 us
  waiting for transfers between devices  77 us (42%)
  blocking collectives  36 us (20%)
  starting transfers between devices  23.4 us (13%)
  Pallas kernels  17.3 us (9%)
  between operations  14.1 us (8%)
  local copies, waits for them, and re-layouts  10.8 us (6%)
    all_to_all x1, waiting for transfers between devices, per_device(): lax.all_to_all(sent, EXPERT, split_axis=0, concat_axis=0, tiled=True)  48.8 us
    all_to_all x1, waiting for transfers between devices, per_device(): lax.all_to_all(slot_grad, EXPERT, split_axis=0, concat_axis=0, tiled=True)  24.5 us
    all_gather x1, blocking collectives, per_device(): lax.all_gather(term, DP, axis=0, tiled=True)  19.9 us
    pallas_call x4, Pallas kernels, run(): pl.pallas_call(kernel, out_shape=[jax.ShapeDtypeStruct(s, d) for s, d in...  17.3 us
    all_to_all x1, blocking collectives, per_device(): term = lax.all_to_all(term, EXPERT, split_axis=0, concat_axis=0, tiled=True)  16.1 us
    all_to_all x1, starting transfers between devices, per_device(): lax.all_to_all(sent, EXPERT, split_axis=0, concat_axis=0, tiled=True)  13.8 us
    unnamed x16, local copies, waits for them, and re-layouts  6.64 us
    all_to_all x1, starting transfers between devices, per_device(): lax.all_to_all(slot_grad, EXPERT, split_axis=0, concat_axis=0, tiled=True)  5.59 us
  transfers between devices with their start and end apart: 5, of which 3 were waited for; matrix products, arithmetic and copies ran while one was open for 1% of the time, Pallas kernels for 4%

profile of v1, /device:TPU:1, one launch (start us, length us, event | category | flops | bytes accessed | tf_op | source)
XLA Modules:
  0.0 180.4 jit_solution(12966063868560977055)
XLA Ops:
  7.2 0.0 all-gather.3.cloned.1.call-start
  7.2 0.7 fusion
  7.9 0.9 slice.19
  8.8 1.7 maximum_maximum_fusion
  10.5 0.0 all-gather.3.cloned.1.call-update
  10.5 0.8 copy.15.routes_ref
  11.3 0.0 copy-start.4
  11.3 0.9 copy-done.4
  12.3 0.0 copy-start.5
  12.3 0.9 copy-done.5
  13.2 0.0 copy-start.6
  13.2 0.7 copy-done.6
  13.9 1.3 dispatch.1
  15.2 0.0 copy-start
  15.2 1.4 copy-done
  16.6 0.0 copy-start.3
  16.6 13.8 %all-to-all-start = ((bf16[32,32,1024]{2,1,0:T(8,128)(2,1)}), bf16[32,32,1024]{2,1,0:T(8,128)(2,1)S(1)}, u32[]{:S(2)}, u32[]{:S(2)}) async-start(bf16[32,32,1024]{2,1,0:T(8,128)(2,1)} %copy-done), calls=%async_computation | async-start | bytes 4194304 | tf_op jit(solution)/shard_map/all_to_all | solution.py:201
  30.4 0.0 reduce-scatter.2.cloned.1.call-start
  30.5 48.8 %all-to-all-done.slots_ref = bf16[32,32,1024]{2,1,0:T(8,128)(2,1)S(1)} async-done(((bf16[32,32,1024]{2,1,0:T(8,128)(2,1)}), bf16[32,32,1024]{2,1,0:T(8,128)(2,1)S(1)}, u32[]{:S(2)}, u32[]{:S(2)}) %all-to-all-start) | async-done | bytes 2097184 | tf_op jit(solution)/shard_map/all_to_all | solution.py:201
  79.3 0.0 all-gather.3.cloned.1.call-done
  79.3 0.0 copy-done.3
  79.3 9.4 %deltas.1 = (bf16[16,128,768]{2,1,0:T(8,128)(2,1)}, bf16[512,1536]{1,0:T(8,128)(2,1)S(1)}, f32[512,32]{1,0:T(8,128)S(1)}, f32[32,1024]{1,0:T(8,128)S(1)}) custom-call(s32[1]{0:T(128)} %bitcast.1.expert_ref, bf16[32,32,1024]{2,1,0:T(8,128)(2,1)S(1)} %all-to-all-done.slots_ref, bf16[16,192,768]{2,1,0:T(8,128)(2,1)} %bitcast.20, f32[32,1024]{1,0:T(8,128)S(1)} %copy-done.3), custom_call_target="tpu_custom_call" | custom-call | flops 4026531840 | bytes 10485760 | tf_op jit(solution)/shard_map/deltas/pallas_call | solution.py:155
  88.7 0.0 copy-start.1
  88.7 1.2 copy-done.1
  90.0 0.0 copy-start.2
  90.0 0.0 reduce-scatter.2.cloned.1.call-update
  90.0 0.1 copy.16
  90.1 16.1 %all_to_all.34 = f32[32,1,1024]{2,1,0:T(1,128)S(1)} all-to-all(f32[32,1,1024]{2,1,0:T(1,128)S(1)} %copy.16), channel_id=1, replica_groups=mesh['y'=8,'core'=2,'x'=4,'z'=8] {'x','z'}, dimensions={0} | all-to-all | bytes 262144 | tf_op jit(solution)/shard_map/all_to_all | solution.py:237
  106.2 0.1 reduce_sum.18
  106.3 19.9 %all-gather = f32[16384]{0:T(1024)S(1)} all-gather(f32[1024]{0:T(1024)S(1)} %reduce_sum.18), channel_id=2, replica_groups=mesh['y'=8,'core'=2,'x'=4,'z'=8] {'y','core'}, dimensions={0}, use_global_device_ids=true | all-gather | bytes 69632 | tf_op jit(solution)/shard_map/all_gather | solution.py:239
  126.3 0.7 broadcast_in_dim.18
  127.0 3.9 %all-to-all-start.3 = ((f32[32,1,1024]{2,1,0:T(1,128)}), f32[32,1,1024]{2,1,0:T(1,128)S(1)}, u32[]{:S(2)}, u32[]{:S(2)}) async-start(f32[32,1,1024]{2,1,0:T(1,128)} %broadcast_in_dim.18), calls=%async_computation.4 | async-start | bytes 262144 | tf_op jit(solution)/shard_map/all_to_all | solution.py:240
  130.9 0.0 copy-done.2
  130.9 5.5 %slot_grad.1 = bf16[512,1024]{1,0:T(8,128)(2,1)} custom-call(bf16[512,1536]{1,0:T(8,128)(2,1)S(1)} %copy-done.2, bf16[16,192,768]{2,1,0:T(8,128)(2,1)} %bitcast.21, f32[512,32]{1,0:T(8,128)S(1)} %get-tuple-element.13.share_ref, f32[32,1024]{1,0:T(8,128)S(1)} %copy-done.3), custom_call_target="tpu_custom_call" | custom-call | flops 1610612736 | bytes 6291456 | tf_op jit(solution)/shard_map/slot_grad/pallas_call | solution.py:155
  136.4 3.6 %all-to-all-done.3 = f32[32,1,1024]{2,1,0:T(1,128)S(1)} async-done(((f32[32,1,1024]{2,1,0:T(1,128)}), f32[32,1,1024]{2,1,0:T(1,128)S(1)}, u32[]{:S(2)}, u32[]{:S(2)}) %all-to-all-start.3) | async-done | bytes 131104 | tf_op jit(solution)/shard_map/all_to_all | solution.py:240
  140.0 5.6 %all-to-all-start.1 = ((bf16[32,16,1024]{2,1,0:T(8,128)(2,1)}), bf16[32,16,1024]{2,1,0:T(8,128)(2,1)S(1)}, u32[]{:S(2)}, u32[]{:S(2)}) async-start(bf16[32,16,1024]{2,1,0:T(8,128)(2,1)} %bitcast.6), calls=%async_computation.1 | async-start | bytes 2097152 | tf_op jit(solution)/shard_map/all_to_all | solution.py:228
  145.6 0.7 copy.19
  146.3 24.5 %all-to-all-done.1 = bf16[32,16,1024]{2,1,0:T(8,128)(2,1)S(1)} async-done(((bf16[32,16,1024]{2,1,0:T(8,128)(2,1)}), bf16[32,16,1024]{2,1,0:T(8,128)(2,1)S(1)}, u32[]{:S(2)}, u32[]{:S(2)}) %all-to-all-start.1) | async-done | bytes 1048608 | tf_op jit(solution)/shard_map/all_to_all | solution.py:228
  170.8 1.1 combine.1
  171.9 0.0 reduce-scatter.2.cloned.1.call-done
  171.9 1.6 slice_bitcast_fusion
  (2 shorter events, 0.0 us)
Async XLA Ops:
  7.2 72.2 %all-gather.3.cloned.1.call-start = ((), (), s32[]{:S(2)}) async-start(), calls=%async_computation.5 | async-start | bytes 5013504 | tf_op jit(solution)/shard_map/all_gather | solution.py:191
  11.3 0.9 copy-start.4
  12.3 0.9 copy-start.5
  13.2 0.7 copy-start.6
  15.2 1.4 copy-start
  16.6 62.8 %copy-start.3 = (f32[32,1024]{1,0:T(8,128)S(1)}, f32[32,1024]{1,0:T(8,128)}, u32[]{:S(2)}) copy-start(f32[32,1024]{1,0:T(8,128)} %router_ref.3) | copy-start | bytes 393220
  16.6 62.7 %all-to-all-start = ((bf16[32,32,1024]{2,1,0:T(8,128)(2,1)}), bf16[32,32,1024]{2,1,0:T(8,128)(2,1)S(1)}, u32[]{:S(2)}, u32[]{:S(2)}) async-start(bf16[32,32,1024]{2,1,0:T(8,128)(2,1)} %copy-done), calls=%async_computation | async-start | bytes 4194304 | tf_op jit(solution)/shard_map/all_to_all | solution.py:201
  30.4 141.5 %reduce-scatter.2.cloned.1.call-start = ((), (), s32[]{:S(2)}) async-start(), calls=%async_computation.6 | async-start | bytes 3342336 | tf_op jit(solution)/shard_map/reduce_scatter | solution.py:218
  88.7 1.2 copy-start.1
  90.0 40.9 %copy-start.2 = (bf16[512,1536]{1,0:T(8,128)(2,1)S(1)}, bf16[512,1536]{1,0:T(8,128)(2,1)}, u32[]{:S(2)}) copy-start(bf16[512,1536]{1,0:T(8,128)(2,1)} %copy-done.1) | copy-start | bytes 4718596
  127.0 13.0 %all-to-all-start.3 = ((f32[32,1,1024]{2,1,0:T(1,128)}), f32[32,1,1024]{2,1,0:T(1,128)S(1)}, u32[]{:S(2)}, u32[]{:S(2)}) async-start(f32[32,1,1024]{2,1,0:T(1,128)} %broadcast_in_dim.18), calls=%async_computation.4 | async-start | bytes 262144 | tf_op jit(solution)/shard_map/all_to_all | solution.py:240
  140.0 30.8 %all-to-all-start.1 = ((bf16[32,16,1024]{2,1,0:T(8,128)(2,1)}), bf16[32,16,1024]{2,1,0:T(8,128)(2,1)S(1)}, u32[]{:S(2)}, u32[]{:S(2)}) async-start(bf16[32,16,1024]{2,1,0:T(8,128)(2,1)} %bitcast.6), calls=%async_computation.1 | async-start | bytes 2097152 | tf_op jit(solution)/shard_map/all_to_all | solution.py:228
Sparse Core Ops, SparseCore 0:
  10.7 51.2 all-gather.2
  90.1 60.8 reduce-scatter.1

commit v2 on v1

v2 whole, which is shorter than its diff:
```python
import jax
import jax.numpy as jnp
from jax import lax
from jax.experimental import pallas as pl
from jax.experimental.pallas import tpu as pltpu
from jax.sharding import Mesh, PartitionSpec as P

f32 = jnp.float32
bf16 = jnp.bfloat16
DP = ("y", "core")
EXPERT = ("x", "z")
CHUNK = 256
ROWS = (((0,), (0,)), ((), ()))
LAST = (((1,), (1,)), ((), ()))
PLAIN = (((1,), (0,)), ((), ()))


def dot(left, right, dims=PLAIN):
    return lax.dot_general(left, right, dims, preferred_element_type=f32)


def split3(value):
    high = value.astype(bf16)
    rest = value - high.astype(f32)
    mid = rest.astype(bf16)
    low = (rest - mid.astype(f32)).astype(bf16)
    return high, mid, low


def dispatch_kernel(routes_ref, mask_ref, tokens_ref, cotangent_ref, sent_ref, select_ref):
    experts, both, _ = sent_ref.shape
    capacity = both // 2
    tok_rows, top_count = routes_ref.shape
    slots = experts * capacity

    @pl.when(pl.program_id(0) == 0)
    def _():
        lane = lax.broadcasted_iota(jnp.int32, (tok_rows, experts), 1)
        live = jnp.zeros((tok_rows, experts), f32)
        for k in range(top_count):
            live = live + jnp.where(routes_ref[:, k : k + 1] == lane, 1.0, 0.0)
        row = lax.broadcasted_iota(jnp.int32, (tok_rows, tok_rows), 0)
        column = lax.broadcasted_iota(jnp.int32, (tok_rows, tok_rows), 1)
        same = jnp.where(row == column, 1.0, 0.0).astype(bf16)
        earlier = jnp.where(row < column, 1.0, 0.0).astype(bf16)
        live = dot(live.astype(bf16), same, ROWS)
        live = jnp.where(mask_ref[...] == 1, live, 0.0)
        before = dot(live.astype(bf16), earlier)
        place = jnp.where(live > 0.5, before, -1.0).astype(bf16)
        owner = lax.broadcasted_iota(jnp.int32, (slots, experts), 0) // capacity
        spread = jnp.where(owner == lax.broadcasted_iota(jnp.int32, (slots, experts), 1), 1.0, 0.0)
        place = dot(spread.astype(bf16), place)
        index = lax.broadcasted_iota(jnp.int32, (slots, tok_rows), 0) % capacity
        select_ref[...] = jnp.where(place == index.astype(f32), 1.0, 0.0).astype(bf16)

    for half, ref in enumerate((tokens_ref, cotangent_ref)):
        packed = dot(select_ref[...], ref[...]).astype(bf16)
        sent_ref[:, half * capacity : (half + 1) * capacity, :] = packed.reshape(
            experts, capacity, ref.shape[1]
        )


def load_shards(place_ref, shard_refs, weights_ref, sems, rows):
    return [
        pltpu.make_async_copy(
            ref.at[pl.ds(0, rows)], weights_ref.at[place_ref[i]], sems.at[i]
        )
        for i, ref in enumerate(shard_refs)
    ]


def delta_kernel(shards, place_ref, slots_ref, *refs):
    shard_refs = refs[:shards]
    (router_ref, keep_ref, give_ref, delta_ref, share_ref, term_ref,
     weights_ref, flipped_ref, down_ref, sems) = refs[shards:]
    sources, both, features = slots_ref.shape
    capacity = both // 2
    slots = sources * capacity
    _, shard_rows, hidden = weights_ref.shape
    part = shard_rows // 3
    narrow = hidden // shards
    experts = router_ref.shape[0]
    copies = load_shards(place_ref, shard_refs, weights_ref, sems, shard_rows)
    for copy in copies:
        copy.start()
    expert, my_y, my_core = place_ref[shards], place_ref[shards + 1], place_ref[shards + 2]
    slot_tokens = slots_ref[:, :capacity, :].reshape(slots, features)
    slot_cotangent = slots_ref[:, capacity:, :].reshape(slots, features)
    flipped = slot_tokens.T
    ring = shards // 2
    for s in range(shards):
        away = lax.rem(s // 2 - my_y + ring, ring)
        other = jnp.bitwise_xor(my_core, s % 2)
        flipped_ref[other, away] = flipped[s * part : (s + 1) * part, :]

    stack = jnp.concatenate(split3(router_ref[...]), axis=0)
    logits = dot(slot_tokens, stack, LAST)
    logits = logits[:, :experts] + (
        logits[:, experts : 2 * experts] + logits[:, 2 * experts :]
    )
    weights = jnp.exp(logits)
    probs = weights / jnp.sum(weights, axis=1, keepdims=True)
    mine = lax.broadcasted_iota(jnp.int32, (slots, experts), 1) == expert
    own = jnp.sum(jnp.where(mine, probs, 0.0), axis=1, keepdims=True)
    rounded = own.astype(bf16).astype(f32)

    for copy in copies:
        copy.wait()
    down_ref[:, :hidden] = weights_ref[:, 2 * part : 2 * part + narrow, :].reshape(hidden, hidden)
    extra = features - hidden
    pieces = [
        weights_ref[:, 2 * part + narrow :, i * extra : (i + 1) * extra]
        for i in range(hidden // extra)
    ]
    down_ref[:, hidden:] = jnp.stack(pieces, axis=1).reshape(hidden, extra)

    prob_grad = jnp.zeros((slots, 1), f32)
    for start in range(0, hidden, CHUNK):
        columns = slice(start, start + CHUNK)
        gate = weights_ref[:, :part, columns].reshape(features, CHUNK)
        up = weights_ref[:, part : 2 * part, columns].reshape(features, CHUNK)
        gate_proj = dot(slot_tokens, gate)
        up_proj = dot(slot_tokens, up)
        hidden_grad = dot(slot_cotangent, down_ref[columns, :], LAST)
        sigmoid_gate = 1.0 / (1.0 + jnp.exp(-gate_proj))
        activated = gate_proj * sigmoid_gate
        slope = sigmoid_gate * (1.0 + gate_proj * (1.0 - sigmoid_gate))
        prob_grad = prob_grad + jnp.sum(
            hidden_grad * activated * up_proj, axis=1, keepdims=True
        )
        scaled = rounded * hidden_grad
        gate_delta = (scaled * up_proj * slope).astype(bf16)
        up_delta = (scaled * activated).astype(bf16)
        delta_ref[:, columns] = gate_delta
        delta_ref[:, hidden + start : hidden + start + CHUNK] = up_delta
        for half, delta in enumerate((gate_delta, up_delta)):
            for other, ref in enumerate((keep_ref, give_ref)):
                product = dot(flipped_ref[other].reshape(ring * part, slots), delta).astype(bf16)
                ref[:, half * part : (half + 1) * part, columns] = product.reshape(
                    ring, part, CHUNK
                )
    share = prob_grad.astype(bf16).astype(f32) * own
    share = share * (jnp.where(mine, 1.0, 0.0) - probs)
    share_ref[...] = share
    term = dot(jnp.concatenate(split3(share), axis=1), slot_tokens, ROWS)
    term_ref[...] = term[:experts] + (term[experts : 2 * experts] + term[2 * experts :])


def slot_grad_kernel(shards, place_ref, delta_ref, *refs):
    shard_refs = refs[:shards]
    share_ref, router_ref, grad_ref, weights_ref, sems = refs[shards:]
    _, shard_rows, hidden = weights_ref.shape
    part = shard_rows // 2
    features = grad_ref.shape[1]
    step = CHUNK // part
    copies = load_shards(place_ref, shard_refs, weights_ref, sems, shard_rows)
    for copy in copies:
        copy.start()
    share_high, share_mid, _ = split3(share_ref[...])
    router_high, router_mid, _ = split3(router_ref[...])
    left = jnp.concatenate([share_high, share_high, share_mid], axis=1)
    right = jnp.concatenate([router_high, router_mid, router_high], axis=0)
    for copy in copies:
        copy.wait()
    for block in range(features // CHUNK):
        gate = weights_ref[block * step : (block + 1) * step, :part, :].reshape(CHUNK, hidden)
        up = weights_ref[block * step : (block + 1) * step, part:, :].reshape(CHUNK, hidden)
        columns = slice(block * CHUNK, (block + 1) * CHUNK)
        total = dot(delta_ref[:, :hidden], gate, LAST) + dot(delta_ref[:, hidden:], up, LAST)
        grad_ref[:, columns] = (total + dot(left, right[:, columns])).astype(bf16)


def combine_kernel(select_ref, back_ref, out_ref):
    for start in range(0, out_ref.shape[1], CHUNK):
        columns = slice(start, start + CHUNK)
        out_ref[:, columns] = dot(select_ref[...], back_ref[:, columns], ROWS).astype(bf16)


def call(kernel, specs, outs, flops, size, name, scratch=(), **more):
    return pl.pallas_call(
        kernel,
        out_shape=[jax.ShapeDtypeStruct(s, d) for s, d in outs],
        in_specs=specs,
        scratch_shapes=list(scratch),
        compiler_params=pltpu.CompilerParams(vmem_limit_bytes=48 * 1024 * 1024),
        cost_estimate=pl.CostEstimate(flops=flops, bytes_accessed=size, transcendentals=0),
        name=name,
        **more,
    )


SMEM = pl.BlockSpec(memory_space=pltpu.SMEM)
VMEM = pl.BlockSpec(memory_space=pltpu.VMEM)
ANY = pl.BlockSpec(memory_space=pl.ANY)


def pack_down(down_shard, hidden):
    extra = down_shard.shape[1] - hidden
    tail = down_shard[:, hidden:].reshape(hidden // extra, -1, extra)
    return jnp.concatenate(
        [down_shard[:, :hidden], jnp.concatenate([t for t in tail], axis=1)], axis=0
    )


def turn(value, axis, by):
    size = lax.axis_size(axis)
    return lax.ppermute(value, axis, [(i, (i + by) % size) for i in range(size)])


def swap(value, axis, by=1):
    size = lax.axis_size(axis)
    return lax.ppermute(value, axis, [(i, i ^ by) for i in range(size)])


def gather_shards(shard):
    ring = lax.axis_size("y")
    y, core = lax.axis_index("y"), lax.axis_index("core")
    found = {0: shard}
    up = down = shard
    for step in range(1, ring // 2 + 1):
        up = turn(up, "y", 1)
        found[-step] = up
        if step < ring // 2:
            down = turn(down, "y", -1)
            found[step] = down
    arrays, places = [], []
    for away, array in found.items():
        row = lax.rem(y + away + ring, ring) * 2
        arrays += [array, swap(array, "core")]
        places += [row + core, row + 1 - core]
    return arrays, places


def ring_sum(keep, give):
    got = swap(give, "core")
    ring = keep.shape[0]
    half = keep.shape[1] // 2

    def chunk(r):
        return keep[r % ring].astype(f32) + got[r % ring].astype(f32)

    middle = chunk(ring // 2)
    left = turn(middle[:half].astype(bf16), "y", -1)
    right = turn(middle[half:].astype(bf16), "y", 1)
    nothing = jnp.zeros_like(left)
    left = jnp.concatenate([left, nothing], axis=0)
    right = jnp.concatenate([nothing, right], axis=0)
    for r in range(ring // 2 - 1, 0, -1):
        left = turn((chunk(-r) + left.astype(f32)).astype(bf16), "y", -1)
        right = turn((chunk(r) + right.astype(f32)).astype(bf16), "y", 1)
    return (chunk(0) + left.astype(f32) + right.astype(f32)).astype(bf16)


def per_device(
    tokens, cotangent, router_weight, gate_weight, up_weight, down_weight, routes, drop_mask
):
    tok_rows, features = tokens.shape
    experts = router_weight.shape[0]
    top_count = routes.shape[1]
    _, part, hidden = gate_weight.shape
    shards = features // part
    ring = shards // 2
    capacity = tok_rows * top_count * 2 // (3 * experts)
    slots = experts * capacity

    def whole(shape):
        return pl.BlockSpec(shape, lambda i: (0,) * len(shape))

    sent, select = call(
        dispatch_kernel,
        [
            whole((tok_rows, top_count)),
            whole((1, tok_rows)),
            pl.BlockSpec((tok_rows, CHUNK), lambda i: (0, i)),
            pl.BlockSpec((tok_rows, CHUNK), lambda i: (0, i)),
        ],
        [((experts, 2 * capacity, features), bf16), ((slots, tok_rows), bf16)],
        4 * slots * tok_rows * features,
        3 * 2**20,
        "dispatch",
        grid=(features // CHUNK,),
        out_specs=[
            pl.BlockSpec((experts, 2 * capacity, CHUNK), lambda i: (0, 0, i)),
            whole((slots, tok_rows)),
        ],
    )(routes, drop_mask.reshape(1, tok_rows), tokens, cotangent)
    slot_rows = lax.all_to_all(sent, EXPERT, split_axis=0, concat_axis=0, tiled=True)

    shard = jnp.concatenate(
        [gate_weight[0], up_weight[0], pack_down(down_weight[0], hidden)], axis=0
    )
    arrays, places = gather_shards(shard)
    places += [lax.axis_index(EXPERT), lax.axis_index("y"), lax.axis_index("core")]
    place = jnp.stack(places).astype(jnp.int32)

    keep, give, deltas, share, term = call(
        lambda *refs: delta_kernel(shards, *refs),
        [SMEM, VMEM] + [ANY] * shards + [VMEM],
        [
            ((ring, 2 * part, hidden), bf16),
            ((ring, 2 * part, hidden), bf16),
            ((slots, 2 * hidden), bf16),
            ((slots, experts), f32),
            ((experts, features), f32),
        ],
        10 * slots * features * hidden,
        10 * 2**20,
        "deltas",
        scratch=[
            pltpu.VMEM((shards, 3 * part, hidden), bf16),
            pltpu.VMEM((2, ring, part, slots), bf16),
            pltpu.VMEM((hidden, features), bf16),
            pltpu.SemaphoreType.DMA((shards,)),
        ],
    )(place, slot_rows, *arrays, router_weight)
    sums = ring_sum(keep, give)
    (slot_grad,) = call(
        lambda *refs: slot_grad_kernel(shards, *refs),
        [SMEM, VMEM] + [ANY] * shards + [VMEM, VMEM],
        [((slots, features), bf16)],
        4 * slots * features * hidden,
        6 * 2**20,
        "slot_grad",
        scratch=[
            pltpu.VMEM((shards, 2 * part, hidden), bf16),
            pltpu.SemaphoreType.DMA((shards,)),
        ],
    )(place, deltas, *arrays, share, router_weight)

    term = lax.all_to_all(term, EXPERT, split_axis=0, concat_axis=0, tiled=True)
    slot_grad, term = lax.optimization_barrier((slot_grad, term))
    back = lax.all_to_all(slot_grad, EXPERT, split_axis=0, concat_axis=0, tiled=True)
    (token_grad,) = call(
        combine_kernel,
        [VMEM, VMEM],
        [((tok_rows, features), bf16)],
        2 * slots * tok_rows * features,
        2 * 2**20,
        "combine",
    )(select, back)

    term = jnp.sum(term.reshape(experts, -1, 128), axis=0)
    for axis, by in (("core", 1), ("y", 1), ("y", 2), ("y", 4)):
        term = term + swap(term, axis, by)
    term = jnp.broadcast_to(term.reshape(1, features), (experts, features))
    router_grad = lax.all_to_all(term, EXPERT, split_axis=0, concat_axis=0, tiled=True)
    return token_grad, sums[:part][None], sums[part:][None], router_grad


def solution(mesh):
    fine = Mesh(mesh.devices.reshape(8, 2, 4, 8), DP + EXPERT)
    rows = P(DP + EXPERT, None)
    shard = P(EXPERT, DP, None)
    return jax.shard_map(
        per_device,
        mesh=fine,
        in_specs=(rows, rows, P(), shard, shard, shard, rows, P(DP + EXPERT)),
        out_specs=(rows, shard, shard, P()),
        check_vma=False,
    )
```

time: 183 us -> 219 us (1.20)
  the two profiles are of different devices: /device:TPU:1 before, /device:TPU:2 now
where the time goes in v2:
time: 219 us; the launch traced here: 217 us
  starting transfers between devices  121 us (55%)
  waiting for transfers between devices  51.4 us (23%)
  Pallas kernels  24.9 us (11%)
  local copies, waits for them, and re-layouts  11.4 us (5%)
  other arithmetic  7.51 us (3%)
    ppermute x15, starting transfers between devices, turn(): lax.ppermute(value, axis, [(i, (i + by) % size) for i in range(size)])  47.9 us
    ppermute x15, waiting for transfers between devices, turn(): lax.ppermute(value, axis, [(i, (i + by) % size) for i in range(size)])  36.4 us
    ppermute x13, starting transfers between devices, swap(): return lax.ppermute(value, axis, [(i, i ^ by) for i in range(size)])  34 us
    all_to_all x1, starting transfers between devices, per_device(): lax.all_to_all(sent, EXPERT, split_axis=0, concat_axis=0, tiled=True)  13.7 us
    pallas_call x1, Pallas kernels, per_device(): call(lambda *refs: delta_kernel(shards, *refs), [SMEM, VMEM] + [ANY] * sh...  11.4 us
    ppermute x13, waiting for transfers between devices, swap(): return lax.ppermute(value, axis, [(i, i ^ by) for i in range(size)])  10.7 us
    all_to_all x1, starting transfers between devices, per_device(): term = lax.all_to_all(term, EXPERT, split_axis=0, concat_axis=0, tiled=True)  9.85 us
    all_to_all x1, starting transfers between devices, per_device(): lax.all_to_all(term, EXPERT, split_axis=0, concat_axis=0, tiled=True)  9.78 us
  transfers between devices with their start and end apart: 32, of which 14 were waited for; matrix products, arithmetic and copies ran while one was open for 4% of the time, Pallas kernels for 5%

profile of v2, /device:TPU:2, one launch (start us, length us, event | category | flops | bytes accessed | tf_op | source)
XLA Modules:
  0.0 217.1 jit_solution(13911725889763442734)
XLA Ops:
  0.6 0.8 copy.13.routes_ref
  1.4 0.9 copy-done.6
  2.4 0.9 copy-done.7
  4.0 3.3 %dispatch.1 = (bf16[32,32,1024]{2,1,0:T(8,128)(2,1)}, bf16[512,128]{1,0:T(8,128)(2,1)S(1)}) custom-call(s32[128,6]{1,0:T(8,128)S(1)} %copy.13.routes_ref, s32[1,128]{1,0:T(1,128)S(1)} %bitcast.78, bf16[128,1024]{1,0:T(8,128)(2,1)S(1)} %copy-done.6, bf16[128,1024]{1,0:T(8,128)(2,1)S(1)} %copy-done.7), custom_call_target="tpu_custom_call" | custom-call | flops 268435456 | bytes 3145728 | tf_op jit(solution)/shard_map/dispatch/pallas_call | solution.py:269
  7.9 13.7 %all-to-all-start = ((bf16[32,32,1024]{2,1,0:T(8,128)(2,1)}), bf16[32,32,1024]{2,1,0:T(8,128)(2,1)}, u32[]{:S(2)}, u32[]{:S(2)}) async-start(bf16[32,32,1024]{2,1,0:T(8,128)(2,1)} %get-tuple-element.14), calls=%async_computation | async-start | bytes 4194304 | tf_op jit(solution)/shard_map/all_to_all | solution.py:287
  21.7 3.5 %collective-permute-start.1 = (bf16[192,768]{1,0:T(8,128)(2,1)S(1)}, bf16[192,768]{1,0:T(8,128)(2,1)S(1)}, u32[]{:S(2)}, u32[]{:S(2)}) collective-permute-start(bf16[192,768]{1,0:T(8,128)(2,1)S(1)} %maximum_maximum_fusion.refs_2_), channel_id=1, source_target_pairs={{0,64},{64,128},{128,192},{192,256},{256,320},{320,384},{384,448},... | collective-permute-start | bytes 884744 | tf_op jit(solution)/shard_map/ppermute | solution.py:207
  25.2 3.8 %collective-permute-start.3 = (bf16[192,768]{1,0:T(8,128)(2,1)S(1)}, bf16[192,768]{1,0:T(8,128)(2,1)S(1)}, u32[]{:S(2)}, u32[]{:S(2)}) collective-permute-start(bf16[192,768]{1,0:T(8,128)(2,1)S(1)} %maximum_maximum_fusion.refs_2_), channel_id=1, source_target_pairs={{0,448},{64,0},{128,64},{192,128},{256,192},{320,256},{384,320},{4... | collective-permute-start | bytes 884744 | tf_op jit(solution)/shard_map/ppermute | solution.py:207
  29.0 4.5 %collective-permute-done.1.refs_4_ = bf16[192,768]{1,0:T(8,128)(2,1)S(1)} collective-permute-done((bf16[192,768]{1,0:T(8,128)(2,1)S(1)}, bf16[192,768]{1,0:T(8,128)(2,1)S(1)}, u32[]{:S(2)}, u32[]{:S(2)}) %collective-permute-start.1) | collective-permute-done | bytes 294944 | tf_op jit(solution)/shard_map/ppermute | solution.py:207
  33.5 1.9 collective-permute-start.5
  35.4 5.1 %collective-permute-start.7 = (bf16[192,768]{1,0:T(8,128)(2,1)S(1)}, bf16[192,768]{1,0:T(8,128)(2,1)S(1)}, u32[]{:S(2)}, u32[]{:S(2)}) collective-permute-start(bf16[192,768]{1,0:T(8,128)(2,1)S(1)} %collective-permute-done.3.refs_6_), channel_id=1, source_target_pairs={{0,448},{64,0},{128,64},{192,128},{256,192},{320,256},{384,320},{4... | collective-permute-start | bytes 884744 | tf_op jit(solution)/shard_map/ppermute | solution.py:207
  40.6 3.7 %collective-permute-done.5.refs_8_ = bf16[192,768]{1,0:T(8,128)(2,1)S(1)} collective-permute-done((bf16[192,768]{1,0:T(8,128)(2,1)S(1)}, bf16[192,768]{1,0:T(8,128)(2,1)S(1)}, u32[]{:S(2)}, u32[]{:S(2)}) %collective-permute-start.5) | collective-permute-done | bytes 294944 | tf_op jit(solution)/shard_map/ppermute | solution.py:207
  44.3 1.9 collective-permute-start.9
  46.2 1.9 collective-permute-start
  48.1 2.4 %collective-permute-start.4 = (bf16[192,768]{1,0:T(8,128)(2,1)S(1)}, bf16[192,768]{1,0:T(8,128)(2,1)S(1)}, u32[]{:S(2)}, u32[]{:S(2)}) collective-permute-start(bf16[192,768]{1,0:T(8,128)(2,1)S(1)} %collective-permute-done.3.refs_6_), channel_id=1, source_target_pairs={{0,32},{32,0},{1,33},{33,1},{2,34},{34,2},{3,35},{35,3},{4,36},{36... | collective-permute-start | bytes 884744 | tf_op jit(solution)/shard_map/ppermute | solution.py:212
  50.5 1.9 collective-permute-start.2
  52.5 5.1 %collective-permute-start.11 = (bf16[192,768]{1,0:T(8,128)(2,1)S(1)}, bf16[192,768]{1,0:T(8,128)(2,1)S(1)}, u32[]{:S(2)}, u32[]{:S(2)}) collective-permute-start(bf16[192,768]{1,0:T(8,128)(2,1)S(1)} %collective-permute-done.7.refs_10_), channel_id=1, source_target_pairs={{0,448},{64,0},{128,64},{192,128},{256,192},{320,256},{384,320},{4... | collective-permute-start | bytes 884744 | tf_op jit(solution)/shard_map/ppermute | solution.py:207
  57.6 1.9 collective-permute-start.13
  59.6 2.1 collective-permute-start.8
  61.7 2.2 %collective-permute-start.6 = (bf16[192,768]{1,0:T(8,128)(2,1)S(1)}, bf16[192,768]{1,0:T(8,128)(2,1)}, u32[]{:S(2)}, u32[]{:S(2)}) collective-permute-start(bf16[192,768]{1,0:T(8,128)(2,1)S(1)} %collective-permute-done.5.refs_8_), channel_id=1, source_target_pairs={{0,32},{32,0},{1,33},{33,1},{2,34},{34,2},{3,35},{35,3},{4,36},{36... | collective-permute-start | bytes 884744 | tf_op jit(solution)/shard_map/ppermute | solution.py:212
  63.9 2.1 collective-permute-start.10
  66.1 2.2 %collective-permute-start.12 = (bf16[192,768]{1,0:T(8,128)(2,1)S(1)}, bf16[192,768]{1,0:T(8,128)(2,1)}, u32[]{:S(2)}, u32[]{:S(2)}) collective-permute-start(bf16[192,768]{1,0:T(8,128)(2,1)S(1)} %collective-permute-done.11.refs_14_), channel_id=1, source_target_pairs={{0,32},{32,0},{1,33},{33,1},{2,34},{34,2},{3,35},{35,3},{4,36},{36... | collective-permute-start | bytes 884744 | tf_op jit(solution)/shard_map/ppermute | solution.py:212
  68.3 1.6 collective-permute-done.13.refs_16_
  69.9 1.9 collective-permute-start.14
  72.0 1.5 collective-permute-done.14.refs_17_
  73.5 0.9 copy-done.2
  74.4 11.4 %deltas.1 = (bf16[8,128,768]{2,1,0:T(8,128)(2,1)}, bf16[8,128,768]{2,1,0:T(8,128)(2,1)}, bf16[512,1536]{1,0:T(8,128)(2,1)}, f32[512,32]{1,0:T(8,128)S(1)}, f32[32,1024]{1,0:T(8,128)S(1)}) custom-call(s32[19]{0:T(128)S(1)} %stack.79.refs_0_, bf16[32,32,1024]{2,1,0:T(8,128)(2,1)} %all-to-all-done.refs_1_, bf16[192,768]{1,0:T(8,128)(2,1)S(1)} %maximum_maximum_fusion.refs_2_, ...), custom_call_target="tpu_custom_call" | custom-call | flops 4026531840 | bytes 10485760 | tf_op jit(solution)/shard_map/deltas/pallas_call | solution.py:296
  86.5 2.0 collective-permute-start.15
  89.3 9.9 %all-to-all-start.1 = ((f32[32,1,1024]{2,1,0:T(1,128)}), f32[32,1,1024]{2,1,0:T(1,128)}, u32[]{:S(2)}, u32[]{:S(2)}) async-start(f32[32,1,1024]{2,1,0:T(1,128)} %copy.14), calls=%async_computation.1 | async-start | bytes 262144 | tf_op jit(solution)/shard_map/all_to_all | solution.py:330
  99.2 0.9 copy-done.1
  100.1 0.9 copy-done.3
  101.0 9.1 %slot_grad.1 = bf16[512,1024]{1,0:T(8,128)(2,1)} custom-call(s32[19]{0:T(128)S(1)} %stack.79.refs_0_, bf16[512,1536]{1,0:T(8,128)(2,1)} %get-tuple-element.15.refs_1_, bf16[192,768]{1,0:T(8,128)(2,1)S(1)} %maximum_maximum_fusion.refs_2_, bf16[192,768]{1,0:T(8,128)(2,1)S(1)} %collective-permute-done.refs_3_, ...), custom_call_target="tpu_custom_call" | custom-call | flops 1610612736 | bytes 6291456 | tf_op jit(solution)/shard_map/slot_grad/pallas_call | solution.py:317
  110.2 0.9 copy.20
  111.1 1.9 collective-permute-start.24
  113.1 1.1 collective-permute-done.24
  114.2 1.9 collective-permute-start.25
  116.1 3.6 %collective-permute-done.25 = f32[8,128]{1,0:T(8,128)S(1)} collective-permute-done((f32[8,128]{1,0:T(8,128)S(1)}, f32[8,128]{1,0:T(8,128)S(1)}, u32[]{:S(2)}, u32[]{:S(2)}) %collective-permute-start.25) | collective-permute-done | bytes 4128 | tf_op jit(solution)/shard_map/ppermute | solution.py:212
  119.7 4.4 %collective-permute-start.26 = (f32[8,128]{1,0:T(8,128)S(1)}, f32[8,128]{1,0:T(8,128)S(1)}, u32[]{:S(2)}, u32[]{:S(2)}) collective-permute-start(f32[8,128]{1,0:T(8,128)S(1)} %fusion.9), channel_id=1, source_target_pairs={{0,128},{64,192},{128,0},{192,64},{256,384},{320,448},{384,256},{4... | collective-permute-start | bytes 12296 | tf_op jit(solution)/shard_map/ppermute | solution.py:212
  124.1 1.9 collective-permute-done.26
  126.1 6.9 %collective-permute-start.27 = (f32[8,128]{1,0:T(8,128)S(1)}, f32[8,128]{1,0:T(8,128)S(1)}, u32[]{:S(2)}, u32[]{:S(2)}) collective-permute-start(f32[8,128]{1,0:T(8,128)S(1)} %add.232), channel_id=1, source_target_pairs={{0,256},{64,320},{128,384},{192,448},{256,0},{320,64},{384,128},{4... | collective-permute-start | bytes 12296 | tf_op jit(solution)/shard_map/ppermute | solution.py:212
  133.0 2.5 %collective-permute-done.27 = f32[8,128]{1,0:T(8,128)S(1)} collective-permute-done((f32[8,128]{1,0:T(8,128)S(1)}, f32[8,128]{1,0:T(8,128)S(1)}, u32[]{:S(2)}, u32[]{:S(2)}) %collective-permute-start.27) | collective-permute-done | bytes 4128 | tf_op jit(solution)/shard_map/ppermute | solution.py:212
  136.2 9.8 %all-to-all-start.3 = ((f32[32,1,1024]{2,1,0:T(1,128)}), f32[32,1,1024]{2,1,0:T(1,128)S(1)}, u32[]{:S(2)}, u32[]{:S(2)}) async-start(f32[32,1,1024]{2,1,0:T(1,128)} %broadcast_in_dim.17), calls=%async_computation.3 | async-start | bytes 262144 | tf_op jit(solution)/shard_map/all_to_all | solution.py:346
  146.0 1.2 add_convert_fusion
  147.2 3.6 %collective-permute-start.16 = (bf16[64,768]{1,0:T(8,128)(2,1)S(1)}, bf16[64,768]{1,0:T(8,128)(2,1)S(1)}, u32[]{:S(2)}, u32[]{:S(2)}) collective-permute-start(bf16[64,768]{1,0:T(8,128)(2,1)S(1)} %get-tuple-element.26), channel_id=1, source_target_pairs={{0,448},{64,0},{128,64},{192,128},{256,192},{320,256},{384,320},{4... | collective-permute-start | bytes 294920 | tf_op jit(solution)/shard_map/ppermute | solution.py:207
  150.8 4.3 %all-to-all-done.3 = f32[32,1,1024]{2,1,0:T(1,128)S(1)} async-done(((f32[32,1,1024]{2,1,0:T(1,128)}), f32[32,1,1024]{2,1,0:T(1,128)S(1)}, u32[]{:S(2)}, u32[]{:S(2)}) %all-to-all-start.3) | async-done | bytes 131104 | tf_op jit(solution)/shard_map/all_to_all | solution.py:346
  155.1 5.5 %all-to-all-start.2 = ((bf16[32,16,1024]{2,1,0:T(8,128)(2,1)}), bf16[32,16,1024]{2,1,0:T(8,128)(2,1)S(1)}, u32[]{:S(2)}, u32[]{:S(2)}) async-start(bf16[32,16,1024]{2,1,0:T(8,128)(2,1)} %bitcast.24), calls=%async_computation.2 | async-start | bytes 2097152 | tf_op jit(solution)/shard_map/all_to_all | solution.py:332
  160.6 1.0 fusion.3
  161.6 3.4 %collective-permute-start.17 = (bf16[128,768]{1,0:T(8,128)(2,1)S(1)}, bf16[128,768]{1,0:T(8,128)(2,1)S(1)}, u32[]{:S(2)}, u32[]{:S(2)}) collective-permute-start(bf16[128,768]{1,0:T(8,128)(2,1)S(1)} %fusion.3), channel_id=1, source_target_pairs={{0,448},{64,0},{128,64},{192,128},{256,192},{320,256},{384,320},{4... | collective-permute-start | bytes 589832 | tf_op jit(solution)/shard_map/ppermute | solution.py:207
  165.1 4.1 %collective-permute-done.17 = bf16[128,768]{1,0:T(8,128)(2,1)S(1)} collective-permute-done((bf16[128,768]{1,0:T(8,128)(2,1)S(1)}, bf16[128,768]{1,0:T(8,128)(2,1)S(1)}, u32[]{:S(2)}, u32[]{:S(2)}) %collective-permute-start.17) | collective-permute-done | bytes 196640 | tf_op jit(solution)/shard_map/ppermute | solution.py:207
  169.2 1.0 fusion.4
  170.2 4.7 %collective-permute-start.18 = (bf16[128,768]{1,0:T(8,128)(2,1)S(1)}, bf16[128,768]{1,0:T(8,128)(2,1)S(1)}, u32[]{:S(2)}, u32[]{:S(2)}) collective-permute-start(bf16[128,768]{1,0:T(8,128)(2,1)S(1)} %fusion.4), channel_id=1, source_target_pairs={{0,448},{64,0},{128,64},{192,128},{256,192},{320,256},{384,320},{4... | collective-permute-start | bytes 589832 | tf_op jit(solution)/shard_map/ppermute | solution.py:207
  174.9 2.1 collective-permute-start.20
  176.9 5.8 %collective-permute-done.20 = bf16[64,768]{1,0:T(8,128)(2,1)S(1)} collective-permute-done((bf16[64,768]{1,0:T(8,128)(2,1)S(1)}, bf16[64,768]{1,0:T(8,128)(2,1)S(1)}, u32[]{:S(2)}, u32[]{:S(2)}) %collective-permute-start.20) | collective-permute-done | bytes 98336 | tf_op jit(solution)/shard_map/ppermute | solution.py:207
  182.7 1.2 fusion.5
  183.9 1.9 collective-permute-start.21
  185.8 8.0 %collective-permute-done.21 = bf16[128,768]{1,0:T(8,128)(2,1)S(1)} collective-permute-done((bf16[128,768]{1,0:T(8,128)(2,1)S(1)}, bf16[128,768]{1,0:T(8,128)(2,1)S(1)}, u32[]{:S(2)}, u32[]{:S(2)}) %collective-permute-start.21) | collective-permute-done | bytes 196640 | tf_op jit(solution)/shard_map/ppermute | solution.py:207
  193.8 1.0 fusion.1
  194.8 1.9 collective-permute-start.22
  196.7 5.1 %collective-permute-start.19 = (bf16[128,768]{1,0:T(8,128)(2,1)S(1)}, bf16[128,768]{1,0:T(8,128)(2,1)}, u32[]{:S(2)}, u32[]{:S(2)}) collective-permute-start(bf16[128,768]{1,0:T(8,128)(2,1)S(1)} %get-tuple-element.22), channel_id=1, source_target_pairs={{0,448},{64,0},{128,64},{192,128},{256,192},{320,256},{384,320},{4... | collective-permute-start | bytes 589832 | tf_op jit(solution)/shard_map/ppermute | solution.py:207
  201.9 3.6 %collective-permute-done.22 = bf16[128,768]{1,0:T(8,128)(2,1)S(1)} collective-permute-done((bf16[128,768]{1,0:T(8,128)(2,1)S(1)}, bf16[128,768]{1,0:T(8,128)(2,1)S(1)}, u32[]{:S(2)}, u32[]{:S(2)}) %collective-permute-start.22) | collective-permute-done | bytes 196640 | tf_op jit(solution)/shard_map/ppermute | solution.py:207
  205.5 1.0 fusion.2
  206.5 1.9 collective-permute-start.23
  209.1 1.1 combine.1
  210.2 5.1 %collective-permute-done.23 = bf16[128,768]{1,0:T(8,128)(2,1)S(1)} collective-permute-done((bf16[128,768]{1,0:T(8,128)(2,1)S(1)}, bf16[128,768]{1,0:T(8,128)(2,1)S(1)}, u32[]{:S(2)}, u32[]{:S(2)}) %collective-permute-start.23) | collective-permute-done | bytes 196640 | tf_op jit(solution)/shard_map/ppermute | solution.py:207
  215.3 1.1 fusion.7
  (53 shorter events, 5.1 us)
Async XLA Ops:
  1.4 0.9 copy-start.6
  2.4 0.9 copy-start.7
  3.3 0.7 copy-start.8
  7.3 0.7 copy-start.4
  7.9 13.7 %copy-start.12 = (bf16[1,48,1024]{2,1,0:T(8,128)(2,1)S(1)}, bf16[1,48,1024]{2,1,0:T(8,128)(2,1)}, u32[]{:S(2)}) copy-start(bf16[1,48,1024]{2,1,0:T(8,128)(2,1)} %param.13) | copy-start | bytes 294916
  7.9 13.7 %copy-start.10 = (bf16[1,64,768]{2,1,0:T(8,128)(2,1)S(1)}, bf16[1,64,768]{2,1,0:T(8,128)(2,1)}, u32[]{:S(2)}) copy-start(bf16[1,64,768]{2,1,0:T(8,128)(2,1)} %param.12) | copy-start | bytes 294916
  7.9 13.7 %copy-start.11 = (bf16[1,64,768]{2,1,0:T(8,128)(2,1)S(1)}, bf16[1,64,768]{2,1,0:T(8,128)(2,1)}, u32[]{:S(2)}) copy-start(bf16[1,64,768]{2,1,0:T(8,128)(2,1)} %param.11) | copy-start | bytes 294916
  7.9 65.5 %all-to-all-start = ((bf16[32,32,1024]{2,1,0:T(8,128)(2,1)}), bf16[32,32,1024]{2,1,0:T(8,128)(2,1)}, u32[]{:S(2)}, u32[]{:S(2)}) async-start(bf16[32,32,1024]{2,1,0:T(8,128)(2,1)} %get-tuple-element.14), calls=%async_computation | async-start | bytes 4194304 | tf_op jit(solution)/shard_map/all_to_all | solution.py:287
  21.7 11.8 %collective-permute-start.1 = (bf16[192,768]{1,0:T(8,128)(2,1)S(1)}, bf16[192,768]{1,0:T(8,128)(2,1)S(1)}, u32[]{:S(2)}, u32[]{:S(2)}) collective-permute-start(bf16[192,768]{1,0:T(8,128)(2,1)S(1)} %maximum_maximum_fusion.refs_2_), channel_id=1, source_target_pairs={{0,64},{64,128},{128,192},{192,256},{256,320},{320,384},{384,448},... | collective-permute-start | bytes 884744 | tf_op jit(solution)/shard_map/ppermute | solution.py:207
  25.2 10.2 %collective-permute-start.3 = (bf16[192,768]{1,0:T(8,128)(2,1)S(1)}, bf16[192,768]{1,0:T(8,128)(2,1)S(1)}, u32[]{:S(2)}, u32[]{:S(2)}) collective-permute-start(bf16[192,768]{1,0:T(8,128)(2,1)S(1)} %maximum_maximum_fusion.refs_2_), channel_id=1, source_target_pairs={{0,448},{64,0},{128,64},{192,128},{256,192},{320,256},{384,320},{4... | collective-permute-start | bytes 884744 | tf_op jit(solution)/shard_map/ppermute | solution.py:207
  33.5 10.8 %collective-permute-start.5 = (bf16[192,768]{1,0:T(8,128)(2,1)S(1)}, bf16[192,768]{1,0:T(8,128)(2,1)S(1)}, u32[]{:S(2)}, u32[]{:S(2)}) collective-permute-start(bf16[192,768]{1,0:T(8,128)(2,1)S(1)} %collective-permute-done.1.refs_4_), channel_id=1, source_target_pairs={{0,64},{64,128},{128,192},{192,256},{256,320},{320,384},{384,448},... | collective-permute-start | bytes 884744 | tf_op jit(solution)/shard_map/ppermute | solution.py:207
  35.4 17.0 %collective-permute-start.7 = (bf16[192,768]{1,0:T(8,128)(2,1)S(1)}, bf16[192,768]{1,0:T(8,128)(2,1)S(1)}, u32[]{:S(2)}, u32[]{:S(2)}) collective-permute-start(bf16[192,768]{1,0:T(8,128)(2,1)S(1)} %collective-permute-done.3.refs_6_), channel_id=1, source_target_pairs={{0,448},{64,0},{128,64},{192,128},{256,192},{320,256},{384,320},{4... | collective-permute-start | bytes 884744 | tf_op jit(solution)/shard_map/ppermute | solution.py:207
  44.3 13.3 %collective-permute-start.9 = (bf16[192,768]{1,0:T(8,128)(2,1)S(1)}, bf16[192,768]{1,0:T(8,128)(2,1)S(1)}, u32[]{:S(2)}, u32[]{:S(2)}) collective-permute-start(bf16[192,768]{1,0:T(8,128)(2,1)S(1)} %collective-permute-done.5.refs_8_), channel_id=1, source_target_pairs={{0,64},{64,128},{128,192},{192,256},{256,320},{320,384},{384,448},... | collective-permute-start | bytes 884744 | tf_op jit(solution)/shard_map/ppermute | solution.py:207
  46.2 13.4 %collective-permute-start = (bf16[192,768]{1,0:T(8,128)(2,1)S(1)}, bf16[192,768]{1,0:T(8,128)(2,1)S(1)}, u32[]{:S(2)}, u32[]{:S(2)}) collective-permute-start(bf16[192,768]{1,0:T(8,128)(2,1)S(1)} %maximum_maximum_fusion.refs_2_), channel_id=1, source_target_pairs={{0,32},{32,0},{1,33},{33,1},{2,34},{34,2},{3,35},{35,3},{4,36},{36... | collective-permute-start | bytes 884744 | tf_op jit(solution)/shard_map/ppermute | solution.py:212
  48.1 13.6 %collective-permute-start.4 = (bf16[192,768]{1,0:T(8,128)(2,1)S(1)}, bf16[192,768]{1,0:T(8,128)(2,1)S(1)}, u32[]{:S(2)}, u32[]{:S(2)}) collective-permute-start(bf16[192,768]{1,0:T(8,128)(2,1)S(1)} %collective-permute-done.3.refs_6_), channel_id=1, source_target_pairs={{0,32},{32,0},{1,33},{33,1},{2,34},{34,2},{3,35},{35,3},{4,36},{36... | collective-permute-start | bytes 884744 | tf_op jit(solution)/shard_map/ppermute | solution.py:212
  50.5 13.4 %collective-permute-start.2 = (bf16[192,768]{1,0:T(8,128)(2,1)S(1)}, bf16[192,768]{1,0:T(8,128)(2,1)S(1)}, u32[]{:S(2)}, u32[]{:S(2)}) collective-permute-start(bf16[192,768]{1,0:T(8,128)(2,1)S(1)} %collective-permute-done.1.refs_4_), channel_id=1, source_target_pairs={{0,32},{32,0},{1,33},{33,1},{2,34},{34,2},{3,35},{35,3},{4,36},{36... | collective-permute-start | bytes 884744 | tf_op jit(solution)/shard_map/ppermute | solution.py:212
  52.5 13.6 %collective-permute-start.11 = (bf16[192,768]{1,0:T(8,128)(2,1)S(1)}, bf16[192,768]{1,0:T(8,128)(2,1)S(1)}, u32[]{:S(2)}, u32[]{:S(2)}) collective-permute-start(bf16[192,768]{1,0:T(8,128)(2,1)S(1)} %collective-permute-done.7.refs_10_), channel_id=1, source_target_pairs={{0,448},{64,0},{128,64},{192,128},{256,192},{320,256},{384,320},{4... | collective-permute-start | bytes 884744 | tf_op jit(solution)/shard_map/ppermute | solution.py:207
  57.6 12.2 %collective-permute-start.13 = (bf16[192,768]{1,0:T(8,128)(2,1)S(1)}, bf16[192,768]{1,0:T(8,128)(2,1)S(1)}, u32[]{:S(2)}, u32[]{:S(2)}) collective-permute-start(bf16[192,768]{1,0:T(8,128)(2,1)S(1)} %collective-permute-done.9.refs_12_), channel_id=1, source_target_pairs={{0,64},{64,128},{128,192},{192,256},{256,320},{320,384},{384,448},... | collective-permute-start | bytes 884744 | tf_op jit(solution)/shard_map/ppermute | solution.py:207
  59.6 12.3 %collective-permute-start.8 = (bf16[192,768]{1,0:T(8,128)(2,1)S(1)}, bf16[192,768]{1,0:T(8,128)(2,1)S(1)}, u32[]{:S(2)}, u32[]{:S(2)}) collective-permute-start(bf16[192,768]{1,0:T(8,128)(2,1)S(1)} %collective-permute-done.7.refs_10_), channel_id=1, source_target_pairs={{0,32},{32,0},{1,33},{33,1},{2,34},{34,2},{3,35},{35,3},{4,36},{36... | collective-permute-start | bytes 884744 | tf_op jit(solution)/shard_map/ppermute | solution.py:212
  61.7 10.2 %collective-permute-start.6 = (bf16[192,768]{1,0:T(8,128)(2,1)S(1)}, bf16[192,768]{1,0:T(8,128)(2,1)}, u32[]{:S(2)}, u32[]{:S(2)}) collective-permute-start(bf16[192,768]{1,0:T(8,128)(2,1)S(1)} %collective-permute-done.5.refs_8_), channel_id=1, source_target_pairs={{0,32},{32,0},{1,33},{33,1},{2,34},{34,2},{3,35},{35,3},{4,36},{36... | collective-permute-start | bytes 884744 | tf_op jit(solution)/shard_map/ppermute | solution.py:212
  63.9 8.0 %collective-permute-start.10 = (bf16[192,768]{1,0:T(8,128)(2,1)S(1)}, bf16[192,768]{1,0:T(8,128)(2,1)}, u32[]{:S(2)}, u32[]{:S(2)}) collective-permute-start(bf16[192,768]{1,0:T(8,128)(2,1)S(1)} %collective-permute-done.9.refs_12_), channel_id=1, source_target_pairs={{0,32},{32,0},{1,33},{33,1},{2,34},{34,2},{3,35},{35,3},{4,36},{36... | collective-permute-start | bytes 884744 | tf_op jit(solution)/shard_map/ppermute | solution.py:212
  66.1 5.9 %collective-permute-start.12 = (bf16[192,768]{1,0:T(8,128)(2,1)S(1)}, bf16[192,768]{1,0:T(8,128)(2,1)}, u32[]{:S(2)}, u32[]{:S(2)}) collective-permute-start(bf16[192,768]{1,0:T(8,128)(2,1)S(1)} %collective-permute-done.11.refs_14_), channel_id=1, source_target_pairs={{0,32},{32,0},{1,33},{33,1},{2,34},{34,2},{3,35},{35,3},{4,36},{36... | collective-permute-start | bytes 884744 | tf_op jit(solution)/shard_map/ppermute | solution.py:212
  69.9 3.6 %collective-permute-start.14 = (bf16[192,768]{1,0:T(8,128)(2,1)S(1)}, bf16[192,768]{1,0:T(8,128)(2,1)}, u32[]{:S(2)}, u32[]{:S(2)}) collective-permute-start(bf16[192,768]{1,0:T(8,128)(2,1)S(1)} %collective-permute-done.13.refs_16_), channel_id=1, source_target_pairs={{0,32},{32,0},{1,33},{33,1},{2,34},{34,2},{3,35},{35,3},{4,36},{36... | collective-permute-start | bytes 884744 | tf_op jit(solution)/shard_map/ppermute | solution.py:212
  73.5 0.9 copy-start.2
  85.8 0.7 copy-start
  86.5 59.5 %collective-permute-start.15 = (bf16[8,128,768]{2,1,0:T(8,128)(2,1)}, bf16[8,128,768]{2,1,0:T(8,128)(2,1)}, u32[]{:S(2)}, u32[]{:S(2)}) collective-permute-start(bf16[8,128,768]{2,1,0:T(8,128)(2,1)} %get-tuple-element.20), channel_id=1, source_target_pairs={{0,32},{32,0},{1,33},{33,1},{2,34},{34,2},{3,35},{35,3},{4,36},{36... | collective-permute-start | bytes 4718600 | tf_op jit(solution)/shard_map/ppermute | solution.py:212
  89.3 20.8 %all-to-all-start.1 = ((f32[32,1,1024]{2,1,0:T(1,128)}), f32[32,1,1024]{2,1,0:T(1,128)}, u32[]{:S(2)}, u32[]{:S(2)}) async-start(f32[32,1,1024]{2,1,0:T(1,128)} %copy.14), calls=%async_computation.1 | async-start | bytes 262144 | tf_op jit(solution)/shard_map/all_to_all | solution.py:330
  99.2 1.0 copy-start.1
  100.1 0.9 copy-start.3
  111.1 3.1 %collective-permute-start.24 = (f32[8,128]{1,0:T(8,128)S(1)}, f32[8,128]{1,0:T(8,128)S(1)}, u32[]{:S(2)}, u32[]{:S(2)}) collective-permute-start(f32[8,128]{1,0:T(8,128)S(1)} %bitcast.85), channel_id=1, source_target_pairs={{0,32},{32,0},{1,33},{33,1},{2,34},{34,2},{3,35},{35,3},{4,36},{36... | collective-permute-start | bytes 12296 | tf_op jit(solution)/shard_map/ppermute | solution.py:212
  114.2 5.5 %collective-permute-start.25 = (f32[8,128]{1,0:T(8,128)S(1)}, f32[8,128]{1,0:T(8,128)S(1)}, u32[]{:S(2)}, u32[]{:S(2)}) collective-permute-start(f32[8,128]{1,0:T(8,128)S(1)} %bitcast_add_fusion.7), channel_id=1, source_target_pairs={{0,64},{64,0},{128,192},{192,128},{256,320},{320,256},{384,448},{4... | collective-permute-start | bytes 12296 | tf_op jit(solution)/shard_map/ppermute | solution.py:212
  119.7 6.4 %collective-permute-start.26 = (f32[8,128]{1,0:T(8,128)S(1)}, f32[8,128]{1,0:T(8,128)S(1)}, u32[]{:S(2)}, u32[]{:S(2)}) collective-permute-start(f32[8,128]{1,0:T(8,128)S(1)} %fusion.9), channel_id=1, source_target_pairs={{0,128},{64,192},{128,0},{192,64},{256,384},{320,448},{384,256},{4... | collective-permute-start | bytes 12296 | tf_op jit(solution)/shard_map/ppermute | solution.py:212
  126.1 9.4 %collective-permute-start.27 = (f32[8,128]{1,0:T(8,128)S(1)}, f32[8,128]{1,0:T(8,128)S(1)}, u32[]{:S(2)}, u32[]{:S(2)}) collective-permute-start(f32[8,128]{1,0:T(8,128)S(1)} %add.232), channel_id=1, source_target_pairs={{0,256},{64,320},{128,384},{192,448},{256,0},{320,64},{384,128},{4... | collective-permute-start | bytes 12296 | tf_op jit(solution)/shard_map/ppermute | solution.py:212
  136.2 18.9 %all-to-all-start.3 = ((f32[32,1,1024]{2,1,0:T(1,128)}), f32[32,1,1024]{2,1,0:T(1,128)S(1)}, u32[]{:S(2)}, u32[]{:S(2)}) async-start(f32[32,1,1024]{2,1,0:T(1,128)} %broadcast_in_dim.17), calls=%async_computation.3 | async-start | bytes 262144 | tf_op jit(solution)/shard_map/all_to_all | solution.py:346
  146.0 14.6 %copy-start.9 = (bf16[8,128,768]{2,1,0:T(8,128)(2,1)S(1)}, bf16[8,128,768]{2,1,0:T(8,128)(2,1)}, u32[]{:S(2)}) copy-start(bf16[8,128,768]{2,1,0:T(8,128)(2,1)} %get-tuple-element.19) | copy-start | bytes 4718596
  147.2 13.4 %collective-permute-start.16 = (bf16[64,768]{1,0:T(8,128)(2,1)S(1)}, bf16[64,768]{1,0:T(8,128)(2,1)S(1)}, u32[]{:S(2)}, u32[]{:S(2)}) collective-permute-start(bf16[64,768]{1,0:T(8,128)(2,1)S(1)} %get-tuple-element.26), channel_id=1, source_target_pairs={{0,448},{64,0},{128,64},{192,128},{256,192},{320,256},{384,320},{4... | collective-permute-start | bytes 294920 | tf_op jit(solution)/shard_map/ppermute | solution.py:207
  155.1 54.0 %all-to-all-start.2 = ((bf16[32,16,1024]{2,1,0:T(8,128)(2,1)}), bf16[32,16,1024]{2,1,0:T(8,128)(2,1)S(1)}, u32[]{:S(2)}, u32[]{:S(2)}) async-start(bf16[32,16,1024]{2,1,0:T(8,128)(2,1)} %bitcast.24), calls=%async_computation.2 | async-start | bytes 2097152 | tf_op jit(solution)/shard_map/all_to_all | solution.py:332
  161.6 7.6 %collective-permute-start.17 = (bf16[128,768]{1,0:T(8,128)(2,1)S(1)}, bf16[128,768]{1,0:T(8,128)(2,1)S(1)}, u32[]{:S(2)}, u32[]{:S(2)}) collective-permute-start(bf16[128,768]{1,0:T(8,128)(2,1)S(1)} %fusion.3), channel_id=1, source_target_pairs={{0,448},{64,0},{128,64},{192,128},{256,192},{320,256},{384,320},{4... | collective-permute-start | bytes 589832 | tf_op jit(solution)/shard_map/ppermute | solution.py:207
  170.2 12.5 %collective-permute-start.18 = (bf16[128,768]{1,0:T(8,128)(2,1)S(1)}, bf16[128,768]{1,0:T(8,128)(2,1)S(1)}, u32[]{:S(2)}, u32[]{:S(2)}) collective-permute-start(bf16[128,768]{1,0:T(8,128)(2,1)S(1)} %fusion.4), channel_id=1, source_target_pairs={{0,448},{64,0},{128,64},{192,128},{256,192},{320,256},{384,320},{4... | collective-permute-start | bytes 589832 | tf_op jit(solution)/shard_map/ppermute | solution.py:207
  174.9 34.3 %copy-start.5 = (bf16[512,128]{1,0:T(8,128)(2,1)S(1)}, bf16[512,128]{1,0:T(8,128)(2,1)}, u32[]{:S(2)}) copy-start(bf16[512,128]{1,0:T(8,128)(2,1)} %copy-done.4) | copy-start | bytes 393220
  174.9 7.9 %collective-permute-start.20 = (bf16[64,768]{1,0:T(8,128)(2,1)S(1)}, bf16[64,768]{1,0:T(8,128)(2,1)S(1)}, u32[]{:S(2)}, u32[]{:S(2)}) collective-permute-start(bf16[64,768]{1,0:T(8,128)(2,1)S(1)} %get-tuple-element.27), channel_id=1, source_target_pairs={{0,64},{64,128},{128,192},{192,256},{256,320},{320,384},{384,448},... | collective-permute-start | bytes 294920 | tf_op jit(solution)/shard_map/ppermute | solution.py:207
  183.9 9.9 %collective-permute-start.21 = (bf16[128,768]{1,0:T(8,128)(2,1)S(1)}, bf16[128,768]{1,0:T(8,128)(2,1)S(1)}, u32[]{:S(2)}, u32[]{:S(2)}) collective-permute-start(bf16[128,768]{1,0:T(8,128)(2,1)S(1)} %get-tuple-element.23), channel_id=1, source_target_pairs={{0,64},{64,128},{128,192},{192,256},{256,320},{320,384},{384,448},... | collective-permute-start | bytes 589832 | tf_op jit(solution)/shard_map/ppermute | solution.py:207
  194.8 10.7 %collective-permute-start.22 = (bf16[128,768]{1,0:T(8,128)(2,1)S(1)}, bf16[128,768]{1,0:T(8,128)(2,1)S(1)}, u32[]{:S(2)}, u32[]{:S(2)}) collective-permute-start(bf16[128,768]{1,0:T(8,128)(2,1)S(1)} %fusion.1), channel_id=1, source_target_pairs={{0,64},{64,128},{128,192},{192,256},{256,320},{320,384},{384,448},... | collective-permute-start | bytes 589832 | tf_op jit(solution)/shard_map/ppermute | solution.py:207
  196.7 13.5 %collective-permute-start.19 = (bf16[128,768]{1,0:T(8,128)(2,1)S(1)}, bf16[128,768]{1,0:T(8,128)(2,1)}, u32[]{:S(2)}, u32[]{:S(2)}) collective-permute-start(bf16[128,768]{1,0:T(8,128)(2,1)S(1)} %get-tuple-element.22), channel_id=1, source_target_pairs={{0,448},{64,0},{128,64},{192,128},{256,192},{320,256},{384,320},{4... | collective-permute-start | bytes 589832 | tf_op jit(solution)/shard_map/ppermute | solution.py:207
  206.5 8.8 %collective-permute-start.23 = (bf16[128,768]{1,0:T(8,128)(2,1)S(1)}, bf16[128,768]{1,0:T(8,128)(2,1)S(1)}, u32[]{:S(2)}, u32[]{:S(2)}) collective-permute-start(bf16[128,768]{1,0:T(8,128)(2,1)S(1)} %fusion.2), channel_id=1, source_target_pairs={{0,64},{64,128},{128,192},{192,256},{256,320},{320,384},{384,448},... | collective-permute-start | bytes 589832 | tf_op jit(solution)/shard_map/ppermute | solution.py:207

commit v3 on v2

v3 whole, which is shorter than its diff:
```python
import jax
import jax.numpy as jnp
from jax import lax
from jax.experimental import pallas as pl
from jax.experimental.pallas import tpu as pltpu
from jax.sharding import Mesh, PartitionSpec as P

f32 = jnp.float32
bf16 = jnp.bfloat16
DP = ("y", "core")
EXPERT = ("x", "z")
CHUNK = 256
ROWS = (((0,), (0,)), ((), ()))
LAST = (((1,), (1,)), ((), ()))
PLAIN = (((1,), (0,)), ((), ()))


def dot(left, right, dims=PLAIN):
    return lax.dot_general(left, right, dims, preferred_element_type=f32)


def split3(value):
    high = value.astype(bf16)
    rest = value - high.astype(f32)
    mid = rest.astype(bf16)
    low = (rest - mid.astype(f32)).astype(bf16)
    return high, mid, low


def dispatch_kernel(
    routes_ref, mask_ref, tokens_ref, cotangent_ref, sent_ref, select_ref,
    tokens, cotangent, packed, select, sems,
):
    experts, both, _ = sent_ref.shape
    capacity = both // 2
    top_count, tok_rows = routes_ref.shape
    slots = experts * capacity
    load_tokens = pltpu.make_async_copy(tokens_ref, tokens, sems.at[0])
    load_cotangent = pltpu.make_async_copy(cotangent_ref, cotangent, sems.at[1])
    load_tokens.start()
    load_cotangent.start()
    owner = lax.broadcasted_iota(jnp.int32, (experts, tok_rows), 0)
    live = jnp.zeros((experts, tok_rows), f32)
    for k in range(top_count):
        live = live + jnp.where(routes_ref[k : k + 1, :] == owner, 1.0, 0.0)
    live = jnp.where(mask_ref[...] == 1, live, 0.0)
    row = lax.broadcasted_iota(jnp.int32, (tok_rows, tok_rows), 0)
    column = lax.broadcasted_iota(jnp.int32, (tok_rows, tok_rows), 1)
    earlier = jnp.where(row < column, 1.0, 0.0).astype(bf16)
    before = dot(live.astype(bf16), earlier)
    place = jnp.where(live > 0.5, before, -1.0).astype(bf16)
    owner = lax.broadcasted_iota(jnp.int32, (slots, experts), 0) // capacity
    spread = jnp.where(owner == lax.broadcasted_iota(jnp.int32, (slots, experts), 1), 1.0, 0.0)
    place = dot(spread.astype(bf16), place)
    index = lax.broadcasted_iota(jnp.int32, (slots, tok_rows), 0) % capacity
    select[...] = jnp.where(place == index.astype(f32), 1.0, 0.0).astype(bf16)
    stores = [pltpu.make_async_copy(select, select_ref, sems.at[2])]
    stores[0].start()
    load_tokens.wait()
    load_cotangent.wait()
    pieces = 4
    step = experts // pieces
    for piece in range(pieces):
        some = slice(piece * step, (piece + 1) * step)
        rows = select[piece * step * capacity : (piece + 1) * step * capacity, :]
        for half, ref in enumerate((tokens, cotangent)):
            packed[some, half * capacity : (half + 1) * capacity, :] = (
                dot(rows, ref[...]).astype(bf16).reshape(step, capacity, ref.shape[1])
            )
        store = pltpu.make_async_copy(packed.at[some], sent_ref.at[some], sems.at[3 + piece])
        store.start()
        stores.append(store)
    for store in stores:
        store.wait()


def order_kernel(shards, place_ref, *refs):
    shard_refs = refs[:shards]
    pair_ref, down_ref = refs[shards:]
    _, both, hidden = pair_ref.shape
    narrow, features = down_ref.shape[1:]
    extra = features - hidden
    for i, ref in enumerate(shard_refs):
        place = place_ref[i]
        pair_ref[place] = ref[:both, :]
        down_ref[place, :, :hidden] = ref[both : both + narrow, :]
        down_ref[place, :, hidden:] = jnp.concatenate(
            [ref[both + narrow :, j * extra : (j + 1) * extra] for j in range(hidden // extra)],
            axis=0,
        )


def delta_kernel(
    place_ref, slots_ref, pair_ref, down_ref, router_ref,
    keep_ref, give_ref, delta_ref, share_ref, term_ref, flipped_ref,
):
    sources, both, features = slots_ref.shape
    capacity = both // 2
    slots = sources * capacity
    shards, part, hidden = pair_ref.shape
    part = part // 2
    experts = router_ref.shape[0]
    expert, my_y, my_core = place_ref[0], place_ref[1], place_ref[2]
    slot_tokens = slots_ref[:, :capacity, :].reshape(slots, features)
    slot_cotangent = slots_ref[:, capacity:, :].reshape(slots, features)
    down = down_ref[...].reshape(hidden, features)
    flipped = slot_tokens.T
    ring = shards // 2
    for s in range(shards):
        away = lax.rem(s // 2 - my_y + ring, ring)
        other = jnp.bitwise_xor(my_core, s % 2)
        flipped_ref[other, away] = flipped[s * part : (s + 1) * part, :]

    stack = jnp.concatenate(split3(router_ref[...]), axis=0)
    logits = dot(slot_tokens, stack, LAST)
    logits = logits[:, :experts] + (
        logits[:, experts : 2 * experts] + logits[:, 2 * experts :]
    )
    weights = jnp.exp(logits)
    probs = weights / jnp.sum(weights, axis=1, keepdims=True)
    mine = lax.broadcasted_iota(jnp.int32, (slots, experts), 1) == expert
    own = jnp.sum(jnp.where(mine, probs, 0.0), axis=1, keepdims=True)
    rounded = own.astype(bf16).astype(f32)

    prob_grad = jnp.zeros((slots, 1), f32)
    for start in range(0, hidden, CHUNK):
        columns = slice(start, start + CHUNK)
        gate = pair_ref[:, :part, columns].reshape(features, CHUNK)
        up = pair_ref[:, part:, columns].reshape(features, CHUNK)
        gate_proj = dot(slot_tokens, gate)
        up_proj = dot(slot_tokens, up)
        hidden_grad = dot(slot_cotangent, down[columns, :], LAST)
        sigmoid_gate = 1.0 / (1.0 + jnp.exp(-gate_proj))
        activated = gate_proj * sigmoid_gate
        slope = sigmoid_gate * (1.0 + gate_proj * (1.0 - sigmoid_gate))
        prob_grad = prob_grad + jnp.sum(
            hidden_grad * activated * up_proj, axis=1, keepdims=True
        )
        scaled = rounded * hidden_grad
        gate_delta = (scaled * up_proj * slope).astype(bf16)
        up_delta = (scaled * activated).astype(bf16)
        delta_ref[:, columns] = gate_delta
        delta_ref[:, hidden + start : hidden + start + CHUNK] = up_delta
        for half, delta in enumerate((gate_delta, up_delta)):
            for other, ref in enumerate((keep_ref, give_ref)):
                product = dot(flipped_ref[other].reshape(ring * part, slots), delta).astype(bf16)
                ref[:, half * part : (half + 1) * part, columns] = product.reshape(
                    ring, part, CHUNK
                )
    share = prob_grad.astype(bf16).astype(f32) * own
    share = share * (jnp.where(mine, 1.0, 0.0) - probs)
    share_ref[...] = share
    term = dot(jnp.concatenate(split3(share), axis=1), slot_tokens, ROWS)
    term = term[:experts] + (term[experts : 2 * experts] + term[2 * experts :])
    for i in range(term_ref.shape[1]):
        term_ref[:, i, :] = term[:, i * 128 : (i + 1) * 128]


def slot_grad_kernel(delta_ref, pair_ref, share_ref, router_ref, grad_ref):
    shards, part, hidden = pair_ref.shape
    part = part // 2
    features = grad_ref.shape[1]
    step = CHUNK // part
    share_high, share_mid, _ = split3(share_ref[...])
    router_high, router_mid, _ = split3(router_ref[...])
    left = jnp.concatenate([share_high, share_high, share_mid], axis=1)
    right = jnp.concatenate([router_high, router_mid, router_high], axis=0)
    for block in range(features // CHUNK):
        gate = pair_ref[block * step : (block + 1) * step, :part, :].reshape(CHUNK, hidden)
        up = pair_ref[block * step : (block + 1) * step, part:, :].reshape(CHUNK, hidden)
        columns = slice(block * CHUNK, (block + 1) * CHUNK)
        total = dot(delta_ref[:, :hidden], gate, LAST) + dot(delta_ref[:, hidden:], up, LAST)
        grad_ref[:, columns] = (total + dot(left, right[:, columns])).astype(bf16)


def message_kernel(keep_ref, got_ref, row_ref, own_ref, *message_refs):
    rows = keep_ref.shape[1]
    own_ref[...] = keep_ref[0].astype(f32) + got_ref[0].astype(f32)
    high, mid, _ = split3(row_ref[...])
    blank = jnp.zeros((row_ref.shape[0], keep_ref.shape[2] - 256), bf16)
    tail = jnp.concatenate([high, mid, blank], axis=1)
    for r, ref in enumerate(message_refs):
        ref[:rows, :] = (keep_ref[r + 1].astype(f32) + got_ref[r + 1].astype(f32)).astype(bf16)
        ref[rows:, :] = tail


def total_kernel(own_ref, row_ref, *refs):
    message_refs = refs[:-3]
    gate_ref, up_ref, total_ref = refs[-3:]
    half = gate_ref.shape[0]
    rows = 2 * half
    row = row_ref[...]
    for ref in message_refs:
        row = row + (ref[rows:, :128].astype(f32) + ref[rows:, 128:256].astype(f32))
    total_ref[...] = row
    for i, out_ref in enumerate((gate_ref, up_ref)):
        some = slice(i * half, (i + 1) * half)
        total = own_ref[some, :]
        for ref in message_refs:
            total = total + ref[some, :].astype(f32)
        out_ref[...] = total.astype(bf16)


def combine_kernel(select_ref, back_ref, out_ref):
    for start in range(0, out_ref.shape[1], CHUNK):
        columns = slice(start, start + CHUNK)
        out_ref[:, columns] = dot(select_ref[...], back_ref[:, columns], ROWS).astype(bf16)


def call(kernel, specs, outs, flops, size, name, mib, scratch=(), **more):
    return pl.pallas_call(
        kernel,
        out_shape=[jax.ShapeDtypeStruct(s, d) for s, d in outs],
        in_specs=specs,
        scratch_shapes=list(scratch),
        compiler_params=pltpu.CompilerParams(vmem_limit_bytes=mib * 2**20),
        cost_estimate=pl.CostEstimate(flops=flops, bytes_accessed=size, transcendentals=0),
        name=name,
        **more,
    )


SMEM = pl.BlockSpec(memory_space=pltpu.SMEM)
VMEM = pl.BlockSpec(memory_space=pltpu.VMEM)
HBM = pl.BlockSpec(memory_space=pltpu.HBM)


def pack_down(down_shard, hidden):
    extra = down_shard.shape[1] - hidden
    tail = down_shard[:, hidden:].reshape(hidden // extra, -1, extra)
    return jnp.concatenate(
        [down_shard[:, :hidden], jnp.concatenate([t for t in tail], axis=1)], axis=0
    )


def turn(value, axis, by):
    size = lax.axis_size(axis)
    return lax.ppermute(value, axis, [(i, (i + by) % size) for i in range(size)])


def swap(value, axis, by=1):
    size = lax.axis_size(axis)
    return lax.ppermute(value, axis, [(i, i ^ by) for i in range(size)])


def gather_shards(shard):
    ring = lax.axis_size("y")
    y, core = lax.axis_index("y"), lax.axis_index("core")
    found = {0: shard}
    up = down = shard
    for step in range(1, ring // 2 + 1):
        up = turn(up, "y", 1)
        found[-step] = up
        if step < ring // 2:
            down = turn(down, "y", -1)
            found[step] = down
    arrays, places = [], []
    for away, array in found.items():
        row = lax.rem(y + away + ring, ring) * 2
        arrays += [array, swap(array, "core")]
        places += [row + core, row + 1 - core]
    return arrays, places


def sum_over_dp(keep, give, row):
    got = swap(give, "core")
    row = row + swap(row, "core")
    ring, rows, hidden = keep.shape
    message = ((rows + row.shape[0], hidden), bf16)
    own, *messages = call(
        message_kernel,
        [VMEM] * 3,
        [((rows, hidden), f32)] + [message] * (ring - 1),
        2**20,
        5 * 2**20,
        "messages",
        16,
    )(keep, got, row)
    found = [None] * (ring - 1)
    for r in (4, 3, 5, 2, 6, 1, 7):
        found[r - 1] = turn(messages[r - 1], "y", r)
    half = ((rows // 2, hidden), bf16)
    return call(
        total_kernel,
        [VMEM] * (ring + 1),
        [half, half, (row.shape, f32)],
        2**20,
        2 * 2**20,
        "totals",
        16,
    )(own, row, *found)


def per_device(
    tokens, cotangent, router_weight, gate_weight, up_weight, down_weight, routes, drop_mask
):
    tok_rows, features = tokens.shape
    experts = router_weight.shape[0]
    top_count = routes.shape[1]
    _, part, hidden = gate_weight.shape
    shards = features // part
    ring = shards // 2
    capacity = tok_rows * top_count * 2 // (3 * experts)
    slots = experts * capacity

    sent, select = call(
        dispatch_kernel,
        [VMEM, VMEM, HBM, HBM],
        [((experts, 2 * capacity, features), bf16), ((slots, tok_rows), bf16)],
        4 * slots * tok_rows * features,
        3 * 2**20,
        "dispatch",
        16,
        scratch=[
            pltpu.VMEM((tok_rows, features), bf16),
            pltpu.VMEM((tok_rows, features), bf16),
            pltpu.VMEM((experts, 2 * capacity, features), bf16),
            pltpu.VMEM((slots, tok_rows), bf16),
            pltpu.SemaphoreType.DMA((7,)),
        ],
        out_specs=[HBM, HBM],
    )(routes.T, drop_mask.reshape(1, tok_rows), tokens, cotangent)
    slot_rows = lax.all_to_all(sent, EXPERT, split_axis=0, concat_axis=0, tiled=True)

    shard = jnp.concatenate(
        [gate_weight[0], up_weight[0], pack_down(down_weight[0], hidden)], axis=0
    )
    arrays, places = gather_shards(shard)
    pair, down = call(
        lambda *refs: order_kernel(shards, *refs),
        [SMEM] + [VMEM] * shards,
        [((shards, 2 * part, hidden), bf16), ((shards, hidden // shards, features), bf16)],
        2**20,
        9 * 2**20,
        "order",
        16,
    )(jnp.stack(places).astype(jnp.int32), *arrays)
    here = jnp.stack([lax.axis_index(EXPERT), lax.axis_index("y"), lax.axis_index("core")])

    keep, give, deltas, share, term = call(
        delta_kernel,
        [SMEM] + [VMEM] * 4,
        [
            ((ring, 2 * part, hidden), bf16),
            ((ring, 2 * part, hidden), bf16),
            ((slots, 2 * hidden), bf16),
            ((slots, experts), f32),
            ((experts, features // 128, 128), f32),
        ],
        10 * slots * features * hidden,
        10 * 2**20,
        "deltas",
        40,
        scratch=[pltpu.VMEM((2, ring, part, slots), bf16)],
    )(here.astype(jnp.int32), slot_rows, pair, down, router_weight)
    (slot_grad,) = call(
        slot_grad_kernel,
        [VMEM] * 4,
        [((slots, features), bf16)],
        4 * slots * features * hidden,
        6 * 2**20,
        "slot_grad",
        24,
    )(deltas, pair, share, router_weight)

    term = lax.all_to_all(term, EXPERT, split_axis=0, concat_axis=0, tiled=True)
    slot_grad, term = lax.optimization_barrier((slot_grad, term))
    back = lax.all_to_all(slot_grad, EXPERT, split_axis=0, concat_axis=0, tiled=True)
    (token_grad,) = call(
        combine_kernel,
        [VMEM, VMEM],
        [((tok_rows, features), bf16)],
        2 * slots * tok_rows * features,
        2 * 2**20,
        "combine",
        16,
    )(select, back)

    gate_grad, up_grad, row = sum_over_dp(keep, give, jnp.sum(term, axis=0))
    row, _ = lax.optimization_barrier((row, back))
    router_grad = lax.all_to_all(
        jnp.broadcast_to(row[None], (experts,) + row.shape),
        EXPERT,
        split_axis=0,
        concat_axis=0,
        tiled=True,
    )
    return token_grad, gate_grad[None], up_grad[None], router_grad.reshape(experts, features)


def solution(mesh):
    fine = Mesh(mesh.devices.reshape(8, 2, 4, 8), DP + EXPERT)
    rows = P(DP + EXPERT, None)
    shard = P(EXPERT, DP, None)
    return jax.shard_map(
        per_device,
        mesh=fine,
        in_specs=(rows, rows, P(), shard, shard, shard, rows, P(DP + EXPERT)),
        out_specs=(rows, shard, shard, P()),
        check_vma=False,
    )
```

time: 219 us -> 222 us (1.014)
  the two profiles are of different devices: /device:TPU:2 before, /device:TPU:1 now
where the time goes in v3:
time: 222 us; the launch traced here: 220 us
  starting transfers between devices  112 us (50%)
  waiting for transfers between devices  49.8 us (22%)
  local copies, waits for them, and re-layouts  39.6 us (18%)
  Pallas kernels  17.1 us (8%)
    ppermute x14, starting transfers between devices, turn(): lax.ppermute(value, axis, [(i, (i + by) % size) for i in range(size)])  50.2 us
    unnamed x99, local copies, waits for them, and re-layouts  38.8 us
    ppermute x14, waiting for transfers between devices, turn(): lax.ppermute(value, axis, [(i, (i + by) % size) for i in range(size)])  35.9 us
    ppermute x10, starting transfers between devices, swap(): return lax.ppermute(value, axis, [(i, i ^ by) for i in range(size)])  24.5 us
    all_to_all x1, starting transfers between devices, per_device(): lax.all_to_all(sent, EXPERT, split_axis=0, concat_axis=0, tiled=True)  14 us
    all_to_all x1, starting transfers between devices, per_device(): lax.all_to_all(jnp.broadcast_to(row[None], (experts,) + row.shape), EXPER...  9.5 us
    all_to_all x1, starting transfers between devices, per_device(): term = lax.all_to_all(term, EXPERT, split_axis=0, concat_axis=0, tiled=True)  8.96 us
    all_to_all x1, waiting for transfers between devices, per_device(): lax.all_to_all(jnp.broadcast_to(row[None], (experts,) + row.shape), EXPER...  8.1 us
  transfers between devices with their start and end apart: 28, of which 10 were waited for; matrix products, arithmetic and copies ran while one was open for 1% of the time, Pallas kernels for 3%

profile of v3, /device:TPU:1, one launch (start us, length us, event | category | flops | bytes accessed | tf_op | source)
XLA Modules:
  0.0 220.4 jit_solution(13558827455426736044)
XLA Ops:
  1.6 0.9 copy-done.43
  3.9 2.3 %dispatch.1 = (bf16[32,32,1024]{2,1,0:T(8,128)(2,1)}, bf16[512,128]{1,0:T(8,128)(2,1)S(1)}) custom-call(s32[6,128]{1,0:T(8,128)S(1)} %bitcast.33, s32[1,128]{1,0:T(1,128)S(1)} %bitcast.34, bf16[128,1024]{1,0:T(8,128)(2,1)S(1)} %copy-done.42, bf16[128,1024]{1,0:T(8,128)(2,1)S(1)} %copy-done.43), custom_call_target="tpu_custom_call" | custom-call | flops 268435456 | bytes 3145728 | tf_op jit(solution)/shard_map/dispatch/pallas_call | solution.py:306
  6.8 14.0 %all-to-all-start = ((bf16[32,32,1024]{2,1,0:T(8,128)(2,1)}), bf16[32,32,1024]{2,1,0:T(8,128)(2,1)}, u32[]{:S(2)}, u32[]{:S(2)}) async-start(bf16[32,32,1024]{2,1,0:T(8,128)(2,1)} %get-tuple-element.28), calls=%async_computation | async-start | bytes 4194304 | tf_op jit(solution)/shard_map/all_to_all | solution.py:323
  20.9 3.2 %collective-permute-start.1 = (bf16[192,768]{1,0:T(8,128)(2,1)S(1)}, bf16[192,768]{1,0:T(8,128)(2,1)S(1)}, u32[]{:S(2)}, u32[]{:S(2)}) collective-permute-start(bf16[192,768]{1,0:T(8,128)(2,1)S(1)} %maximum_maximum_fusion.refs_1_), channel_id=1, source_target_pairs={{0,64},{64,128},{128,192},{192,256},{256,320},{320,384},{384,448},... | collective-permute-start | bytes 884744 | tf_op jit(solution)/shard_map/ppermute | solution.py:238
  24.1 3.8 %collective-permute-start.3 = (bf16[192,768]{1,0:T(8,128)(2,1)S(1)}, bf16[192,768]{1,0:T(8,128)(2,1)S(1)}, u32[]{:S(2)}, u32[]{:S(2)}) collective-permute-start(bf16[192,768]{1,0:T(8,128)(2,1)S(1)} %maximum_maximum_fusion.refs_1_), channel_id=1, source_target_pairs={{0,448},{64,0},{128,64},{192,128},{256,192},{320,256},{384,320},{4... | collective-permute-start | bytes 884744 | tf_op jit(solution)/shard_map/ppermute | solution.py:238
  27.9 4.6 %collective-permute-done.1.refs_3_ = bf16[192,768]{1,0:T(8,128)(2,1)S(1)} collective-permute-done((bf16[192,768]{1,0:T(8,128)(2,1)S(1)}, bf16[192,768]{1,0:T(8,128)(2,1)S(1)}, u32[]{:S(2)}, u32[]{:S(2)}) %collective-permute-start.1) | collective-permute-done | bytes 294944 | tf_op jit(solution)/shard_map/ppermute | solution.py:238
  32.5 1.9 collective-permute-start.5
  34.4 4.6 %collective-permute-start.7 = (bf16[192,768]{1,0:T(8,128)(2,1)S(1)}, bf16[192,768]{1,0:T(8,128)(2,1)S(1)}, u32[]{:S(2)}, u32[]{:S(2)}) collective-permute-start(bf16[192,768]{1,0:T(8,128)(2,1)S(1)} %collective-permute-done.3.refs_5_), channel_id=1, source_target_pairs={{0,448},{64,0},{128,64},{192,128},{256,192},{320,256},{384,320},{4... | collective-permute-start | bytes 884744 | tf_op jit(solution)/shard_map/ppermute | solution.py:238
  39.0 3.7 %collective-permute-done.5.refs_7_ = bf16[192,768]{1,0:T(8,128)(2,1)S(1)} collective-permute-done((bf16[192,768]{1,0:T(8,128)(2,1)S(1)}, bf16[192,768]{1,0:T(8,128)(2,1)S(1)}, u32[]{:S(2)}, u32[]{:S(2)}) %collective-permute-start.5) | collective-permute-done | bytes 294944 | tf_op jit(solution)/shard_map/ppermute | solution.py:238
  42.7 1.9 collective-permute-start.9
  44.7 4.2 %collective-permute-start = (bf16[192,768]{1,0:T(8,128)(2,1)S(1)}, bf16[192,768]{1,0:T(8,128)(2,1)S(1)}, u32[]{:S(2)}, u32[]{:S(2)}) collective-permute-start(bf16[192,768]{1,0:T(8,128)(2,1)S(1)} %maximum_maximum_fusion.refs_1_), channel_id=1, source_target_pairs={{0,32},{32,0},{1,33},{33,1},{2,34},{34,2},{3,35},{35,3},{4,36},{36... | collective-permute-start | bytes 884744 | tf_op jit(solution)/shard_map/ppermute | solution.py:243
  48.8 1.9 collective-permute-start.4
  51.5 2.4 %collective-permute-start.2 = (bf16[192,768]{1,0:T(8,128)(2,1)S(1)}, bf16[192,768]{1,0:T(8,128)(2,1)S(1)}, u32[]{:S(2)}, u32[]{:S(2)}) collective-permute-start(bf16[192,768]{1,0:T(8,128)(2,1)S(1)} %collective-permute-done.1.refs_3_), channel_id=1, source_target_pairs={{0,32},{32,0},{1,33},{33,1},{2,34},{34,2},{3,35},{35,3},{4,36},{36... | collective-permute-start | bytes 884744 | tf_op jit(solution)/shard_map/ppermute | solution.py:243
  54.6 4.8 %collective-permute-start.11 = (bf16[192,768]{1,0:T(8,128)(2,1)S(1)}, bf16[192,768]{1,0:T(8,128)(2,1)S(1)}, u32[]{:S(2)}, u32[]{:S(2)}) collective-permute-start(bf16[192,768]{1,0:T(8,128)(2,1)S(1)} %collective-permute-done.7.refs_9_), channel_id=1, source_target_pairs={{0,448},{64,0},{128,64},{192,128},{256,192},{320,256},{384,320},{4... | collective-permute-start | bytes 884744 | tf_op jit(solution)/shard_map/ppermute | solution.py:238
  59.5 1.9 collective-permute-start.13
  62.1 2.2 collective-permute-start.8
  65.7 2.1 collective-permute-start.6
  69.3 2.2 collective-permute-start.10
  72.2 2.1 collective-permute-start.12
  75.1 2.2 collective-permute-start.14
  81.9 1.0 copy-done.5
  82.8 1.0 copy-done.7
  83.8 1.0 copy-done.9
  84.8 1.0 copy-done.11
  85.7 1.0 copy-done.13
  86.7 1.0 copy-done.15
  87.7 1.0 copy-done.17
  88.6 1.0 copy-done.19
  89.6 1.0 copy-done.21
  90.5 1.0 copy-done.23
  91.5 1.0 copy-done.25
  92.5 1.0 copy-done.27
  93.4 1.0 copy-done.29
  94.4 1.0 copy-done.31
  95.3 1.0 copy-done.33
  97.2 1.2 copy-done.40
  99.3 1.4 copy-done.41
  100.7 7.2 %deltas.1 = (bf16[8,128,768]{2,1,0:T(8,128)(2,1)S(1)}, bf16[8,128,768]{2,1,0:T(8,128)(2,1)S(1)}, bf16[512,1536]{1,0:T(8,128)(2,1)S(1)}, f32[512,32]{1,0:T(8,128)S(1)}, f32[32,8,128]{2,1,0:T(8,128)S(1)}) custom-call(s32[3]{0:T(128)S(1)} %pad_add_fusion.place_ref, bf16[32,32,1024]{2,1,0:T(8,128)(2,1)} %all-to-all-done.slots_ref, ...), custom_call_target="tpu_custom_call" | custom-call | flops 4026531840 | bytes 10485760 | tf_op jit(solution)/shard_map/deltas/pallas_call | solution.py:340
  107.9 1.1 copy-done
  109.0 1.2 copy-done.2
  110.9 1.2 copy-done.39
  112.0 9.0 %all-to-all-start.1 = ((f32[32,8,128]{2,1,0:T(8,128)}), f32[32,8,128]{2,1,0:T(8,128)}, u32[]{:S(2)}, u32[]{:S(2)}) async-start(f32[32,8,128]{2,1,0:T(8,128)} %copy-done.36), calls=%async_computation.1 | async-start | bytes 262144 | tf_op jit(solution)/shard_map/all_to_all | solution.py:366
  121.0 1.4 copy-done.3
  122.4 3.1 %slot_grad.1 = bf16[512,1024]{1,0:T(8,128)(2,1)} custom-call(bf16[512,1536]{1,0:T(8,128)(2,1)S(1)} %copy-done.3, bf16[16,128,768]{2,1,0:T(8,128)(2,1)S(1)} %get-tuple-element.29.pair_ref, f32[512,32]{1,0:T(8,128)S(1)} %get-tuple-element.32.share_ref, f32[32,1024]{1,0:T(8,128)S(1)} %copy-done.35), custom_call_target="tpu_custom_call" | custom-call | flops 1610612736 | bytes 6291456 | tf_op jit(solution)/shard_map/slot_grad/pallas_call | solution.py:356
  125.5 4.6 %all-to-all-done.1 = f32[32,8,128]{2,1,0:T(8,128)} async-done(((f32[32,8,128]{2,1,0:T(8,128)}), f32[32,8,128]{2,1,0:T(8,128)}, u32[]{:S(2)}, u32[]{:S(2)}) %all-to-all-start.1) | async-done | bytes 131104 | tf_op jit(solution)/shard_map/all_to_all | solution.py:366
  130.1 4.7 %all-to-all-start.2 = ((bf16[32,16,1024]{2,1,0:T(8,128)(2,1)}), bf16[32,16,1024]{2,1,0:T(8,128)(2,1)S(1)}, u32[]{:S(2)}, u32[]{:S(2)}) async-start(bf16[32,16,1024]{2,1,0:T(8,128)(2,1)} %bitcast.24), calls=%async_computation.2 | async-start | bytes 2097152 | tf_op jit(solution)/shard_map/all_to_all | solution.py:368
  134.8 3.3 %collective-permute-start.15 = (bf16[8,128,768]{2,1,0:T(8,128)(2,1)}, bf16[8,128,768]{2,1,0:T(8,128)(2,1)}, u32[]{:S(2)}, u32[]{:S(2)}) collective-permute-start(bf16[8,128,768]{2,1,0:T(8,128)(2,1)} %copy-done.39), channel_id=1, source_target_pairs={{0,32},{32,0},{1,33},{33,1},{2,34},{34,2},{3,35},{35,3},{4,36},{36... | collective-permute-start | bytes 4718600 | tf_op jit(solution)/shard_map/ppermute | solution.py:243
  139.0 1.9 collective-permute-start.16
  141.0 1.1 collective-permute-done.16
  142.1 1.8 messages.1
  143.9 2.1 collective-permute-start.17
  145.9 7.4 %collective-permute-start.18 = (bf16[136,768]{1,0:T(8,128)(2,1)S(1)}, bf16[136,768]{1,0:T(8,128)(2,1)S(1)}, u32[]{:S(2)}, u32[]{:S(2)}) collective-permute-start(bf16[136,768]{1,0:T(8,128)(2,1)S(1)} %get-tuple-element.40), channel_id=1, source_target_pairs={{0,128},{64,192},{128,256},{192,320},{256,384},{320,448},{384,0},{... | collective-permute-start | bytes 626696 | tf_op jit(solution)/shard_map/ppermute | solution.py:238
  153.4 1.9 collective-permute-start.19
  155.3 4.6 %collective-permute-start.20 = (bf16[136,768]{1,0:T(8,128)(2,1)S(1)}, bf16[136,768]{1,0:T(8,128)(2,1)S(1)}, u32[]{:S(2)}, u32[]{:S(2)}) collective-permute-start(bf16[136,768]{1,0:T(8,128)(2,1)S(1)} %get-tuple-element.42), channel_id=1, source_target_pairs={{0,256},{64,320},{128,384},{192,448},{256,0},{320,64},{384,128},{4... | collective-permute-start | bytes 626696 | tf_op jit(solution)/shard_map/ppermute | solution.py:238
  160.0 4.3 %collective-permute-start.21 = (bf16[136,768]{1,0:T(8,128)(2,1)S(1)}, bf16[136,768]{1,0:T(8,128)(2,1)S(1)}, u32[]{:S(2)}, u32[]{:S(2)}) collective-permute-start(bf16[136,768]{1,0:T(8,128)(2,1)S(1)} %get-tuple-element.43), channel_id=1, source_target_pairs={{0,320},{64,384},{128,448},{192,0},{256,64},{320,128},{384,192},{4... | collective-permute-start | bytes 626696 | tf_op jit(solution)/shard_map/ppermute | solution.py:238
  164.2 4.6 %collective-permute-start.22 = (bf16[136,768]{1,0:T(8,128)(2,1)S(1)}, bf16[136,768]{1,0:T(8,128)(2,1)S(1)}, u32[]{:S(2)}, u32[]{:S(2)}) collective-permute-start(bf16[136,768]{1,0:T(8,128)(2,1)S(1)} %get-tuple-element.44), channel_id=1, source_target_pairs={{0,384},{64,448},{128,0},{192,64},{256,128},{320,192},{384,256},{4... | collective-permute-start | bytes 626696 | tf_op jit(solution)/shard_map/ppermute | solution.py:238
  168.8 3.1 %collective-permute-start.23 = (bf16[136,768]{1,0:T(8,128)(2,1)S(1)}, bf16[136,768]{1,0:T(8,128)(2,1)S(1)}, u32[]{:S(2)}, u32[]{:S(2)}) collective-permute-start(bf16[136,768]{1,0:T(8,128)(2,1)S(1)} %get-tuple-element.45), channel_id=1, source_target_pairs={{0,448},{64,0},{128,64},{192,128},{256,192},{320,256},{384,320},{4... | collective-permute-start | bytes 626696 | tf_op jit(solution)/shard_map/ppermute | solution.py:238
  171.9 1.2 collective-permute-done.19.refs_2_
  173.2 8.2 %collective-permute-done.20.refs_3_ = bf16[136,768]{1,0:T(8,128)(2,1)S(1)} collective-permute-done((bf16[136,768]{1,0:T(8,128)(2,1)S(1)}, bf16[136,768]{1,0:T(8,128)(2,1)S(1)}, u32[]{:S(2)}, u32[]{:S(2)}) %collective-permute-start.20) | collective-permute-done | bytes 208928 | tf_op jit(solution)/shard_map/ppermute | solution.py:238
  181.9 13.2 %collective-permute-done.22.refs_5_ = bf16[136,768]{1,0:T(8,128)(2,1)S(1)} collective-permute-done((bf16[136,768]{1,0:T(8,128)(2,1)S(1)}, bf16[136,768]{1,0:T(8,128)(2,1)S(1)}, u32[]{:S(2)}, u32[]{:S(2)}) %collective-permute-start.22) | collective-permute-done | bytes 208928 | tf_op jit(solution)/shard_map/ppermute | solution.py:238
  195.1 4.4 %collective-permute-done.23.refs_6_ = bf16[136,768]{1,0:T(8,128)(2,1)S(1)} collective-permute-done((bf16[136,768]{1,0:T(8,128)(2,1)S(1)}, bf16[136,768]{1,0:T(8,128)(2,1)S(1)}, u32[]{:S(2)}, u32[]{:S(2)}) %collective-permute-start.23) | collective-permute-done | bytes 208928 | tf_op jit(solution)/shard_map/ppermute | solution.py:238
  201.1 9.5 %all-to-all-start.3 = ((f32[32,8,128]{2,1,0:T(8,128)}), f32[32,8,128]{2,1,0:T(8,128)S(1)}, u32[]{:S(2)}, u32[]{:S(2)}) async-start(f32[32,8,128]{2,1,0:T(8,128)} %broadcast_in_dim.14), calls=%async_computation.3 | async-start | bytes 262144 | tf_op jit(solution)/shard_map/all_to_all | solution.py:381
  210.6 1.1 combine.1
  211.6 8.1 %all-to-all-done.3 = f32[32,8,128]{2,1,0:T(8,128)S(1)} async-done(((f32[32,8,128]{2,1,0:T(8,128)}), f32[32,8,128]{2,1,0:T(8,128)S(1)}, u32[]{:S(2)}, u32[]{:S(2)}) %all-to-all-start.3) | async-done | bytes 131104 | tf_op jit(solution)/shard_map/all_to_all | solution.py:381
  (106 shorter events, 20.0 us)
Async XLA Ops:
  0.6 1.0 copy-start.42
  1.6 0.9 copy-start.43
  6.8 14.0 %copy-start.48 = (bf16[1,48,1024]{2,1,0:T(8,128)(2,1)S(1)}, bf16[1,48,1024]{2,1,0:T(8,128)(2,1)}, u32[]{:S(2)}) copy-start(bf16[1,48,1024]{2,1,0:T(8,128)(2,1)} %param.13) | copy-start | bytes 294916
  6.8 14.0 %copy-start.46 = (bf16[1,64,768]{2,1,0:T(8,128)(2,1)S(1)}, bf16[1,64,768]{2,1,0:T(8,128)(2,1)}, u32[]{:S(2)}) copy-start(bf16[1,64,768]{2,1,0:T(8,128)(2,1)} %param.12) | copy-start | bytes 294916
  6.8 14.0 %copy-start.47 = (bf16[1,64,768]{2,1,0:T(8,128)(2,1)S(1)}, bf16[1,64,768]{2,1,0:T(8,128)(2,1)}, u32[]{:S(2)}) copy-start(bf16[1,64,768]{2,1,0:T(8,128)(2,1)} %param.11) | copy-start | bytes 294916
  6.8 91.5 %all-to-all-start = ((bf16[32,32,1024]{2,1,0:T(8,128)(2,1)}), bf16[32,32,1024]{2,1,0:T(8,128)(2,1)}, u32[]{:S(2)}, u32[]{:S(2)}) async-start(bf16[32,32,1024]{2,1,0:T(8,128)(2,1)} %get-tuple-element.28), calls=%async_computation | async-start | bytes 4194304 | tf_op jit(solution)/shard_map/all_to_all | solution.py:323
  20.9 11.6 %collective-permute-start.1 = (bf16[192,768]{1,0:T(8,128)(2,1)S(1)}, bf16[192,768]{1,0:T(8,128)(2,1)S(1)}, u32[]{:S(2)}, u32[]{:S(2)}) collective-permute-start(bf16[192,768]{1,0:T(8,128)(2,1)S(1)} %maximum_maximum_fusion.refs_1_), channel_id=1, source_target_pairs={{0,64},{64,128},{128,192},{192,256},{256,320},{320,384},{384,448},... | collective-permute-start | bytes 884744 | tf_op jit(solution)/shard_map/ppermute | solution.py:238
  24.1 10.3 %collective-permute-start.3 = (bf16[192,768]{1,0:T(8,128)(2,1)S(1)}, bf16[192,768]{1,0:T(8,128)(2,1)S(1)}, u32[]{:S(2)}, u32[]{:S(2)}) collective-permute-start(bf16[192,768]{1,0:T(8,128)(2,1)S(1)} %maximum_maximum_fusion.refs_1_), channel_id=1, source_target_pairs={{0,448},{64,0},{128,64},{192,128},{256,192},{320,256},{384,320},{4... | collective-permute-start | bytes 884744 | tf_op jit(solution)/shard_map/ppermute | solution.py:238
  32.5 10.3 %collective-permute-start.5 = (bf16[192,768]{1,0:T(8,128)(2,1)S(1)}, bf16[192,768]{1,0:T(8,128)(2,1)S(1)}, u32[]{:S(2)}, u32[]{:S(2)}) collective-permute-start(bf16[192,768]{1,0:T(8,128)(2,1)S(1)} %collective-permute-done.1.refs_3_), channel_id=1, source_target_pairs={{0,64},{64,128},{128,192},{192,256},{256,320},{320,384},{384,448},... | collective-permute-start | bytes 884744 | tf_op jit(solution)/shard_map/ppermute | solution.py:238
  34.4 20.2 %collective-permute-start.7 = (bf16[192,768]{1,0:T(8,128)(2,1)S(1)}, bf16[192,768]{1,0:T(8,128)(2,1)S(1)}, u32[]{:S(2)}, u32[]{:S(2)}) collective-permute-start(bf16[192,768]{1,0:T(8,128)(2,1)S(1)} %collective-permute-done.3.refs_5_), channel_id=1, source_target_pairs={{0,448},{64,0},{128,64},{192,128},{256,192},{320,256},{384,320},{4... | collective-permute-start | bytes 884744 | tf_op jit(solution)/shard_map/ppermute | solution.py:238
  42.7 16.7 %collective-permute-start.9 = (bf16[192,768]{1,0:T(8,128)(2,1)S(1)}, bf16[192,768]{1,0:T(8,128)(2,1)S(1)}, u32[]{:S(2)}, u32[]{:S(2)}) collective-permute-start(bf16[192,768]{1,0:T(8,128)(2,1)S(1)} %collective-permute-done.5.refs_7_), channel_id=1, source_target_pairs={{0,64},{64,128},{128,192},{192,256},{256,320},{320,384},{384,448},... | collective-permute-start | bytes 884744 | tf_op jit(solution)/shard_map/ppermute | solution.py:238
  44.7 16.7 %collective-permute-start = (bf16[192,768]{1,0:T(8,128)(2,1)S(1)}, bf16[192,768]{1,0:T(8,128)(2,1)S(1)}, u32[]{:S(2)}, u32[]{:S(2)}) collective-permute-start(bf16[192,768]{1,0:T(8,128)(2,1)S(1)} %maximum_maximum_fusion.refs_1_), channel_id=1, source_target_pairs={{0,32},{32,0},{1,33},{33,1},{2,34},{34,2},{3,35},{35,3},{4,36},{36... | collective-permute-start | bytes 884744 | tf_op jit(solution)/shard_map/ppermute | solution.py:243
  48.8 16.2 %collective-permute-start.4 = (bf16[192,768]{1,0:T(8,128)(2,1)S(1)}, bf16[192,768]{1,0:T(8,128)(2,1)S(1)}, u32[]{:S(2)}, u32[]{:S(2)}) collective-permute-start(bf16[192,768]{1,0:T(8,128)(2,1)S(1)} %collective-permute-done.3.refs_5_), channel_id=1, source_target_pairs={{0,32},{32,0},{1,33},{33,1},{2,34},{34,2},{3,35},{35,3},{4,36},{36... | collective-permute-start | bytes 884744 | tf_op jit(solution)/shard_map/ppermute | solution.py:243
  51.5 17.1 %collective-permute-start.2 = (bf16[192,768]{1,0:T(8,128)(2,1)S(1)}, bf16[192,768]{1,0:T(8,128)(2,1)S(1)}, u32[]{:S(2)}, u32[]{:S(2)}) collective-permute-start(bf16[192,768]{1,0:T(8,128)(2,1)S(1)} %collective-permute-done.1.refs_3_), channel_id=1, source_target_pairs={{0,32},{32,0},{1,33},{33,1},{2,34},{34,2},{3,35},{35,3},{4,36},{36... | collective-permute-start | bytes 884744 | tf_op jit(solution)/shard_map/ppermute | solution.py:243
  54.6 17.6 %collective-permute-start.11 = (bf16[192,768]{1,0:T(8,128)(2,1)S(1)}, bf16[192,768]{1,0:T(8,128)(2,1)S(1)}, u32[]{:S(2)}, u32[]{:S(2)}) collective-permute-start(bf16[192,768]{1,0:T(8,128)(2,1)S(1)} %collective-permute-done.7.refs_9_), channel_id=1, source_target_pairs={{0,448},{64,0},{128,64},{192,128},{256,192},{320,256},{384,320},{4... | collective-permute-start | bytes 884744 | tf_op jit(solution)/shard_map/ppermute | solution.py:238
  59.5 15.6 %collective-permute-start.13 = (bf16[192,768]{1,0:T(8,128)(2,1)S(1)}, bf16[192,768]{1,0:T(8,128)(2,1)S(1)}, u32[]{:S(2)}, u32[]{:S(2)}) collective-permute-start(bf16[192,768]{1,0:T(8,128)(2,1)S(1)} %collective-permute-done.9.refs_11_), channel_id=1, source_target_pairs={{0,64},{64,128},{128,192},{192,256},{256,320},{320,384},{384,448},... | collective-permute-start | bytes 884744 | tf_op jit(solution)/shard_map/ppermute | solution.py:238
  62.1 16.1 %collective-permute-start.8 = (bf16[192,768]{1,0:T(8,128)(2,1)S(1)}, bf16[192,768]{1,0:T(8,128)(2,1)S(1)}, u32[]{:S(2)}, u32[]{:S(2)}) collective-permute-start(bf16[192,768]{1,0:T(8,128)(2,1)S(1)} %collective-permute-done.7.refs_9_), channel_id=1, source_target_pairs={{0,32},{32,0},{1,33},{33,1},{2,34},{34,2},{3,35},{35,3},{4,36},{36... | collective-permute-start | bytes 884744 | tf_op jit(solution)/shard_map/ppermute | solution.py:243
  65.7 13.2 %collective-permute-start.6 = (bf16[192,768]{1,0:T(8,128)(2,1)S(1)}, bf16[192,768]{1,0:T(8,128)(2,1)S(1)}, u32[]{:S(2)}, u32[]{:S(2)}) collective-permute-start(bf16[192,768]{1,0:T(8,128)(2,1)S(1)} %collective-permute-done.5.refs_7_), channel_id=1, source_target_pairs={{0,32},{32,0},{1,33},{33,1},{2,34},{34,2},{3,35},{35,3},{4,36},{36... | collective-permute-start | bytes 884744 | tf_op jit(solution)/shard_map/ppermute | solution.py:243
  69.3 11.2 %collective-permute-start.10 = (bf16[192,768]{1,0:T(8,128)(2,1)S(1)}, bf16[192,768]{1,0:T(8,128)(2,1)S(1)}, u32[]{:S(2)}, u32[]{:S(2)}) collective-permute-start(bf16[192,768]{1,0:T(8,128)(2,1)S(1)} %collective-permute-done.9.refs_11_), channel_id=1, source_target_pairs={{0,32},{32,0},{1,33},{33,1},{2,34},{34,2},{3,35},{35,3},{4,36},{36... | collective-permute-start | bytes 884744 | tf_op jit(solution)/shard_map/ppermute | solution.py:243
  71.5 0.8 copy-start.12
  72.2 7.4 %collective-permute-start.12 = (bf16[192,768]{1,0:T(8,128)(2,1)S(1)}, bf16[192,768]{1,0:T(8,128)(2,1)S(1)}, u32[]{:S(2)}, u32[]{:S(2)}) collective-permute-start(bf16[192,768]{1,0:T(8,128)(2,1)S(1)} %collective-permute-done.11.refs_13_), channel_id=1, source_target_pairs={{0,32},{32,0},{1,33},{33,1},{2,34},{34,2},{3,35},{35,3},{4,36},{36... | collective-permute-start | bytes 884744 | tf_op jit(solution)/shard_map/ppermute | solution.py:243
  74.4 0.7 copy-start.20
  75.1 6.1 %collective-permute-start.14 = (bf16[192,768]{1,0:T(8,128)(2,1)S(1)}, bf16[192,768]{1,0:T(8,128)(2,1)S(1)}, u32[]{:S(2)}, u32[]{:S(2)}) collective-permute-start(bf16[192,768]{1,0:T(8,128)(2,1)S(1)} %collective-permute-done.13.refs_15_), channel_id=1, source_target_pairs={{0,32},{32,0},{1,33},{33,1},{2,34},{34,2},{3,35},{35,3},{4,36},{36... | collective-permute-start | bytes 884744 | tf_op jit(solution)/shard_map/ppermute | solution.py:243
  78.2 0.7 copy-start.24
  78.9 0.7 copy-start.26
  79.7 0.8 copy-start.30
  81.2 0.7 copy-start.32
  81.9 1.0 copy-start.5
  82.8 1.0 copy-start.7
  83.8 1.0 copy-start.9
  84.8 1.0 copy-start.11
  85.7 1.0 copy-start.13
  86.7 1.0 copy-start.15
  87.7 1.0 copy-start.17
  88.6 1.0 copy-start.19
  89.6 1.0 copy-start.21
  90.5 1.0 copy-start.23
  91.5 1.0 copy-start.25
  92.5 1.0 copy-start.27
  93.4 1.0 copy-start.29
  94.4 1.0 copy-start.31
  95.3 1.0 copy-start.33
  97.2 1.2 copy-start.40
  98.3 0.9 copy-start.34
  99.2 1.4 copy-start.41
  100.7 20.3 %copy-start.35 = (f32[32,1024]{1,0:T(8,128)S(1)}, f32[32,1024]{1,0:T(8,128)}, u32[]{:S(2)}) copy-start(f32[32,1024]{1,0:T(8,128)} %router_ref.3) | copy-start | bytes 393220
  107.9 1.1 copy-start
  109.0 1.2 copy-start.2
  110.9 1.2 copy-start.39
  112.0 18.1 %all-to-all-start.1 = ((f32[32,8,128]{2,1,0:T(8,128)}), f32[32,8,128]{2,1,0:T(8,128)}, u32[]{:S(2)}, u32[]{:S(2)}) async-start(f32[32,8,128]{2,1,0:T(8,128)} %copy-done.36), calls=%async_computation.1 | async-start | bytes 262144 | tf_op jit(solution)/shard_map/all_to_all | solution.py:366
  121.0 1.4 copy-start.3
  125.5 16.6 %copy-start.1 = (bf16[8,128,768]{2,1,0:T(8,128)(2,1)S(1)}, bf16[8,128,768]{2,1,0:T(8,128)(2,1)}, u32[]{:S(2)}) copy-start(bf16[8,128,768]{2,1,0:T(8,128)(2,1)} %copy-done) | copy-start | bytes 4718596
  130.1 70.3 %all-to-all-start.2 = ((bf16[32,16,1024]{2,1,0:T(8,128)(2,1)}), bf16[32,16,1024]{2,1,0:T(8,128)(2,1)S(1)}, u32[]{:S(2)}, u32[]{:S(2)}) async-start(bf16[32,16,1024]{2,1,0:T(8,128)(2,1)} %bitcast.24), calls=%async_computation.2 | async-start | bytes 2097152 | tf_op jit(solution)/shard_map/all_to_all | solution.py:368
  134.8 7.3 %collective-permute-start.15 = (bf16[8,128,768]{2,1,0:T(8,128)(2,1)}, bf16[8,128,768]{2,1,0:T(8,128)(2,1)}, u32[]{:S(2)}, u32[]{:S(2)}) collective-permute-start(bf16[8,128,768]{2,1,0:T(8,128)(2,1)} %copy-done.39), channel_id=1, source_target_pairs={{0,32},{32,0},{1,33},{33,1},{2,34},{34,2},{3,35},{35,3},{4,36},{36... | collective-permute-start | bytes 4718600 | tf_op jit(solution)/shard_map/ppermute | solution.py:243
  139.0 3.1 %collective-permute-start.16 = (f32[8,128]{1,0:T(8,128)S(1)}, f32[8,128]{1,0:T(8,128)S(1)}, u32[]{:S(2)}, u32[]{:S(2)}) collective-permute-start(f32[8,128]{1,0:T(8,128)S(1)} %reduce_sum.9), channel_id=1, source_target_pairs={{0,32},{32,0},{1,33},{33,1},{2,34},{34,2},{3,35},{35,3},{4,36},{36... | collective-permute-start | bytes 12296 | tf_op jit(solution)/shard_map/ppermute | solution.py:243
  143.9 66.7 %copy-start.38 = (bf16[512,128]{1,0:T(8,128)(2,1)S(1)}, bf16[512,128]{1,0:T(8,128)(2,1)}, u32[]{:S(2)}) copy-start(bf16[512,128]{1,0:T(8,128)(2,1)} %copy-done.37) | copy-start | bytes 393220
  143.9 20.4 %collective-permute-start.17 = (bf16[136,768]{1,0:T(8,128)(2,1)S(1)}, bf16[136,768]{1,0:T(8,128)(2,1)S(1)}, u32[]{:S(2)}, u32[]{:S(2)}) collective-permute-start(bf16[136,768]{1,0:T(8,128)(2,1)S(1)} %get-tuple-element.39), channel_id=1, source_target_pairs={{0,64},{64,128},{128,192},{192,256},{256,320},{320,384},{384,448},... | collective-permute-start | bytes 626696 | tf_op jit(solution)/shard_map/ppermute | solution.py:238
  145.9 22.9 %collective-permute-start.18 = (bf16[136,768]{1,0:T(8,128)(2,1)S(1)}, bf16[136,768]{1,0:T(8,128)(2,1)S(1)}, u32[]{:S(2)}, u32[]{:S(2)}) collective-permute-start(bf16[136,768]{1,0:T(8,128)(2,1)S(1)} %get-tuple-element.40), channel_id=1, source_target_pairs={{0,128},{64,192},{128,256},{192,320},{256,384},{320,448},{384,0},{... | collective-permute-start | bytes 626696 | tf_op jit(solution)/shard_map/ppermute | solution.py:238
  153.4 19.8 %collective-permute-start.19 = (bf16[136,768]{1,0:T(8,128)(2,1)S(1)}, bf16[136,768]{1,0:T(8,128)(2,1)S(1)}, u32[]{:S(2)}, u32[]{:S(2)}) collective-permute-start(bf16[136,768]{1,0:T(8,128)(2,1)S(1)} %get-tuple-element.41), channel_id=1, source_target_pairs={{0,192},{64,256},{128,320},{192,384},{256,448},{320,0},{384,64},{4... | collective-permute-start | bytes 626696 | tf_op jit(solution)/shard_map/ppermute | solution.py:238
  155.3 26.1 %collective-permute-start.20 = (bf16[136,768]{1,0:T(8,128)(2,1)S(1)}, bf16[136,768]{1,0:T(8,128)(2,1)S(1)}, u32[]{:S(2)}, u32[]{:S(2)}) collective-permute-start(bf16[136,768]{1,0:T(8,128)(2,1)S(1)} %get-tuple-element.42), channel_id=1, source_target_pairs={{0,256},{64,320},{128,384},{192,448},{256,0},{320,64},{384,128},{4... | collective-permute-start | bytes 626696 | tf_op jit(solution)/shard_map/ppermute | solution.py:238
  160.0 21.9 %collective-permute-start.21 = (bf16[136,768]{1,0:T(8,128)(2,1)S(1)}, bf16[136,768]{1,0:T(8,128)(2,1)S(1)}, u32[]{:S(2)}, u32[]{:S(2)}) collective-permute-start(bf16[136,768]{1,0:T(8,128)(2,1)S(1)} %get-tuple-element.43), channel_id=1, source_target_pairs={{0,320},{64,384},{128,448},{192,0},{256,64},{320,128},{384,192},{4... | collective-permute-start | bytes 626696 | tf_op jit(solution)/shard_map/ppermute | solution.py:238
  164.2 30.9 %collective-permute-start.22 = (bf16[136,768]{1,0:T(8,128)(2,1)S(1)}, bf16[136,768]{1,0:T(8,128)(2,1)S(1)}, u32[]{:S(2)}, u32[]{:S(2)}) collective-permute-start(bf16[136,768]{1,0:T(8,128)(2,1)S(1)} %get-tuple-element.44), channel_id=1, source_target_pairs={{0,384},{64,448},{128,0},{192,64},{256,128},{320,192},{384,256},{4... | collective-permute-start | bytes 626696 | tf_op jit(solution)/shard_map/ppermute | solution.py:238
  168.8 30.7 %collective-permute-start.23 = (bf16[136,768]{1,0:T(8,128)(2,1)S(1)}, bf16[136,768]{1,0:T(8,128)(2,1)S(1)}, u32[]{:S(2)}, u32[]{:S(2)}) collective-permute-start(bf16[136,768]{1,0:T(8,128)(2,1)S(1)} %get-tuple-element.45), channel_id=1, source_target_pairs={{0,448},{64,0},{128,64},{192,128},{256,192},{320,256},{384,320},{4... | collective-permute-start | bytes 626696 | tf_op jit(solution)/shard_map/ppermute | solution.py:238
  201.1 18.7 %all-to-all-start.3 = ((f32[32,8,128]{2,1,0:T(8,128)}), f32[32,8,128]{2,1,0:T(8,128)S(1)}, u32[]{:S(2)}, u32[]{:S(2)}) async-start(f32[32,8,128]{2,1,0:T(8,128)} %broadcast_in_dim.14), calls=%async_computation.3 | async-start | bytes 262144 | tf_op jit(solution)/shard_map/all_to_all | solution.py:381
  (13 other events, 9.1 us)

commit v4 on v1

v4 whole, which is shorter than its diff:
```python
import jax
import jax.numpy as jnp
from jax import lax
from jax.experimental import pallas as pl
from jax.experimental.pallas import tpu as pltpu
from jax.sharding import Mesh, PartitionSpec as P

f32 = jnp.float32
bf16 = jnp.bfloat16
DP = ("y", "core")
EXPERT = ("x", "z")
CHUNK = 256
WHOLE_MIB = 63
ZEROTH = 128
FIRST = 896
ROWS = (((0,), (0,)), ((), ()))
LAST = (((1,), (1,)), ((), ()))
PLAIN = (((1,), (0,)), ((), ()))


def dot(left, right, dims=PLAIN):
    return lax.dot_general(left, right, dims, preferred_element_type=f32)


def split3(value):
    high = value.astype(bf16)
    rest = value - high.astype(f32)
    mid = rest.astype(bf16)
    low = (rest - mid.astype(f32)).astype(bf16)
    return high, mid, low


def pack_shard(gate_hbm, up_hbm, down_hbm, shard, sems):
    part, hidden = gate_hbm.shape
    narrow, features = down_hbm.shape
    extra = features - hidden
    lines = part - narrow
    moves = [
        (gate_hbm, shard.at[pl.ds(0, part)]),
        (up_hbm, shard.at[pl.ds(part, part)]),
        (down_hbm.at[:, pl.ds(0, hidden)], shard.at[pl.ds(2 * part, narrow)]),
    ]
    for i in range(hidden // extra):
        moves.append(
            (
                down_hbm.at[pl.ds(i * lines, lines), pl.ds(hidden, extra)],
                shard.at[pl.ds(2 * part + narrow, lines), pl.ds(i * extra, extra)],
            )
        )
    return [
        pltpu.make_async_copy(source, target, sems.at[i])
        for i, (source, target) in enumerate(moves)
    ]


def dispatch_kernel(
    routes_ref, mask_ref, tokens_ref, cotangent_ref, gate_hbm, up_hbm, down_hbm,
    sent_ref, select_ref, shard_hbm, tokens, cotangent, packed, select, shard, sems, shard_sems,
):
    experts, both, _ = sent_ref.shape
    capacity = both // 2
    top_count, tok_rows = routes_ref.shape
    slots = experts * capacity
    load_tokens = pltpu.make_async_copy(tokens_ref, tokens, sems.at[0])
    load_cotangent = pltpu.make_async_copy(cotangent_ref, cotangent, sems.at[1])
    load_tokens.start()
    load_cotangent.start()
    loads = pack_shard(gate_hbm, up_hbm, down_hbm, shard, shard_sems)
    for load in loads:
        load.start()
    owner = lax.broadcasted_iota(jnp.int32, (experts, tok_rows), 0)
    live = jnp.zeros((experts, tok_rows), f32)
    for k in range(top_count):
        live = live + jnp.where(routes_ref[k : k + 1, :] == owner, 1.0, 0.0)
    live = jnp.where(mask_ref[...] == 1, live, 0.0)
    row = lax.broadcasted_iota(jnp.int32, (tok_rows, tok_rows), 0)
    column = lax.broadcasted_iota(jnp.int32, (tok_rows, tok_rows), 1)
    earlier = jnp.where(row < column, 1.0, 0.0).astype(bf16)
    before = dot(live.astype(bf16), earlier)
    place = jnp.where(live > 0.5, before, -1.0).astype(bf16)
    owner = lax.broadcasted_iota(jnp.int32, (slots, experts), 0) // capacity
    spread = jnp.where(owner == lax.broadcasted_iota(jnp.int32, (slots, experts), 1), 1.0, 0.0)
    place = dot(spread.astype(bf16), place)
    index = lax.broadcasted_iota(jnp.int32, (slots, tok_rows), 0) % capacity
    select[...] = jnp.where(place == index.astype(f32), 1.0, 0.0).astype(bf16)
    stores = [pltpu.make_async_copy(select, select_ref, sems.at[2])]
    stores[0].start()
    load_tokens.wait()
    load_cotangent.wait()
    pieces = 4
    step = experts // pieces
    for piece in range(pieces):
        some = slice(piece * step, (piece + 1) * step)
        rows = select[piece * step * capacity : (piece + 1) * step * capacity, :]
        for half, ref in enumerate((tokens, cotangent)):
            packed[some, half * capacity : (half + 1) * capacity, :] = (
                dot(rows, ref[...]).astype(bf16).reshape(step, capacity, ref.shape[1])
            )
        store = pltpu.make_async_copy(packed.at[some], sent_ref.at[some], sems.at[3 + piece])
        store.start()
        stores.append(store)
        if piece == 0:
            for load in loads:
                load.wait()
            stores.append(pltpu.make_async_copy(shard, shard_hbm, sems.at[3 + pieces]))
            stores[-1].start()
    for store in stores:
        store.wait()


def expert_kernel(
    expert_ref, slots_ref, router_ref, weights_hbm,
    part_hbm, zeroth_ref, first_ref, second_ref,
    pair_ref, loaded_ref, down_ref, flipped_ref, part_ref, delta_ref, term_ref, sems,
):
    sources, both, features = slots_ref.shape
    capacity = both // 2
    slots = sources * capacity
    chunks, shards, part, _ = pair_ref.shape
    part = part // 2
    hidden = chunks * CHUNK
    narrow = hidden // shards
    extra = features - hidden
    experts = router_ref.shape[0]
    loads = [
        pltpu.make_async_copy(
            weights_hbm.at[:, pl.ds(0, 2 * part), pl.ds(i * CHUNK, CHUNK)],
            pair_ref.at[i],
            sems.at[i],
        )
        for i in range(chunks)
    ]
    load_down = pltpu.make_async_copy(
        weights_hbm.at[:, pl.ds(2 * part, part), :], loaded_ref, sems.at[chunks]
    )
    loads[0].start()
    load_down.start()
    for load in loads[1:]:
        load.start()
    slot_tokens = slots_ref[:, :capacity, :].reshape(slots, features)
    slot_cotangent = slots_ref[:, capacity:, :].reshape(slots, features)
    flipped_ref[...] = slot_tokens.T

    router_high, router_mid, router_low = split3(router_ref[...])
    stack = jnp.concatenate([router_high, router_mid, router_low], axis=0)
    logits = dot(slot_tokens, stack, LAST)
    logits = logits[:, :experts] + (
        logits[:, experts : 2 * experts] + logits[:, 2 * experts :]
    )
    weights = jnp.exp(logits)
    probs = weights / jnp.sum(weights, axis=1, keepdims=True)
    mine = lax.broadcasted_iota(jnp.int32, (slots, experts), 1) == expert_ref[0]
    own = jnp.sum(jnp.where(mine, probs, 0.0), axis=1, keepdims=True)
    rounded = own.astype(bf16).astype(f32)

    prob_grad = jnp.zeros((slots, 1), f32)
    stores = []
    for i, load in enumerate(loads):
        start = i * CHUNK
        columns = slice(start, start + CHUNK)
        load.wait()
        gate = pair_ref[i, :, :part, :].reshape(features, CHUNK)
        up = pair_ref[i, :, part:, :].reshape(features, CHUNK)
        gate_proj = dot(slot_tokens, gate)
        up_proj = dot(slot_tokens, up)
        if i == 0:
            load_down.wait()
            down_ref[:, :hidden] = loaded_ref[:, :narrow, :].reshape(hidden, hidden)
            pieces = [
                loaded_ref[:, narrow:, j * extra : (j + 1) * extra] for j in range(hidden // extra)
            ]
            down_ref[:, hidden:] = jnp.stack(pieces, axis=1).reshape(hidden, extra)
        hidden_grad = dot(slot_cotangent, down_ref[columns, :], LAST)
        sigmoid_gate = 1.0 / (1.0 + jnp.exp(-gate_proj))
        activated = gate_proj * sigmoid_gate
        slope = sigmoid_gate * (1.0 + gate_proj * (1.0 - sigmoid_gate))
        prob_grad = prob_grad + jnp.sum(
            hidden_grad * activated * up_proj, axis=1, keepdims=True
        )
        scaled = rounded * hidden_grad
        gate_delta = (scaled * up_proj * slope).astype(bf16)
        up_delta = (scaled * activated).astype(bf16)
        delta_ref[0, i] = gate_delta
        delta_ref[1, i] = up_delta
        for half, delta in enumerate((gate_delta, up_delta)):
            product = dot(flipped_ref[...], delta).astype(bf16)
            part_ref[:, half * part : (half + 1) * part, columns] = product.reshape(
                shards, part, CHUNK
            )
        stores.append(
            pltpu.make_async_copy(
                part_ref.at[:, :, pl.ds(start, CHUNK)],
                part_hbm.at[:, :, pl.ds(start, CHUNK)],
                sems.at[chunks + 1 + i],
            )
        )
        stores[-1].start()
    share = prob_grad.astype(bf16).astype(f32) * own
    share = share * (jnp.where(mine, 1.0, 0.0) - probs)
    share_high, share_mid, share_low = split3(share)
    term = dot(jnp.concatenate([share_high, share_mid, share_low], axis=1), slot_tokens, ROWS)
    term = term[:experts] + (term[experts : 2 * experts] + term[2 * experts :])
    term_high, term_mid, _ = split3(term)
    for i in range(features // 128):
        columns = slice(i * 128, (i + 1) * 128)
        term_ref[:, i, :] = term_high[:, columns].astype(f32)
        term_ref[:, capacity // 2 + i, :] = term_mid[:, columns].astype(f32)
    zeroth_ref[:, ZEROTH:] = term_ref[...].astype(bf16).reshape(slots, 128)

    left = jnp.concatenate([share_high, share_high, share_mid], axis=1)
    right = jnp.concatenate([router_high, router_mid, router_high], axis=0)
    step = CHUNK // part
    for block in range(features // CHUNK):
        some = slice(block * step, (block + 1) * step)
        start = block * CHUNK
        total = dot(left, right[:, start : start + CHUNK])
        for i in range(chunks):
            gate = pair_ref[i, some, :part, :].reshape(CHUNK, CHUNK)
            up = pair_ref[i, some, part:, :].reshape(CHUNK, CHUNK)
            total = total + dot(delta_ref[0, i], gate, LAST) + dot(delta_ref[1, i], up, LAST)
        total = total.astype(bf16)
        for ref, low, high in (
            (zeroth_ref, 0, ZEROTH),
            (first_ref, ZEROTH, FIRST),
            (second_ref, FIRST, features),
        ):
            begin, end = max(low, start), min(high, start + CHUNK)
            if begin < end:
                ref[:, begin - low : end - low] = total[:, begin - start : end - start]
    for store in stores:
        store.wait()


def fill_kernel(row_ref, given_hbm, second_hbm, block_ref, sem):
    high, mid, _ = split3(row_ref[...])
    block = jnp.concatenate([high.astype(f32), mid.astype(f32)], axis=0).astype(bf16)
    block_ref[...] = jnp.concatenate([block] * (block_ref.shape[0] // block.shape[0]), axis=0)
    place = pl.ds(given_hbm.shape[1] - block.shape[1], block.shape[1])
    store = pltpu.make_async_copy(block_ref, second_hbm.at[:, place], sem)
    store.start()
    store.wait()


def combine_kernel(
    select_ref, zeroth_ref, first_ref, second_ref, sums_ref, out_ref, router_ref, gate_ref, up_ref
):
    experts, features = router_ref.shape
    slots = select_ref.shape[0]
    select = select_ref[...]
    rest = features - FIRST
    out_ref[:, :ZEROTH] = dot(select, zeroth_ref[:, :ZEROTH], ROWS).astype(bf16)
    out_ref[:, ZEROTH:FIRST] = dot(select, first_ref[...], ROWS).astype(bf16)
    out_ref[:, FIRST:] = dot(select, second_ref[:, :rest], ROWS).astype(bf16)
    rows = second_ref[:, rest:].astype(f32).reshape(experts, slots // experts, 128)
    half = slots // experts // 2
    rows = rows[:, :half, :] + rows[:, half:, :]
    for i in range(half):
        router_ref[:, i * 128 : (i + 1) * 128] = rows[:, i, :]
    part = gate_ref.shape[0]
    gate_ref[...] = sums_ref[:part, :]
    up_ref[...] = sums_ref[part:, :]


def call(kernel, specs, outs, flops, size, name, mib, scratch=(), **more):
    return pl.pallas_call(
        kernel,
        out_shape=[jax.ShapeDtypeStruct(s, d) for s, d in outs],
        in_specs=specs,
        scratch_shapes=list(scratch),
        compiler_params=pltpu.CompilerParams(vmem_limit_bytes=int(mib * 2**20)),
        cost_estimate=pl.CostEstimate(flops=flops, bytes_accessed=size, transcendentals=0),
        name=name,
        **more,
    )


SMEM = pl.BlockSpec(memory_space=pltpu.SMEM)
VMEM = pl.BlockSpec(memory_space=pltpu.VMEM)
HBM = pl.BlockSpec(memory_space=pltpu.HBM)


def per_device(
    tokens, cotangent, router_weight, gate_weight, up_weight, down_weight, routes, drop_mask
):
    tok_rows, features = tokens.shape
    experts = router_weight.shape[0]
    top_count = routes.shape[1]
    _, part, hidden = gate_weight.shape
    shards = features // part
    capacity = tok_rows * top_count * 2 // (3 * experts)
    slots = experts * capacity

    sent, select, shard = call(
        dispatch_kernel,
        [VMEM, VMEM] + [HBM] * 5,
        [
            ((experts, 2 * capacity, features), bf16),
            ((slots, tok_rows), bf16),
            ((3 * part, hidden), bf16),
        ],
        4 * slots * tok_rows * features,
        3 * 2**20,
        "dispatch",
        WHOLE_MIB,
        scratch=[
            pltpu.VMEM((tok_rows, features), bf16),
            pltpu.VMEM((tok_rows, features), bf16),
            pltpu.VMEM((experts, 2 * capacity, features), bf16),
            pltpu.VMEM((slots, tok_rows), bf16),
            pltpu.VMEM((3 * part, hidden), bf16),
            pltpu.SemaphoreType.DMA((8,)),
            pltpu.SemaphoreType.DMA((3 + hidden // (features - hidden),)),
        ],
        out_specs=[HBM] * 3,
    )(
        routes.T,
        drop_mask.reshape(1, tok_rows),
        tokens,
        cotangent,
        gate_weight[0],
        up_weight[0],
        down_weight[0],
    )

    slot_rows = lax.all_to_all(sent, EXPERT, split_axis=0, concat_axis=0, tiled=True)
    weights = lax.all_gather(shard, DP, axis=0, tiled=True).reshape(shards, 3 * part, hidden)

    expert = lax.axis_index(EXPERT).astype(jnp.int32).reshape(1)
    chunks = hidden // CHUNK
    second_width = features - FIRST + 128
    parts, zeroth, first, second = call(
        expert_kernel,
        [SMEM, VMEM, VMEM, HBM],
        [
            ((shards, 2 * part, hidden), bf16),
            ((slots, ZEROTH + 128), bf16),
            ((slots, FIRST - ZEROTH), bf16),
            ((slots, second_width), bf16),
        ],
        14 * slots * features * hidden,
        10 * 2**20,
        "expert",
        48,
        scratch=[
            pltpu.VMEM((chunks, shards, 2 * part, CHUNK), bf16),
            pltpu.VMEM((shards, part, hidden), bf16),
            pltpu.VMEM((hidden, features), bf16),
            pltpu.VMEM((features, slots), bf16),
            pltpu.VMEM((shards, 2 * part, hidden), bf16),
            pltpu.VMEM((2, chunks, slots, CHUNK), bf16),
            pltpu.VMEM((experts, capacity, 128), f32),
            pltpu.SemaphoreType.DMA((1 + 2 * chunks,)),
        ],
        out_specs=[HBM, VMEM, VMEM, VMEM],
    )(expert, slot_rows, router_weight, weights)
    sums = lax.psum_scatter(
        parts.reshape(shards * 2 * part, hidden), DP, scatter_dimension=0, tiled=True
    )

    zeroth = lax.all_to_all(zeroth, EXPERT, split_axis=0, concat_axis=0, tiled=True)
    first, zeroth = lax.optimization_barrier((first, zeroth))
    first = lax.all_to_all(first, EXPERT, split_axis=0, concat_axis=0, tiled=True)
    term = zeroth.reshape(experts, capacity, -1)[:, :, ZEROTH:].astype(f32)
    term = jnp.sum(term.reshape(experts, 2, capacity // 2, 128), axis=(0, 1))
    row = jnp.sum(lax.all_gather(term, DP, axis=0), axis=0)
    row, first = lax.optimization_barrier((row, first))
    (second,) = call(
        fill_kernel,
        [VMEM, HBM],
        [((slots, second_width), bf16)],
        2**17,
        2**17,
        "fill",
        16,
        scratch=[pltpu.VMEM((slots, 128), bf16), pltpu.SemaphoreType.DMA],
        out_specs=[HBM],
        input_output_aliases={1: 0},
    )(row, second)
    second = lax.all_to_all(second, EXPERT, split_axis=0, concat_axis=0, tiled=True)
    token_grad, router_grad, gate_grad, up_grad = call(
        combine_kernel,
        [VMEM] * 5,
        [
            ((tok_rows, features), bf16),
            ((experts, features), f32),
            ((part, hidden), bf16),
            ((part, hidden), bf16),
        ],
        2 * slots * tok_rows * features,
        2 * 2**20,
        "combine",
        16,
    )(select, zeroth, first, second, sums)
    return token_grad, gate_grad[None], up_grad[None], router_grad


def solution(mesh):
    fine = Mesh(mesh.devices.reshape(8, 2, 4, 8), DP + EXPERT)
    rows = P(DP + EXPERT, None)
    shard = P(EXPERT, DP, None)
    return jax.shard_map(
        per_device,
        mesh=fine,
        in_specs=(rows, rows, P(), shard, shard, shard, rows, P(DP + EXPERT)),
        out_specs=(rows, shard, shard, P()),
        check_vma=False,
    )
```

time: 183 us -> 157 us (0.86)
  waiting for transfers between devices: 77 us -> 48.9 us
  blocking collectives: 36 us -> 55.6 us
  local copies, waits for them, and re-layouts: 10.8 us -> 0.94 us
  starting transfers between devices: 23.4 us -> 19.9 us
    all_to_all x2 -> x1, waiting for transfers between devices: 28.1 us -> 0.01 us  [per_device(): lax.all_to_all(first, EXPERT, split_axis=0, concat_axis=0, tiled=True)]
    all_to_all x1 -> x2, blocking collectives: 16.1 us -> 36 us  [the longest x1 19.4 us: per_device(): lax.all_to_all(second, EXPERT, split_axis=0, concat_axis=0, tiled=True)]
    unnamed x16 -> x6, local copies, waits for them, and re-layouts: 6.64 us -> 0.94 us
    all_to_all x2 -> x1, starting transfers between devices: 9.45 us -> 6.05 us  [per_device(): lax.all_to_all(first, EXPERT, split_axis=0, concat_axis=0, tiled=True)]
    broadcast_in_dim x2 -> x0, local copies, waits for them, and re-layouts: 2.35 us -> none  [the longest x1 1.63 us: per_device(): return (token_grad, sums[:part][None], sums[part:][None], router_grad)]
  transfers between devices with their start and end apart: 5 -> 4, of which waited for: 3 -> 1; matrix products, arithmetic and copies ran while one was open for 1% -> 0% of each run, Pallas kernels for 4% -> 0%
where the time goes in v4:
time: 157 us; the launch traced here: 155 us
  blocking collectives  55.6 us (35%)
  waiting for transfers between devices  48.9 us (31%)
  starting transfers between devices  19.9 us (13%)
  Pallas kernels  15.5 us (10%)
  between operations  14.1 us (9%)
    all_to_all x1, waiting for transfers between devices, per_device(): lax.all_to_all(sent, EXPERT, split_axis=0, concat_axis=0, tiled=True)  48.9 us
    all_gather x1, blocking collectives, per_device(): row = jnp.sum(lax.all_gather(term, DP, axis=0), axis=0)  19.7 us
    all_to_all x1, blocking collectives, per_device(): lax.all_to_all(second, EXPERT, split_axis=0, concat_axis=0, tiled=True)  19.4 us
    all_to_all x1, blocking collectives, per_device(): lax.all_to_all(zeroth, EXPERT, split_axis=0, concat_axis=0, tiled=True)  16.6 us
    all_to_all x1, starting transfers between devices, per_device(): lax.all_to_all(sent, EXPERT, split_axis=0, concat_axis=0, tiled=True)  13.7 us
    pallas_call x1, Pallas kernels, per_device(): call(expert_kernel, [SMEM, VMEM, VMEM, HBM], [((shards, 2 * part, hidden)...  10.5 us
    all_to_all x1, starting transfers between devices, per_device(): lax.all_to_all(first, EXPERT, split_axis=0, concat_axis=0, tiled=True)  6.05 us
    pallas_call x1, Pallas kernels, per_device(): call(dispatch_kernel, [VMEM, VMEM] + [HBM] * 5, [((experts, 2 * capacity,...  3.86 us
  transfers between devices with their start and end apart: 4, of which 1 were waited for; matrix products, arithmetic and copies ran while one was open for 0% of the time, Pallas kernels for 0%

profile of v4, /device:TPU:1, one launch (start us, length us, event | category | flops | bytes accessed | tf_op | source)
XLA Modules:
  0.0 155.0 jit_solution(16000461162097541961)
XLA Ops:
  7.2 0.0 copy-start.2
  7.2 0.0 all-gather.3.cloned.1.call-start
  7.2 3.9 %dispatch.1 = (bf16[32,32,1024]{2,1,0:T(8,128)(2,1)}, bf16[512,128]{1,0:T(8,128)(2,1)}, bf16[192,768]{1,0:T(8,128)(2,1)}) custom-call(s32[6,128]{1,0:T(8,128)} %bitcast.33, s32[1,128]{1,0:T(1,128)} %bitcast.34, bf16[128,1024]{1,0:T(8,128)(2,1)} %tokens_ref.1, bf16[128,1024]{1,0:T(8,128)(2,1)} %cotangent_ref.1, bf16[64,768]{1,0:T(8,128)(2,1)} %bitcast.28, ...), custom_call_target="tpu_custom_call" | custom-call | flops 268435456 | bytes 3145728 | tf_op jit(solution)/shard_map/dispatch/pallas_call | solution.py:293
  11.1 0.0 all-gather.3.cloned.1.call-update
  11.1 13.7 %all-to-all-start = ((bf16[32,32,1024]{2,1,0:T(8,128)(2,1)}), bf16[32,32,1024]{2,1,0:T(8,128)(2,1)S(1)}, u32[]{:S(2)}, u32[]{:S(2)}) async-start(bf16[32,32,1024]{2,1,0:T(8,128)(2,1)} %get-tuple-element.20), calls=%async_computation | async-start | bytes 4194304 | tf_op jit(solution)/shard_map/all_to_all | solution.py:325
  24.9 0.0 reduce-scatter.2.cloned.1.call-start
  24.9 48.9 %all-to-all-done.slots_ref = bf16[32,32,1024]{2,1,0:T(8,128)(2,1)S(1)} async-done(((bf16[32,32,1024]{2,1,0:T(8,128)(2,1)}), bf16[32,32,1024]{2,1,0:T(8,128)(2,1)S(1)}, u32[]{:S(2)}, u32[]{:S(2)}) %all-to-all-start) | async-done | bytes 2097184 | tf_op jit(solution)/shard_map/all_to_all | solution.py:325
  73.8 0.0 all-gather.3.cloned.1.call-done
  73.8 0.0 copy-done.2
  73.8 10.5 %expert.1 = (bf16[16,128,768]{2,1,0:T(8,128)(2,1)}, bf16[512,256]{1,0:T(8,128)(2,1)S(1)}, bf16[512,768]{1,0:T(8,128)(2,1)}, bf16[512,256]{1,0:T(8,128)(2,1)S(1)}) custom-call(s32[1]{0:T(128)} %bitcast.5.expert_ref, bf16[32,32,1024]{2,1,0:T(8,128)(2,1)S(1)} %all-to-all-done.slots_ref, f32[32,1024]{1,0:T(8,128)S(1)} %copy-done.2, bf16[16,192,768]{2,1,0:T(8,128)(2,1)} %bitcast.27), custom_call_target="tpu_custom_call" | custom-call | flops 5637144576 | bytes 10485760 | tf_op jit(solution)/shard_map/expert/pallas_call | solution.py:331
  84.2 0.0 copy-start.1
  84.3 0.0 reduce-scatter.2.cloned.1.call-update
  84.3 16.6 %all_to_all.40 = bf16[32,16,256]{2,1,0:T(8,128)(2,1)S(1)} all-to-all(bf16[32,16,256]{2,1,0:T(8,128)(2,1)S(1)} %bitcast.25), channel_id=1, replica_groups=mesh['y'=8,'core'=2,'x'=4,'z'=8] {'x','z'}, dimensions={0} | all-to-all | bytes 524288 | tf_op jit(solution)/shard_map/all_to_all | solution.py:360
  100.9 6.1 %all-to-all-start.2 = ((bf16[32,16,768]{2,1,0:T(8,128)(2,1)}), bf16[32,16,768]{2,1,0:T(8,128)(2,1)S(1)}, u32[]{:S(2)}, u32[]{:S(2)}) async-start(bf16[32,16,768]{2,1,0:T(8,128)(2,1)} %bitcast.12), calls=%async_computation.2 | async-start | bytes 1572864 | tf_op jit(solution)/shard_map/all_to_all | solution.py:362
  107.0 19.7 %all-gather = f32[128,128]{1,0:T(8,128)S(1)} all-gather(f32[8,128]{1,0:T(8,128)S(1)} %bitcast_reduce_fusion.1), channel_id=2, replica_groups=mesh['y'=8,'core'=2,'x'=4,'z'=8] {'y','core'}, dimensions={0}, use_global_device_ids=true | all-gather | bytes 69632 | tf_op jit(solution)/shard_map/all_gather | solution.py:365
  126.7 0.0 all-to-all-done.2
  126.7 19.4 %all_to_all.41 = bf16[32,16,256]{2,1,0:T(8,128)(2,1)S(1)} all-to-all(bf16[32,16,256]{2,1,0:T(8,128)(2,1)S(1)} %bitcast.24), channel_id=1, replica_groups=mesh['y'=8,'core'=2,'x'=4,'z'=8] {'x','z'}, dimensions={0} | all-to-all | bytes 524288 | tf_op jit(solution)/shard_map/all_to_all | solution.py:379
  146.1 0.0 reduce-scatter.2.cloned.1.call-done.sums_ref
  146.1 0.0 copy-done.1
  146.1 0.0 copy-start
  146.1 0.9 copy-done
  147.1 1.1 combine.1
  (4 shorter events, 0.1 us)
Async XLA Ops:
  7.2 66.6 %copy-start.2 = (f32[32,1024]{1,0:T(8,128)S(1)}, f32[32,1024]{1,0:T(8,128)}, u32[]{:S(2)}) copy-start(f32[32,1024]{1,0:T(8,128)} %router_ref.1) | copy-start | bytes 393220
  7.2 66.6 %all-gather.3.cloned.1.call-start = ((), (), s32[]{:S(2)}) async-start(), calls=%async_computation.5 | async-start | bytes 5013504 | tf_op jit(solution)/shard_map/all_gather | solution.py:326
  11.1 62.6 %all-to-all-start = ((bf16[32,32,1024]{2,1,0:T(8,128)(2,1)}), bf16[32,32,1024]{2,1,0:T(8,128)(2,1)S(1)}, u32[]{:S(2)}, u32[]{:S(2)}) async-start(bf16[32,32,1024]{2,1,0:T(8,128)(2,1)} %get-tuple-element.20), calls=%async_computation | async-start | bytes 4194304 | tf_op jit(solution)/shard_map/all_to_all | solution.py:325
  24.9 121.3 %reduce-scatter.2.cloned.1.call-start = ((), (), s32[]{:S(2)}) async-start(), calls=%async_computation.6 | async-start | bytes 3342336 | tf_op jit(solution)/shard_map/reduce_scatter | solution.py:356
  84.2 61.9 %copy-start.1 = (bf16[512,128]{1,0:T(8,128)(2,1)S(1)}, bf16[512,128]{1,0:T(8,128)(2,1)}, u32[]{:S(2)}) copy-start(bf16[512,128]{1,0:T(8,128)(2,1)} %get-tuple-element.19.select_ref) | copy-start | bytes 393220
  100.9 25.8 %all-to-all-start.2 = ((bf16[32,16,768]{2,1,0:T(8,128)(2,1)}), bf16[32,16,768]{2,1,0:T(8,128)(2,1)S(1)}, u32[]{:S(2)}, u32[]{:S(2)}) async-start(bf16[32,16,768]{2,1,0:T(8,128)(2,1)} %bitcast.12), calls=%async_computation.2 | async-start | bytes 1572864 | tf_op jit(solution)/shard_map/all_to_all | solution.py:362
  146.1 0.9 copy-start
Sparse Core Ops, SparseCore 0:
  11.2 51.2 all-gather.2
  84.4 61.0 reduce-scatter.1

commit v5 on v4

--- a/solution.py
+++ b/solution.py
@@ -111,7 +111,7 @@
 def expert_kernel(
     expert_ref, slots_ref, router_ref, weights_hbm,
     part_hbm, zeroth_ref, first_ref, second_ref,
-    pair_ref, loaded_ref, down_ref, flipped_ref, part_ref, delta_ref, term_ref, sems,
+    pair_ref, down_ref, flipped_ref, part_ref, delta_ref, term_ref, sems,
 ):
     sources, both, features = slots_ref.shape
     capacity = both // 2
@@ -122,21 +122,36 @@
     narrow = hidden // shards
     extra = features - hidden
     experts = router_ref.shape[0]
-    loads = [
-        pltpu.make_async_copy(
-            weights_hbm.at[:, pl.ds(0, 2 * part), pl.ds(i * CHUNK, CHUNK)],
-            pair_ref.at[i],
-            sems.at[i],
+    lines = part - narrow
+    steps = 1 + hidden // extra
+    loads, known = [], 0
+    for i in range(chunks):
+        until = -(-(i + 1) * CHUNK // narrow)
+        some = pl.ds(known, until - known)
+        known = until
+        moves = [
+            (weights_hbm.at[:, pl.ds(0, 2 * part), pl.ds(i * CHUNK, CHUNK)], pair_ref.at[i]),
+            (
+                weights_hbm.at[some, pl.ds(2 * part, narrow), :],
+                down_ref.at[some, :, pl.ds(0, hidden)],
+            ),
+        ]
+        for j in range(hidden // extra):
+            moves.append(
+                (
+                    weights_hbm.at[some, pl.ds(2 * part + narrow, lines), pl.ds(j * extra, extra)],
+                    down_ref.at[some, pl.ds(j * lines, lines), pl.ds(hidden, extra)],
+                )
+            )
+        loads.append(
+            [
+                pltpu.make_async_copy(source, target, sems.at[i * (1 + steps) + k])
+                for k, (source, target) in enumerate(moves)
+            ]
         )
-        for i in range(chunks)
-    ]
-    load_down = pltpu.make_async_copy(
-        weights_hbm.at[:, pl.ds(2 * part, part), :], loaded_ref, sems.at[chunks]
-    )
-    loads[0].start()
-    load_down.start()
-    for load in loads[1:]:
-        load.start()
+    for load in loads:
+        for piece in load:
+            piece.start()
     slot_tokens = slots_ref[:, :capacity, :].reshape(slots, features)
     slot_cotangent = slots_ref[:, capacity:, :].reshape(slots, features)
     flipped_ref[...] = slot_tokens.T
@@ -154,23 +169,26 @@
     rounded = own.astype(bf16).astype(f32)
 
     prob_grad = jnp.zeros((slots, 1), f32)
-    stores = []
+    stores, todo = [], []
     for i, load in enumerate(loads):
         start = i * CHUNK
         columns = slice(start, start + CHUNK)
-        load.wait()
+        if i == 0:
+            load[0].wait()
         gate = pair_ref[i, :, :part, :].reshape(features, CHUNK)
         up = pair_ref[i, :, part:, :].reshape(features, CHUNK)
         gate_proj = dot(slot_tokens, gate)
         up_proj = dot(slot_tokens, up)
         if i == 0:
-            load_down.wait()
-            down_ref[:, :hidden] = loaded_ref[:, :narrow, :].reshape(hidden, hidden)
-            pieces = [
-                loaded_ref[:, narrow:, j * extra : (j + 1) * extra] for j in range(hidden // extra)
-            ]
-            down_ref[:, hidden:] = jnp.stack(pieces, axis=1).reshape(hidden, extra)
-        hidden_grad = dot(slot_cotangent, down_ref[columns, :], LAST)
+            for piece in load[1:] + loads[1] + loads[2]:
+                piece.wait()
+        pieces, row = [], start
+        while row < start + CHUNK:
+            shard, inside = row // narrow, row % narrow
+            end = min(narrow, inside + start + CHUNK - row)
+            pieces.append(down_ref[shard, inside:end, :])
+            row += end - inside
+        hidden_grad = dot(slot_cotangent, jnp.concatenate(pieces, axis=0), LAST)
         sigmoid_gate = 1.0 / (1.0 + jnp.exp(-gate_proj))
         activated = gate_proj * sigmoid_gate
         slope = sigmoid_gate * (1.0 + gate_proj * (1.0 - sigmoid_gate))
@@ -182,7 +200,10 @@
         up_delta = (scaled * activated).astype(bf16)
         delta_ref[0, i] = gate_delta
         delta_ref[1, i] = up_delta
-        for half, delta in enumerate((gate_delta, up_delta)):
+        todo.append((start, gate_delta, up_delta))
+    for i, (start, *pair) in enumerate(todo):
+        columns = slice(start, start + CHUNK)
+        for half, delta in enumerate(pair):
             product = dot(flipped_ref[...], delta).astype(bf16)
             part_ref[:, half * part : (half + 1) * part, columns] = product.reshape(
                 shards, part, CHUNK
@@ -191,7 +212,7 @@
             pltpu.make_async_copy(
                 part_ref.at[:, :, pl.ds(start, CHUNK)],
                 part_hbm.at[:, :, pl.ds(start, CHUNK)],
-                sems.at[chunks + 1 + i],
+                sems.at[i],
             )
         )
         stores[-1].start()
@@ -343,13 +364,12 @@
         48,
         scratch=[
             pltpu.VMEM((chunks, shards, 2 * part, CHUNK), bf16),
-            pltpu.VMEM((shards, part, hidden), bf16),
-            pltpu.VMEM((hidden, features), bf16),
+            pltpu.VMEM((shards, hidden // shards, features), bf16),
             pltpu.VMEM((features, slots), bf16),
             pltpu.VMEM((shards, 2 * part, hidden), bf16),
             pltpu.VMEM((2, chunks, slots, CHUNK), bf16),
             pltpu.VMEM((experts, capacity, 128), f32),
-            pltpu.SemaphoreType.DMA((1 + 2 * chunks,)),
+            pltpu.SemaphoreType.DMA((chunks * (2 + hidden // (features - hidden)),)),
         ],
         out_specs=[HBM, VMEM, VMEM, VMEM],
     )(expert, slot_rows, router_weight, weights)

time: 157 us -> 156 us (level)
  no operation moved by 1% of the time
where the time goes in v5:
time: 156 us; the launch traced here: 154 us
  blocking collectives  55.7 us (36%)
  waiting for transfers between devices  48.9 us (31%)
  starting transfers between devices  19.9 us (13%)
  Pallas kernels  14.8 us (9%)
  between operations  14.1 us (9%)
    all_to_all x1, waiting for transfers between devices, per_device(): lax.all_to_all(sent, EXPERT, split_axis=0, concat_axis=0, tiled=True)  48.9 us
    all_gather x1, blocking collectives, per_device(): row = jnp.sum(lax.all_gather(term, DP, axis=0), axis=0)  19.7 us
    all_to_all x1, blocking collectives, per_device(): lax.all_to_all(second, EXPERT, split_axis=0, concat_axis=0, tiled=True)  19.4 us
    all_to_all x1, blocking collectives, per_device(): lax.all_to_all(zeroth, EXPERT, split_axis=0, concat_axis=0, tiled=True)  16.6 us
    all_to_all x1, starting transfers between devices, per_device(): lax.all_to_all(sent, EXPERT, split_axis=0, concat_axis=0, tiled=True)  13.7 us
    pallas_call x1, Pallas kernels, per_device(): call(expert_kernel, [SMEM, VMEM, VMEM, HBM], [((shards, 2 * part, hidden)...  9.75 us
    all_to_all x1, starting transfers between devices, per_device(): lax.all_to_all(first, EXPERT, split_axis=0, concat_axis=0, tiled=True)  6.05 us
    pallas_call x1, Pallas kernels, per_device(): call(dispatch_kernel, [VMEM, VMEM] + [HBM] * 5, [((experts, 2 * capacity,...  3.86 us
  transfers between devices with their start and end apart: 4, of which 1 were waited for; matrix products, arithmetic and copies ran while one was open for 0% of the time, Pallas kernels for 0%

profile of v5, /device:TPU:1, one launch (start us, length us, event | category | flops | bytes accessed | tf_op | source)
XLA Modules:
  0.0 154.3 jit_solution(994940005307219320)
XLA Ops:
  7.2 0.0 copy-start.2
  7.2 0.0 all-gather.3.cloned.1.call-start
  7.2 3.9 %dispatch.1 = (bf16[32,32,1024]{2,1,0:T(8,128)(2,1)}, bf16[512,128]{1,0:T(8,128)(2,1)}, bf16[192,768]{1,0:T(8,128)(2,1)}) custom-call(s32[6,128]{1,0:T(8,128)} %bitcast.33, s32[1,128]{1,0:T(1,128)} %bitcast.34, bf16[128,1024]{1,0:T(8,128)(2,1)} %tokens_ref.1, bf16[128,1024]{1,0:T(8,128)(2,1)} %cotangent_ref.1, bf16[64,768]{1,0:T(8,128)(2,1)} %bitcast.28, ...), custom_call_target="tpu_custom_call" | custom-call | flops 268435456 | bytes 3145728 | tf_op jit(solution)/shard_map/dispatch/pallas_call | solution.py:314
  11.1 0.0 all-gather.3.cloned.1.call-update
  11.1 13.7 %all-to-all-start = ((bf16[32,32,1024]{2,1,0:T(8,128)(2,1)}), bf16[32,32,1024]{2,1,0:T(8,128)(2,1)S(1)}, u32[]{:S(2)}, u32[]{:S(2)}) async-start(bf16[32,32,1024]{2,1,0:T(8,128)(2,1)} %get-tuple-element.20), calls=%async_computation | async-start | bytes 4194304 | tf_op jit(solution)/shard_map/all_to_all | solution.py:346
  24.9 0.0 reduce-scatter.2.cloned.1.call-start
  24.9 48.9 %all-to-all-done.slots_ref = bf16[32,32,1024]{2,1,0:T(8,128)(2,1)S(1)} async-done(((bf16[32,32,1024]{2,1,0:T(8,128)(2,1)}), bf16[32,32,1024]{2,1,0:T(8,128)(2,1)S(1)}, u32[]{:S(2)}, u32[]{:S(2)}) %all-to-all-start) | async-done | bytes 2097184 | tf_op jit(solution)/shard_map/all_to_all | solution.py:346
  73.8 0.0 all-gather.3.cloned.1.call-done
  73.8 0.0 copy-done.2
  73.8 9.8 %expert.1 = (bf16[16,128,768]{2,1,0:T(8,128)(2,1)}, bf16[512,256]{1,0:T(8,128)(2,1)S(1)}, bf16[512,768]{1,0:T(8,128)(2,1)}, bf16[512,256]{1,0:T(8,128)(2,1)S(1)}) custom-call(s32[1]{0:T(128)} %bitcast.5.expert_ref, bf16[32,32,1024]{2,1,0:T(8,128)(2,1)S(1)} %all-to-all-done.slots_ref, f32[32,1024]{1,0:T(8,128)S(1)} %copy-done.2, bf16[16,192,768]{2,1,0:T(8,128)(2,1)} %bitcast.27), custom_call_target="tpu_custom_call" | custom-call | flops 5637144576 | bytes 10485760 | tf_op jit(solution)/shard_map/expert/pallas_call | solution.py:352
  83.5 0.0 copy-start.1
  83.5 0.0 reduce-scatter.2.cloned.1.call-update
  83.6 16.6 %all_to_all.40 = bf16[32,16,256]{2,1,0:T(8,128)(2,1)S(1)} all-to-all(bf16[32,16,256]{2,1,0:T(8,128)(2,1)S(1)} %bitcast.25), channel_id=1, replica_groups=mesh['y'=8,'core'=2,'x'=4,'z'=8] {'x','z'}, dimensions={0} | all-to-all | bytes 524288 | tf_op jit(solution)/shard_map/all_to_all | solution.py:380
  100.1 6.1 %all-to-all-start.2 = ((bf16[32,16,768]{2,1,0:T(8,128)(2,1)}), bf16[32,16,768]{2,1,0:T(8,128)(2,1)S(1)}, u32[]{:S(2)}, u32[]{:S(2)}) async-start(bf16[32,16,768]{2,1,0:T(8,128)(2,1)} %bitcast.12), calls=%async_computation.2 | async-start | bytes 1572864 | tf_op jit(solution)/shard_map/all_to_all | solution.py:382
  106.2 19.7 %all-gather = f32[128,128]{1,0:T(8,128)S(1)} all-gather(f32[8,128]{1,0:T(8,128)S(1)} %bitcast_reduce_fusion.1), channel_id=2, replica_groups=mesh['y'=8,'core'=2,'x'=4,'z'=8] {'y','core'}, dimensions={0}, use_global_device_ids=true | all-gather | bytes 69632 | tf_op jit(solution)/shard_map/all_gather | solution.py:385
  125.9 0.0 all-to-all-done.2
  126.0 19.4 %all_to_all.41 = bf16[32,16,256]{2,1,0:T(8,128)(2,1)S(1)} all-to-all(bf16[32,16,256]{2,1,0:T(8,128)(2,1)S(1)} %bitcast.24), channel_id=1, replica_groups=mesh['y'=8,'core'=2,'x'=4,'z'=8] {'x','z'}, dimensions={0} | all-to-all | bytes 524288 | tf_op jit(solution)/shard_map/all_to_all | solution.py:399
  145.4 0.0 reduce-scatter.2.cloned.1.call-done.sums_ref
  145.4 0.0 copy-done.1
  145.4 0.0 copy-start
  145.4 0.9 copy-done
  146.3 1.1 combine.1
  (4 shorter events, 0.1 us)
Async XLA Ops:
  7.2 66.6 %copy-start.2 = (f32[32,1024]{1,0:T(8,128)S(1)}, f32[32,1024]{1,0:T(8,128)}, u32[]{:S(2)}) copy-start(f32[32,1024]{1,0:T(8,128)} %router_ref.1) | copy-start | bytes 393220
  7.2 66.6 %all-gather.3.cloned.1.call-start = ((), (), s32[]{:S(2)}) async-start(), calls=%async_computation.5 | async-start | bytes 5013504 | tf_op jit(solution)/shard_map/all_gather | solution.py:347
  11.1 62.6 %all-to-all-start = ((bf16[32,32,1024]{2,1,0:T(8,128)(2,1)}), bf16[32,32,1024]{2,1,0:T(8,128)(2,1)S(1)}, u32[]{:S(2)}, u32[]{:S(2)}) async-start(bf16[32,32,1024]{2,1,0:T(8,128)(2,1)} %get-tuple-element.20), calls=%async_computation | async-start | bytes 4194304 | tf_op jit(solution)/shard_map/all_to_all | solution.py:346
  24.9 120.6 %reduce-scatter.2.cloned.1.call-start = ((), (), s32[]{:S(2)}) async-start(), calls=%async_computation.6 | async-start | bytes 3342336 | tf_op jit(solution)/shard_map/reduce_scatter | solution.py:376
  83.5 61.9 %copy-start.1 = (bf16[512,128]{1,0:T(8,128)(2,1)S(1)}, bf16[512,128]{1,0:T(8,128)(2,1)}, u32[]{:S(2)}) copy-start(bf16[512,128]{1,0:T(8,128)(2,1)} %get-tuple-element.19.select_ref) | copy-start | bytes 393220
  100.1 25.8 %all-to-all-start.2 = ((bf16[32,16,768]{2,1,0:T(8,128)(2,1)}), bf16[32,16,768]{2,1,0:T(8,128)(2,1)S(1)}, u32[]{:S(2)}, u32[]{:S(2)}) async-start(bf16[32,16,768]{2,1,0:T(8,128)(2,1)} %bitcast.12), calls=%async_computation.2 | async-start | bytes 1572864 | tf_op jit(solution)/shard_map/all_to_all | solution.py:382
  145.4 0.9 copy-start
Sparse Core Ops, SparseCore 0:
  11.2 51.2 all-gather.2
  83.7 61.0 reduce-scatter.1

commit v6 on v5

--- a/solution.py
+++ b/solution.py
@@ -33,20 +33,14 @@
 def pack_shard(gate_hbm, up_hbm, down_hbm, shard, sems):
     part, hidden = gate_hbm.shape
     narrow, features = down_hbm.shape
-    extra = features - hidden
-    lines = part - narrow
-    moves = [
-        (gate_hbm, shard.at[pl.ds(0, part)]),
-        (up_hbm, shard.at[pl.ds(part, part)]),
-        (down_hbm.at[:, pl.ds(0, hidden)], shard.at[pl.ds(2 * part, narrow)]),
-    ]
-    for i in range(hidden // extra):
-        moves.append(
-            (
-                down_hbm.at[pl.ds(i * lines, lines), pl.ds(hidden, extra)],
-                shard.at[pl.ds(2 * part + narrow, lines), pl.ds(i * extra, extra)],
-            )
-        )
+    moves, row = [], 0
+    for start in range(0, hidden, CHUNK):
+        for ref in (gate_hbm, up_hbm):
+            moves.append((ref.at[:, pl.ds(start, CHUNK)], shard.at[pl.ds(row, part)]))
+            row += part
+    for start in range(0, features, CHUNK):
+        moves.append((down_hbm.at[:, pl.ds(start, CHUNK)], shard.at[pl.ds(row, narrow)]))
+        row += narrow
     return [
         pltpu.make_async_copy(source, target, sems.at[i])
         for i, (source, target) in enumerate(moves)
@@ -110,8 +104,8 @@
 
 def expert_kernel(
     expert_ref, slots_ref, router_ref, weights_hbm,
-    part_hbm, zeroth_ref, first_ref, second_ref,
-    pair_ref, down_ref, flipped_ref, part_ref, delta_ref, term_ref, sems,
+    part_hbm, zeroth_ref, first_hbm, second_ref,
+    pair_ref, down_ref, flipped_ref, part_ref, delta_ref, term_ref, first_ref, sems,
 ):
     sources, both, features = slots_ref.shape
     capacity = both // 2
@@ -120,38 +114,24 @@
     part = part // 2
     hidden = chunks * CHUNK
     narrow = hidden // shards
-    extra = features - hidden
     experts = router_ref.shape[0]
-    lines = part - narrow
-    steps = 1 + hidden // extra
-    loads, known = [], 0
-    for i in range(chunks):
-        until = -(-(i + 1) * CHUNK // narrow)
-        some = pl.ds(known, until - known)
-        known = until
-        moves = [
-            (weights_hbm.at[:, pl.ds(0, 2 * part), pl.ds(i * CHUNK, CHUNK)], pair_ref.at[i]),
-            (
-                weights_hbm.at[some, pl.ds(2 * part, narrow), :],
-                down_ref.at[some, :, pl.ds(0, hidden)],
+    loads = [
+        pltpu.make_async_copy(
+            weights_hbm.at[:, pl.ds(2 * part * i, 2 * part), :], pair_ref.at[i], sems.at[i]
+        )
+        for i in range(chunks)
+    ]
+    for i in range(features // CHUNK):
+        loads.insert(
+            1 + i,
+            pltpu.make_async_copy(
+                weights_hbm.at[:, pl.ds(2 * part * chunks + narrow * i, narrow), :],
+                down_ref.at[:, :, pl.ds(i * CHUNK, CHUNK)],
+                sems.at[chunks + i],
             ),
-        ]
-        for j in range(hidden // extra):
-            moves.append(
-                (
-                    weights_hbm.at[some, pl.ds(2 * part + narrow, lines), pl.ds(j * extra, extra)],
-                    down_ref.at[some, pl.ds(j * lines, lines), pl.ds(hidden, extra)],
-                )
-            )
-        loads.append(
-            [
-                pltpu.make_async_copy(source, target, sems.at[i * (1 + steps) + k])
-                for k, (source, target) in enumerate(moves)
-            ]
         )
     for load in loads:
-        for piece in load:
-            piece.start()
+        load.start()
     slot_tokens = slots_ref[:, :capacity, :].reshape(slots, features)
     slot_cotangent = slots_ref[:, capacity:, :].reshape(slots, features)
     flipped_ref[...] = slot_tokens.T
@@ -170,18 +150,18 @@
 
     prob_grad = jnp.zeros((slots, 1), f32)
     stores, todo = [], []
-    for i, load in enumerate(loads):
+    for i in range(chunks):
         start = i * CHUNK
         columns = slice(start, start + CHUNK)
         if i == 0:
-            load[0].wait()
+            loads[0].wait()
         gate = pair_ref[i, :, :part, :].reshape(features, CHUNK)
         up = pair_ref[i, :, part:, :].reshape(features, CHUNK)
         gate_proj = dot(slot_tokens, gate)
         up_proj = dot(slot_tokens, up)
         if i == 0:
-            for piece in load[1:] + loads[1] + loads[2]:
-                piece.wait()
+            for load in loads[1:]:
+                load.wait()
         pieces, row = [], start
         while row < start + CHUNK:
             shard, inside = row // narrow, row % narrow
@@ -205,15 +185,11 @@
         columns = slice(start, start + CHUNK)
         for half, delta in enumerate(pair):
             product = dot(flipped_ref[...], delta).astype(bf16)
-            part_ref[:, half * part : (half + 1) * part, columns] = product.reshape(
-                shards, part, CHUNK
-            )
+            row = (2 * i + half) * part
+            part_ref[:, row : row + part, :] = product.reshape(shards, part, CHUNK)
+        some = pl.ds(2 * i * part, 2 * part)
         stores.append(
-            pltpu.make_async_copy(
-                part_ref.at[:, :, pl.ds(start, CHUNK)],
-                part_hbm.at[:, :, pl.ds(start, CHUNK)],
-                sems.at[i],
-            )
+            pltpu.make_async_copy(part_ref.at[:, some, :], part_hbm.at[:, some, :], sems.at[i])
         )
         stores[-1].start()
     share = prob_grad.astype(bf16).astype(f32) * own
@@ -231,7 +207,8 @@
     left = jnp.concatenate([share_high, share_high, share_mid], axis=1)
     right = jnp.concatenate([router_high, router_mid, router_high], axis=0)
     step = CHUNK // part
-    for block in range(features // CHUNK):
+    blocks = features // CHUNK
+    for block in [blocks - 1, *range(blocks - 1)]:
         some = slice(block * step, (block + 1) * step)
         start = block * CHUNK
         total = dot(left, right[:, start : start + CHUNK])
@@ -248,6 +225,14 @@
             begin, end = max(low, start), min(high, start + CHUNK)
             if begin < end:
                 ref[:, begin - low : end - low] = total[:, begin - start : end - start]
+                if ref is first_ref:
+                    place = pl.ds(begin - low, end - begin)
+                    stores.append(
+                        pltpu.make_async_copy(
+                            first_ref.at[:, place], first_hbm.at[:, place], sems.at[chunks + block]
+                        )
+                    )
+                    stores[-1].start()
     for store in stores:
         store.wait()
 
@@ -278,8 +263,10 @@
     for i in range(half):
         router_ref[:, i * 128 : (i + 1) * 128] = rows[:, i, :]
     part = gate_ref.shape[0]
-    gate_ref[...] = sums_ref[:part, :]
-    up_ref[...] = sums_ref[part:, :]
+    for i in range(gate_ref.shape[1] // CHUNK):
+        columns = slice(i * CHUNK, (i + 1) * CHUNK)
+        gate_ref[:, columns] = sums_ref[2 * i * part : (2 * i + 1) * part, :]
+        up_ref[:, columns] = sums_ref[(2 * i + 1) * part : (2 * i + 2) * part, :]
 
 
 def call(kernel, specs, outs, flops, size, name, mib, scratch=(), **more):
@@ -310,6 +297,8 @@
     shards = features // part
     capacity = tok_rows * top_count * 2 // (3 * experts)
     slots = experts * capacity
+    chunks = hidden // CHUNK
+    lines = 3 * part * chunks
 
     sent, select, shard = call(
         dispatch_kernel,
@@ -317,7 +306,7 @@
         [
             ((experts, 2 * capacity, features), bf16),
             ((slots, tok_rows), bf16),
-            ((3 * part, hidden), bf16),
+            ((lines, CHUNK), bf16),
         ],
         4 * slots * tok_rows * features,
         3 * 2**20,
@@ -328,9 +317,9 @@
             pltpu.VMEM((tok_rows, features), bf16),
             pltpu.VMEM((experts, 2 * capacity, features), bf16),
             pltpu.VMEM((slots, tok_rows), bf16),
-            pltpu.VMEM((3 * part, hidden), bf16),
+            pltpu.VMEM((lines, CHUNK), bf16),
             pltpu.SemaphoreType.DMA((8,)),
-            pltpu.SemaphoreType.DMA((3 + hidden // (features - hidden),)),
+            pltpu.SemaphoreType.DMA((2 * chunks + features // CHUNK,)),
         ],
         out_specs=[HBM] * 3,
     )(
@@ -344,16 +333,15 @@
     )
 
     slot_rows = lax.all_to_all(sent, EXPERT, split_axis=0, concat_axis=0, tiled=True)
-    weights = lax.all_gather(shard, DP, axis=0, tiled=True).reshape(shards, 3 * part, hidden)
+    weights = lax.all_gather(shard, DP, axis=0, tiled=True).reshape(shards, lines, CHUNK)
 
     expert = lax.axis_index(EXPERT).astype(jnp.int32).reshape(1)
-    chunks = hidden // CHUNK
     second_width = features - FIRST + 128
     parts, zeroth, first, second = call(
         expert_kernel,
         [SMEM, VMEM, VMEM, HBM],
         [
-            ((shards, 2 * part, hidden), bf16),
+            ((shards, 2 * part * chunks, CHUNK), bf16),
             ((slots, ZEROTH + 128), bf16),
             ((slots, FIRST - ZEROTH), bf16),
             ((slots, second_width), bf16),
@@ -366,15 +354,16 @@
             pltpu.VMEM((chunks, shards, 2 * part, CHUNK), bf16),
             pltpu.VMEM((shards, hidden // shards, features), bf16),
             pltpu.VMEM((features, slots), bf16),
-            pltpu.VMEM((shards, 2 * part, hidden), bf16),
+            pltpu.VMEM((shards, 2 * part * chunks, CHUNK), bf16),
             pltpu.VMEM((2, chunks, slots, CHUNK), bf16),
             pltpu.VMEM((experts, capacity, 128), f32),
-            pltpu.SemaphoreType.DMA((chunks * (2 + hidden // (features - hidden)),)),
+            pltpu.VMEM((slots, FIRST - ZEROTH), bf16),
+            pltpu.SemaphoreType.DMA((chunks + features // CHUNK,)),
         ],
-        out_specs=[HBM, VMEM, VMEM, VMEM],
+        out_specs=[HBM, VMEM, HBM, VMEM],
     )(expert, slot_rows, router_weight, weights)
     sums = lax.psum_scatter(
-        parts.reshape(shards * 2 * part, hidden), DP, scatter_dimension=0, tiled=True
+        parts.reshape(shards * 2 * part * chunks, CHUNK), DP, scatter_dimension=0, tiled=True
     )
 
     zeroth = lax.all_to_all(zeroth, EXPERT, split_axis=0, concat_axis=0, tiled=True)

time: 156 us -> 156 us (level)
  no operation moved by 1% of the time
where the time goes in v6:
time: 156 us; the launch traced here: 155 us
  blocking collectives  55.7 us (36%)
  waiting for transfers between devices  48.9 us (31%)
  starting transfers between devices  19.9 us (13%)
  Pallas kernels  15 us (10%)
  between operations  14.1 us (9%)
    all_to_all x1, waiting for transfers between devices, per_device(): lax.all_to_all(sent, EXPERT, split_axis=0, concat_axis=0, tiled=True)  48.8 us
    all_gather x1, blocking collectives, per_device(): row = jnp.sum(lax.all_gather(term, DP, axis=0), axis=0)  19.7 us
    all_to_all x1, blocking collectives, per_device(): lax.all_to_all(second, EXPERT, split_axis=0, concat_axis=0, tiled=True)  19.4 us
    all_to_all x1, blocking collectives, per_device(): lax.all_to_all(zeroth, EXPERT, split_axis=0, concat_axis=0, tiled=True)  16.6 us
    all_to_all x1, starting transfers between devices, per_device(): lax.all_to_all(sent, EXPERT, split_axis=0, concat_axis=0, tiled=True)  13.7 us
    pallas_call x1, Pallas kernels, per_device(): call(expert_kernel, [SMEM, VMEM, VMEM, HBM], [((shards, 2 * part * chunks...  9.93 us
    all_to_all x1, starting transfers between devices, per_device(): lax.all_to_all(first, EXPERT, split_axis=0, concat_axis=0, tiled=True)  6.06 us
    pallas_call x1, Pallas kernels, per_device(): call(dispatch_kernel, [VMEM, VMEM] + [HBM] * 5, [((experts, 2 * capacity,...  3.89 us
  transfers between devices with their start and end apart: 4, of which 1 were waited for; matrix products, arithmetic and copies ran while one was open for 0% of the time, Pallas kernels for 0%

profile of v6, /device:TPU:1, one launch (start us, length us, event | category | flops | bytes accessed | tf_op | source)
XLA Modules:
  0.0 154.5 jit_solution(16477450606581335803)
XLA Ops:
  7.2 0.0 copy-start.2
  7.2 0.0 all-gather.3.cloned.1.call-start
  7.2 3.9 %dispatch.1 = (bf16[32,32,1024]{2,1,0:T(8,128)(2,1)}, bf16[512,128]{1,0:T(8,128)(2,1)}, bf16[576,256]{1,0:T(8,128)(2,1)}) custom-call(s32[6,128]{1,0:T(8,128)} %bitcast.33, s32[1,128]{1,0:T(1,128)} %bitcast.34, bf16[128,1024]{1,0:T(8,128)(2,1)} %tokens_ref.1, bf16[128,1024]{1,0:T(8,128)(2,1)} %cotangent_ref.1, bf16[64,768]{1,0:T(8,128)(2,1)} %bitcast.28, ...), custom_call_target="tpu_custom_call" | custom-call | flops 268435456 | bytes 3145728 | tf_op jit(solution)/shard_map/dispatch/pallas_call | solution.py:303
  11.1 0.0 all-gather.3.cloned.1.call-update
  11.1 13.7 %all-to-all-start = ((bf16[32,32,1024]{2,1,0:T(8,128)(2,1)}), bf16[32,32,1024]{2,1,0:T(8,128)(2,1)S(1)}, u32[]{:S(2)}, u32[]{:S(2)}) async-start(bf16[32,32,1024]{2,1,0:T(8,128)(2,1)} %get-tuple-element.20), calls=%async_computation | async-start | bytes 4194304 | tf_op jit(solution)/shard_map/all_to_all | solution.py:335
  24.9 0.0 reduce-scatter.2.cloned.1.call-start
  24.9 48.8 %all-to-all-done.slots_ref = bf16[32,32,1024]{2,1,0:T(8,128)(2,1)S(1)} async-done(((bf16[32,32,1024]{2,1,0:T(8,128)(2,1)}), bf16[32,32,1024]{2,1,0:T(8,128)(2,1)S(1)}, u32[]{:S(2)}, u32[]{:S(2)}) %all-to-all-start) | async-done | bytes 2097184 | tf_op jit(solution)/shard_map/all_to_all | solution.py:335
  73.8 0.0 all-gather.3.cloned.1.call-done
  73.8 0.0 copy-done.2
  73.8 9.9 %expert.1 = (bf16[16,384,256]{2,1,0:T(8,128)(2,1)}, bf16[512,256]{1,0:T(8,128)(2,1)S(1)}, bf16[512,768]{1,0:T(8,128)(2,1)}, bf16[512,256]{1,0:T(8,128)(2,1)S(1)}) custom-call(s32[1]{0:T(128)} %bitcast.5.expert_ref, bf16[32,32,1024]{2,1,0:T(8,128)(2,1)S(1)} %all-to-all-done.slots_ref, f32[32,1024]{1,0:T(8,128)S(1)} %copy-done.2, bf16[16,576,256]{2,1,0:T(8,128)(2,1)} %bitcast.27), custom_call_target="tpu_custom_call" | custom-call | flops 5637144576 | bytes 10485760 | tf_op jit(solution)/shard_map/expert/pallas_call | solution.py:340
  83.7 0.0 copy-start.1
  83.7 0.0 reduce-scatter.2.cloned.1.call-update
  83.8 16.6 %all_to_all.40 = bf16[32,16,256]{2,1,0:T(8,128)(2,1)S(1)} all-to-all(bf16[32,16,256]{2,1,0:T(8,128)(2,1)S(1)} %bitcast.25), channel_id=1, replica_groups=mesh['y'=8,'core'=2,'x'=4,'z'=8] {'x','z'}, dimensions={0} | all-to-all | bytes 524288 | tf_op jit(solution)/shard_map/all_to_all | solution.py:369
  100.4 6.1 %all-to-all-start.2 = ((bf16[32,16,768]{2,1,0:T(8,128)(2,1)}), bf16[32,16,768]{2,1,0:T(8,128)(2,1)S(1)}, u32[]{:S(2)}, u32[]{:S(2)}) async-start(bf16[32,16,768]{2,1,0:T(8,128)(2,1)} %bitcast.12), calls=%async_computation.2 | async-start | bytes 1572864 | tf_op jit(solution)/shard_map/all_to_all | solution.py:371
  106.5 19.7 %all-gather = f32[128,128]{1,0:T(8,128)S(1)} all-gather(f32[8,128]{1,0:T(8,128)S(1)} %bitcast_reduce_fusion.1), channel_id=2, replica_groups=mesh['y'=8,'core'=2,'x'=4,'z'=8] {'y','core'}, dimensions={0}, use_global_device_ids=true | all-gather | bytes 69632 | tf_op jit(solution)/shard_map/all_gather | solution.py:374
  126.1 0.0 all-to-all-done.2
  126.2 19.4 %all_to_all.41 = bf16[32,16,256]{2,1,0:T(8,128)(2,1)S(1)} all-to-all(bf16[32,16,256]{2,1,0:T(8,128)(2,1)S(1)} %bitcast.24), channel_id=1, replica_groups=mesh['y'=8,'core'=2,'x'=4,'z'=8] {'x','z'}, dimensions={0} | all-to-all | bytes 524288 | tf_op jit(solution)/shard_map/all_to_all | solution.py:388
  145.6 0.0 reduce-scatter.2.cloned.1.call-done.sums_ref
  145.6 0.0 copy-done.1
  145.6 0.0 copy-start
  145.6 0.9 copy-done
  146.5 1.1 combine.1
  (4 shorter events, 0.1 us)
Async XLA Ops:
  7.2 66.6 %copy-start.2 = (f32[32,1024]{1,0:T(8,128)S(1)}, f32[32,1024]{1,0:T(8,128)}, u32[]{:S(2)}) copy-start(f32[32,1024]{1,0:T(8,128)} %router_ref.1) | copy-start | bytes 393220
  7.2 66.6 %all-gather.3.cloned.1.call-start = ((), (), s32[]{:S(2)}) async-start(), calls=%async_computation.5 | async-start | bytes 5013504 | tf_op jit(solution)/shard_map/all_gather | solution.py:336
  11.1 62.6 %all-to-all-start = ((bf16[32,32,1024]{2,1,0:T(8,128)(2,1)}), bf16[32,32,1024]{2,1,0:T(8,128)(2,1)S(1)}, u32[]{:S(2)}, u32[]{:S(2)}) async-start(bf16[32,32,1024]{2,1,0:T(8,128)(2,1)} %get-tuple-element.20), calls=%async_computation | async-start | bytes 4194304 | tf_op jit(solution)/shard_map/all_to_all | solution.py:335
  24.9 120.7 %reduce-scatter.2.cloned.1.call-start = ((), (), s32[]{:S(2)}) async-start(), calls=%async_computation.6 | async-start | bytes 3342336 | tf_op jit(solution)/shard_map/reduce_scatter | solution.py:365
  83.7 61.9 %copy-start.1 = (bf16[512,128]{1,0:T(8,128)(2,1)S(1)}, bf16[512,128]{1,0:T(8,128)(2,1)}, u32[]{:S(2)}) copy-start(bf16[512,128]{1,0:T(8,128)(2,1)} %get-tuple-element.19.select_ref) | copy-start | bytes 393220
  100.4 25.8 %all-to-all-start.2 = ((bf16[32,16,768]{2,1,0:T(8,128)(2,1)}), bf16[32,16,768]{2,1,0:T(8,128)(2,1)S(1)}, u32[]{:S(2)}, u32[]{:S(2)}) async-start(bf16[32,16,768]{2,1,0:T(8,128)(2,1)} %bitcast.12), calls=%async_computation.2 | async-start | bytes 1572864 | tf_op jit(solution)/shard_map/all_to_all | solution.py:371
  145.6 0.9 copy-start
Sparse Core Ops, SparseCore 0:
  11.3 51.2 all-gather.2
  83.9 61.0 reduce-scatter.1
